TPU v7x, 32 devices: a whole 2x2x4 slice. The times are simulated.
32 devices in a mesh: scene: 8 (over y, x, core), rows: 4 (over z).
Axes of the slice: x: 2, y: 2, z: 4, core: 2. Of those that a mesh axis runs over, the one named last changes fastest.
Arguments:
- patches: bfloat16 [2, 8, 1024, 576], P(None, 'scene', 'rows'), may hold values from -6 to 6
- scene_length: int32 [2, 8], replicated, may hold values from 256 to 1024, as said below
- target_views: int32 [2, 8], replicated, may hold values from 1 to 12, as said below
- gauss_index: int32 [2, 8, 8, 12, 1024], P(None, 'scene', None, None, 'rows'), may hold values from 0 to 18431
- raster_weight: float32 [2, 8, 8, 12, 1024], P(None, 'scene', None, None, 'rows'), may hold values from 0.2 to 1
- target_color: float32 [2, 8, 3, 12, 1024], P(None, 'scene', None, None, 'rows'), may hold values from 0 to 1
- patch_weight: float32 [576, 1024], P('rows', 'scene'), may hold values from -0.25 to 0.25
- joint_weight: float32 [1024, 3072], P('scene', 'rows'), may hold values from -0.1875 to 0.1875
- output_weight: float32 [1024, 1024], P('scene', 'rows'), may hold values from -0.5 to 0.5
- up_weight: float32 [1024, 4096], P('scene', 'rows'), may hold values from -0.1875 to 0.1875
- down_weight: float32 [4096, 1024], P('scene', 'rows'), may hold values from -0.09375 to 0.09375
- gauss_weight: float32 [1024, 768], P('scene', 'rows'), may hold values from -0.1875 to 0.1875
- vectors: float32 [14080], replicated
- patch_moment: float32 [576, 1024], P('rows', 'scene'), may hold values from -3.0517578e-05 to 3.0517578e-05
- joint_moment: float32 [1024, 3072], P('scene', 'rows'), may hold values from -3.0517578e-05 to 3.0517578e-05
- output_moment: float32 [1024, 1024], P('scene', 'rows'), may hold values from -3.0517578e-05 to 3.0517578e-05
- up_moment: float32 [1024, 4096], P('scene', 'rows'), may hold values from -3.0517578e-05 to 3.0517578e-05
- down_moment: float32 [4096, 1024], P('scene', 'rows'), may hold values from -3.0517578e-05 to 3.0517578e-05
- gauss_moment: float32 [1024, 768], P('scene', 'rows'), may hold values from -3.0517578e-05 to 3.0517578e-05
- vector_moment: float32 [14080], replicated, may hold values from -0.00015258789 to 0.00015258789
- patch_average: float32 [576, 1024], P('rows', 'scene'), may hold values from -0.25 to 0.25
- joint_average: float32 [1024, 3072], P('scene', 'rows'), may hold values from -0.1875 to 0.1875
- output_average: float32 [1024, 1024], P('scene', 'rows'), may hold values from -0.5 to 0.5
- up_average: float32 [1024, 4096], P('scene', 'rows'), may hold values from -0.1875 to 0.1875
- down_average: float32 [4096, 1024], P('scene', 'rows'), may hold values from -0.09375 to 0.09375
- gauss_average: float32 [1024, 768], P('scene', 'rows'), may hold values from -0.1875 to 0.1875
- vector_average: float32 [14080], replicated
Outputs:
- loss_sum: float32 [], replicated
- pixel_count: float32 [], replicated
- grad_norm: float32 [], replicated
- next_patch_moment: float32 [576, 1024], P('rows', 'scene')
- next_joint_moment: float32 [1024, 3072], P('scene', 'rows')
- next_output_moment: float32 [1024, 1024], P('scene', 'rows')
- next_up_moment: float32 [1024, 4096], P('scene', 'rows')
- next_down_moment: float32 [4096, 1024], P('scene', 'rows')
- next_gauss_moment: float32 [1024, 768], P('scene', 'rows')
- next_vector_moment: float32 [14080], replicated
- next_patch_weight: float32 [576, 1024], P('rows', 'scene')
- next_joint_weight: float32 [1024, 3072], P('scene', 'rows')
- next_output_weight: float32 [1024, 1024], P('scene', 'rows')
- next_up_weight: float32 [1024, 4096], P('scene', 'rows')
- next_down_weight: float32 [4096, 1024], P('scene', 'rows')
- next_gauss_weight: float32 [1024, 768], P('scene', 'rows')
- next_vectors: float32 [14080], replicated
- next_patch_average: float32 [576, 1024], P('rows', 'scene')
- next_joint_average: float32 [1024, 3072], P('scene', 'rows')
- next_output_average: float32 [1024, 1024], P('scene', 'rows')
- next_up_average: float32 [1024, 4096], P('scene', 'rows')
- next_down_average: float32 [4096, 1024], P('scene', 'rows')
- next_gauss_average: float32 [1024, 768], P('scene', 'rows')
- next_vector_average: float32 [14080], replicated
Inputs may be any that keep to these rules, and one draw needn't show every extreme that they name: `scene_length`: in each micro-batch one scene has all 1024 tokens. `target_views`: in each micro-batch one scene has 12 target views. `gauss_index`: row r of a block's table is Gaussian r % (768 // 12) of token r // (768 // 12) of the block's tokens with 16 rim tokens on each side.
All inputs are finite; a program needn't handle non-finite values.
Results may differ from a plain program's by a relative error of at most 0.0011.
The roundings to bfloat16 on the way count: a program that leaves them out, or rounds other values in their place, can miss the bound.
Values may be sent and summed in bfloat16 or wider, within the bound.
No kernel may reach another device: no remote copies, remote signals or barrier semaphores. Data moves between devices by JAX's collectives and lax.ppermute only.
A program may use at most 384 MiB of HBM per device.

v0:
```python
import jax
import jax.numpy as jnp
from jax import lax
from jax.sharding import PartitionSpec as P

D = 1024
HEADS = 16
HD = 64
FF = 4096
POUT = 768
HT = 16


HIGHEST = lax.Precision.HIGHEST
EPSILON = 1e-05
CLIP_NORM = 0.002
STEP_RATE = 1250.0
MOMENTUM = 0.9
AVERAGE_DECAY = 0.9


def with_halo(x, sides, width):
    for axis, dim in sides:
        size, length = (lax.axis_size(axis), x.shape[dim])
        up = [(i, (i + 1) % size) for i in range(size - 1)]
        down = [(j, i) for i, j in up]
        last = lax.slice_in_dim(x, length - width, length, axis=dim)
        leading = lax.slice_in_dim(x, 0, width, axis=dim)
        before = lax.ppermute(last, axis, up)
        after = lax.ppermute(leading, axis, down)
        x = jnp.concatenate([before, x, after], axis=dim)
    return x


def split_vectors(vectors):
    pieces = []
    offset = 0
    for extent in [D] * 9 + [FF, POUT]:
        pieces.append(lax.slice_in_dim(vectors, offset, offset + extent))
        offset = offset + extent
    return pieces


def layer_norm(hidden, gain, shift):
    centred = hidden - jnp.mean(hidden, axis=-1, keepdims=True)
    variance = jnp.mean(centred * centred, axis=-1, keepdims=True)
    return centred * lax.rsqrt(variance + EPSILON) * gain + shift


def norm_back(hidden, gain, shift, grad):
    unused, pull = jax.vjp(layer_norm, hidden, gain, shift)
    return pull(grad)


def features_of(colour):
    counter = jnp.arange(48).reshape(16, 3).astype(colour.dtype)
    return jnp.tanh(
        jnp.einsum("fc,ctp->ftp", 0.8 * jnp.cos(1.7 * counter + 0.3), colour, precision=HIGHEST)
    )


def render_sum(extended, index, weight, target, views):
    params = extended.reshape(-1, 12)
    colour = jax.nn.sigmoid(params[:, :3])
    opacity = jax.nn.sigmoid(params[:, 3]) * jnp.exp(
        -0.5 * jnp.mean(params[:, 4:] * params[:, 4:], axis=1)
    )
    table = jnp.concatenate([colour * opacity[:, None], opacity[:, None]], axis=1).T
    picked = jnp.take(table, index, axis=1)
    numerator = jnp.sum(weight * picked[:3], axis=1)
    denominator = 1.0 + jnp.sum(weight * picked[3], axis=0)
    rendered = numerator / denominator
    live = (jnp.arange(index.shape[1]) < views).astype(rendered.dtype)[:, None]
    difference = rendered - target
    error = jnp.sum(difference * difference, axis=0)
    feature_gap = features_of(rendered) - features_of(target)
    error = error + 0.5 * jnp.sum(feature_gap * feature_gap, axis=0)
    return jnp.sum(live * error)


def matmul(left, right):
    return jnp.dot(left, right, preferred_element_type=jnp.float32)


def left_product(left, right):
    return lax.dot_general(
        left, right, (((0,), (0,)), ((), ())), preferred_element_type=jnp.float32
    )


def right_product(left, right):
    return lax.dot_general(
        left, right, (((1,), (1,)), ((), ())), preferred_element_type=jnp.float32
    )


def attention_scores(queries, keys_all, length):
    scores = jnp.einsum(
        "qhd,khd->hqk", queries, keys_all, preferred_element_type=jnp.float32
    ) * HD ** (-0.5)
    visible = jnp.arange(keys_all.shape[0]) < length
    return jnp.where(visible[None, None, :], scores, -1e30)


def layer_forward(weights, vectors, patch, length):
    patch_w, joint_w, output_w, up_w, down_w, gauss_w = weights
    pieces = split_vectors(vectors)
    rows_here = patch.shape[0]
    hidden_zero = matmul(patch, patch_w) + pieces[6]
    normed_one = layer_norm(hidden_zero, pieces[0], pieces[3]).astype(jnp.bfloat16)
    projected = matmul(normed_one, joint_w).astype(jnp.bfloat16).reshape(rows_here, 3, HEADS, HD)
    keys_all, values_all = (
        lax.all_gather(projected[:, 1], "rows", axis=0, tiled=True),
        lax.all_gather(projected[:, 2], "rows", axis=0, tiled=True),
    )
    scores = attention_scores(projected[:, 0], keys_all, length)
    highest = jnp.max(scores, axis=-1, keepdims=True)
    log_total = highest + jnp.log(jnp.sum(jnp.exp(scores - highest), axis=-1, keepdims=True))
    probs = jnp.exp(scores - log_total).astype(jnp.bfloat16)
    mixed = jnp.einsum("hqk,khd->qhd", probs, values_all, preferred_element_type=jnp.float32)
    mixed = mixed.astype(jnp.bfloat16).reshape(rows_here, D)
    hidden_one = hidden_zero + matmul(mixed, output_w) + pieces[7]
    normed_two = layer_norm(hidden_one, pieces[1], pieces[4]).astype(jnp.bfloat16)
    up_input = matmul(normed_two, up_w) + pieces[9]
    activated = jax.nn.gelu(up_input).astype(jnp.bfloat16)
    hidden_two = hidden_one + matmul(activated, down_w) + pieces[8]
    normed_three = layer_norm(hidden_two, pieces[2], pieces[5]).astype(jnp.bfloat16)
    gauss = matmul(normed_three, gauss_w) + pieces[10]
    saved = (
        hidden_zero,
        normed_one,
        projected,
        keys_all,
        values_all,
        log_total,
        mixed,
        hidden_one,
        normed_two,
        up_input,
        activated,
        hidden_two,
        normed_three,
    )
    return (saved, gauss)


def layer_backward(weights, vectors, patch, length, saved, grad_gauss):
    patch_w, joint_w, output_w, up_w, down_w, gauss_w = weights
    pieces = split_vectors(vectors)
    (
        hidden_zero,
        normed_one,
        projected,
        keys_all,
        values_all,
        log_total,
        mixed,
        hidden_one,
        normed_two,
        up_input,
        activated,
        hidden_two,
        normed_three,
    ) = saved
    rows_here = patch.shape[0]
    grad_bias_gauss = jnp.sum(grad_gauss, axis=0)
    grad_gauss_low = grad_gauss.astype(jnp.bfloat16)
    grad_gauss_w = left_product(normed_three, grad_gauss_low)
    grad_hidden_two, grad_gain_three, grad_shift_three = norm_back(
        hidden_two, pieces[2], pieces[5], right_product(grad_gauss_low, gauss_w)
    )
    grad_bias_down = jnp.sum(grad_hidden_two, axis=0)
    grad_down_low = grad_hidden_two.astype(jnp.bfloat16)
    grad_down_w = left_product(activated, grad_down_low)
    unused, gelu_pull = jax.vjp(jax.nn.gelu, up_input)
    grad_up = gelu_pull(right_product(grad_down_low, down_w))[0]
    grad_bias_up = jnp.sum(grad_up, axis=0)
    grad_up_low = grad_up.astype(jnp.bfloat16)
    grad_up_w = left_product(normed_two, grad_up_low)
    grad_norm_two, grad_gain_two, grad_shift_two = norm_back(
        hidden_one, pieces[1], pieces[4], right_product(grad_up_low, up_w)
    )
    grad_hidden_one = grad_hidden_two + grad_norm_two
    grad_bias_out = jnp.sum(grad_hidden_one, axis=0)
    grad_out_low = grad_hidden_one.astype(jnp.bfloat16)
    grad_output_w = left_product(mixed, grad_out_low)
    grad_mixed = (
        right_product(grad_out_low, output_w).astype(jnp.bfloat16).reshape(rows_here, HEADS, HD)
    )
    queries = projected[:, 0]
    probs = jnp.exp(attention_scores(queries, keys_all, length) - log_total)
    grad_probs = jnp.einsum(
        "qhd,khd->hqk", grad_mixed, values_all, preferred_element_type=jnp.float32
    )
    delta = jnp.sum(probs * grad_probs, axis=-1, keepdims=True)
    grad_scores = (probs * (grad_probs - delta) * HD ** (-0.5)).astype(jnp.bfloat16)
    grad_queries = jnp.einsum(
        "hqk,khd->qhd", grad_scores, keys_all, preferred_element_type=jnp.float32
    )
    grad_values = jnp.einsum(
        "hqk,qhd->khd", probs.astype(jnp.bfloat16), grad_mixed, preferred_element_type=jnp.float32
    )
    grad_keys = jnp.einsum("hqk,qhd->khd", grad_scores, queries, preferred_element_type=jnp.float32)
    own_keys, own_values = (
        lax.psum_scatter(
            grad_keys.astype(jnp.bfloat16), "rows", scatter_dimension=0, tiled=True
        ).astype(jnp.float32),
        lax.psum_scatter(
            grad_values.astype(jnp.bfloat16), "rows", scatter_dimension=0, tiled=True
        ).astype(jnp.float32),
    )
    grad_projected = (
        jnp.stack([grad_queries, own_keys, own_values], axis=1)
        .reshape(rows_here, 3 * D)
        .astype(jnp.bfloat16)
    )
    grad_joint_w = left_product(normed_one, grad_projected)
    grad_norm_one, grad_gain_one, grad_shift_one = norm_back(
        hidden_zero, pieces[0], pieces[3], right_product(grad_projected, joint_w)
    )
    grad_hidden_zero = grad_hidden_one + grad_norm_one
    grad_bias_patch = jnp.sum(grad_hidden_zero, axis=0)
    grad_patch_w = left_product(patch, grad_hidden_zero.astype(jnp.bfloat16))
    grad_vectors = jnp.concatenate(
        [
            grad_gain_one,
            grad_gain_two,
            grad_gain_three,
            grad_shift_one,
            grad_shift_two,
            grad_shift_three,
            grad_bias_patch,
            grad_bias_out,
            grad_bias_down,
            grad_bias_up,
            grad_bias_gauss,
        ]
    )
    return [
        grad_patch_w,
        grad_joint_w,
        grad_output_w,
        grad_up_w,
        grad_down_w,
        grad_gauss_w,
        grad_vectors,
    ]


def body(
    patches,
    scene_length,
    target_views,
    gauss_index,
    raster_weight,
    target_color,
    patch_weight,
    joint_weight,
    output_weight,
    up_weight,
    down_weight,
    gauss_weight,
    vectors,
    patch_moment,
    joint_moment,
    output_moment,
    up_moment,
    down_moment,
    gauss_moment,
    vector_moment,
    patch_average,
    joint_average,
    output_average,
    up_average,
    down_average,
    gauss_average,
    vector_average,
):
    masters = (
        patch_weight,
        joint_weight,
        output_weight,
        up_weight,
        down_weight,
        gauss_weight,
        vectors,
    )
    moments = (
        patch_moment,
        joint_moment,
        output_moment,
        up_moment,
        down_moment,
        gauss_moment,
        vector_moment,
    )
    averages = (
        patch_average,
        joint_average,
        output_average,
        up_average,
        down_average,
        gauss_average,
        vector_average,
    )
    lowered = [item.astype(jnp.bfloat16) for item in masters[:6]]
    widened = (
        lax.all_gather(lowered[0], "rows", axis=0, tiled=True),
        lax.all_gather(lowered[1], "rows", axis=1, tiled=True),
        lax.all_gather(lowered[2], "rows", axis=1, tiled=True),
        lax.all_gather(lowered[3], "rows", axis=1, tiled=True),
        lax.all_gather(lowered[4], "rows", axis=1, tiled=True),
        lax.all_gather(lowered[5], "rows", axis=1, tiled=True),
    )
    weights = (
        lax.all_gather(widened[0], "scene", axis=1, tiled=True),
        lax.all_gather(widened[1], "scene", axis=0, tiled=True),
        lax.all_gather(widened[2], "scene", axis=0, tiled=True),
        lax.all_gather(widened[3], "scene", axis=0, tiled=True),
        lax.all_gather(widened[4], "scene", axis=0, tiled=True),
        lax.all_gather(widened[5], "scene", axis=0, tiled=True),
    )
    scene_here = lax.axis_index("scene")
    pixel_count = jnp.sum(target_views).astype(jnp.float32) * (
        raster_weight.shape[-1] * lax.axis_size("rows")
    )
    loss_total = jnp.zeros((), jnp.float32)
    totals = None
    for micro_batch in range(patches.shape[0]):
        length = scene_length[micro_batch, scene_here]
        views = target_views[micro_batch, scene_here]
        patch = patches[micro_batch, 0]
        saved, gauss = layer_forward(weights, vectors, patch, length)
        extended = with_halo(gauss.astype(jnp.bfloat16), (("rows", 0),), HT).astype(gauss.dtype)
        index = gauss_index[micro_batch, 0]
        weight = raster_weight[micro_batch, 0]
        target = target_color[micro_batch, 0]

        def local_loss(table_rows):
            return render_sum(table_rows, index, weight, target, views)

        piece_loss, render_pull = jax.vjp(local_loss, extended)
        grad_extended = render_pull(jnp.ones((), jnp.float32) / pixel_count)[0]
        edges = jnp.concatenate([grad_extended[:HT], grad_extended[-HT:]], axis=0)
        returned = with_halo(edges.astype(jnp.bfloat16), (("rows", 0),), HT).astype(edges.dtype)
        grad_gauss = grad_extended[HT:-HT]
        grad_gauss = grad_gauss.at[:HT].add(returned[:HT]).at[-HT:].add(returned[-HT:])
        grads = layer_backward(weights, vectors, patch, length, saved, grad_gauss)
        loss_total = loss_total + piece_loss
        totals = grads if totals is None else [left + right for left, right in zip(totals, grads)]
    partial_value = (
        lax.psum_scatter(
            totals[0].astype(jnp.bfloat16), "rows", scatter_dimension=0, tiled=True
        ).astype(jnp.float32),
        lax.psum_scatter(
            totals[1].astype(jnp.bfloat16), "rows", scatter_dimension=1, tiled=True
        ).astype(jnp.float32),
        lax.psum_scatter(
            totals[2].astype(jnp.bfloat16), "rows", scatter_dimension=1, tiled=True
        ).astype(jnp.float32),
        lax.psum_scatter(
            totals[3].astype(jnp.bfloat16), "rows", scatter_dimension=1, tiled=True
        ).astype(jnp.float32),
        lax.psum_scatter(
            totals[4].astype(jnp.bfloat16), "rows", scatter_dimension=1, tiled=True
        ).astype(jnp.float32),
        lax.psum_scatter(
            totals[5].astype(jnp.bfloat16), "rows", scatter_dimension=1, tiled=True
        ).astype(jnp.float32),
    )
    reduced = (
        lax.psum_scatter(partial_value[0], "scene", scatter_dimension=1, tiled=True),
        lax.psum_scatter(partial_value[1], "scene", scatter_dimension=0, tiled=True),
        lax.psum_scatter(partial_value[2], "scene", scatter_dimension=0, tiled=True),
        lax.psum_scatter(partial_value[3], "scene", scatter_dimension=0, tiled=True),
        lax.psum_scatter(partial_value[4], "scene", scatter_dimension=0, tiled=True),
        lax.psum_scatter(partial_value[5], "scene", scatter_dimension=0, tiled=True),
    )
    vector_grad, loss_sum = lax.psum((totals[6], loss_total), ("scene", "rows"))
    local_squares = sum((jnp.sum(item * item) for item in reduced))
    squares = lax.psum(local_squares, ("scene", "rows")) + jnp.sum(vector_grad * vector_grad)
    grad_norm = jnp.sqrt(squares)
    factor = jnp.minimum(1.0, CLIP_NORM / (grad_norm + 1e-06))
    grads_all = list(reduced) + [vector_grad]
    next_moments, next_weights, next_averages = ([], [], [])
    for grad, moment, master, average in zip(grads_all, moments, masters, averages):
        clipped = grad * factor
        moment_new = MOMENTUM * moment + clipped
        weight_new = master - STEP_RATE * (clipped + MOMENTUM * moment_new)
        next_moments.append(moment_new)
        next_weights.append(weight_new)
        next_averages.append(AVERAGE_DECAY * average + (1.0 - AVERAGE_DECAY) * weight_new)
    return (
        loss_sum,
        pixel_count,
        grad_norm,
        next_moments[0],
        next_moments[1],
        next_moments[2],
        next_moments[3],
        next_moments[4],
        next_moments[5],
        next_moments[6],
        next_weights[0],
        next_weights[1],
        next_weights[2],
        next_weights[3],
        next_weights[4],
        next_weights[5],
        next_weights[6],
        next_averages[0],
        next_averages[1],
        next_averages[2],
        next_averages[3],
        next_averages[4],
        next_averages[5],
        next_averages[6],
    )


def solution(mesh):
    in_specs = (
        P(None, "scene", "rows", None),
        P(),
        P(),
        P(None, "scene", None, None, "rows"),
        P(None, "scene", None, None, "rows"),
        P(None, "scene", None, None, "rows"),
        P("rows", "scene"),
        P("scene", "rows"),
        P("scene", "rows"),
        P("scene", "rows"),
        P("scene", "rows"),
        P("scene", "rows"),
        P(),
        P("rows", "scene"),
        P("scene", "rows"),
        P("scene", "rows"),
        P("scene", "rows"),
        P("scene", "rows"),
        P("scene", "rows"),
        P(),
        P("rows", "scene"),
        P("scene", "rows"),
        P("scene", "rows"),
        P("scene", "rows"),
        P("scene", "rows"),
        P("scene", "rows"),
        P(),
    )
    out_specs = (
        P(),
        P(),
        P(),
        P("rows", "scene"),
        P("scene", "rows"),
        P("scene", "rows"),
        P("scene", "rows"),
        P("scene", "rows"),
        P("scene", "rows"),
        P(),
        P("rows", "scene"),
        P("scene", "rows"),
        P("scene", "rows"),
        P("scene", "rows"),
        P("scene", "rows"),
        P("scene", "rows"),
        P(),
        P("rows", "scene"),
        P("scene", "rows"),
        P("scene", "rows"),
        P("scene", "rows"),
        P("scene", "rows"),
        P("scene", "rows"),
        P(),
    )
    return jax.shard_map(body, mesh=mesh, in_specs=in_specs, out_specs=out_specs, check_vma=False)
```

profile of v0, /device:TPU:0, one launch (start us, length us, event | category | flops | bytes accessed | tf_op | source)
XLA Modules:
  0.0 2373.3 jit_solution(18351502646998601946)
XLA Ops:
  25.2 18.0 all_gather.50
  51.9 45.2 %all-gather.19.cloned.1.call-done = bf16[1024,3072]{1,0:T(8,128)(2,1)} async-done(((bf16[128,3072]{1,0:T(8,128)(2,1)}), bf16[1024,3072]{1,0:T(8,128)(2,1)}) %all-gather.19.cloned.1.call-update) | async-done | bytes 6291472 | tf_op jit(solution)/shard_map/all_gather | solution.py:317
  106.4 16.9 all_gather.54
  138.7 24.4 %all-gather.27.cloned.1.call-done = bf16[512,1024]{1,0:T(8,128)(2,1)} async-done(((bf16[512,256]{1,0:T(8,128)(2,1)}), bf16[512,1024]{1,0:T(8,128)(2,1)}) %all-gather.27.cloned.1.call-update) | async-done | bytes 1048592 | tf_op jit(solution)/shard_map/all_gather | solution.py:312
  189.9 21.8 all-gather.35.cloned.1.call-done
  221.9 34.8 %all-gather.33.cloned.1.call-done = bf16[1024,1,16,64]{0,3,2,1:T(8,128)(2,1)} async-done(((bf16[256,1,16,64]{0,3,2,1:T(8,128)(2,1)}), bf16[1024,1,16,64]{0,3,2,1:T(8,128)(2,1)}) %all-gather.33.cloned.1.call-update) | async-done | bytes 2097168 | tf_op jit(solution)/shard_map/all_gather | solution.py:114
  265.1 19.6 all-gather.21.cloned.1.call-done
  287.4 45.7 %all-gather.39.cloned.1.call-done = bf16[1024,1,16,64]{0,3,2,1:T(8,128)(2,1)} async-done(((bf16[256,1,16,64]{0,3,2,1:T(8,128)(2,1)}), bf16[1024,1,16,64]{0,3,2,1:T(8,128)(2,1)}) %all-gather.39.cloned.1.call-update) | async-done | bytes 2097168 | tf_op jit(solution)/shard_map/all_gather | solution.py:113
  343.7 36.0 %all-gather.37.cloned.1.call-done = bf16[1024,1,16,64]{0,3,2,1:T(8,128)(2,1)} async-done(((bf16[256,1,16,64]{0,3,2,1:T(8,128)(2,1)}), bf16[1024,1,16,64]{0,3,2,1:T(8,128)(2,1)}) %all-gather.37.cloned.1.call-update) | async-done | bytes 2097168 | tf_op jit(solution)/shard_map/all_gather | solution.py:114
  390.9 43.2 %all-gather.25.cloned.1.call-done = bf16[1024,4096]{1,0:T(8,128)(2,1)} async-done(((bf16[128,4096]{1,0:T(8,128)(2,1)}), bf16[1024,4096]{1,0:T(8,128)(2,1)}) %all-gather.25.cloned.1.call-update) | async-done | bytes 8388624 | tf_op jit(solution)/shard_map/all_gather | solution.py:319
  442.0 48.4 %all-gather.29.cloned.1.call-done = bf16[4096,1024]{1,0:T(8,128)(2,1)} async-done(((bf16[512,1024]{1,0:T(8,128)(2,1)}), bf16[4096,1024]{1,0:T(8,128)(2,1)}) %all-gather.29.cloned.1.call-update) | async-done | bytes 8388624 | tf_op jit(solution)/shard_map/all_gather | solution.py:320
  498.2 19.9 all-gather.31.cloned.1.call-done
  630.7 93.0 %gather_fusion = f32[24576,4]{1,0:T(8,128)} fusion(f32[4,18432]{0,1:T(8,128)} %copy.158, s32[24576]{0:T(1024)} %broadcast_clamp_fusion.1), kind=kCustom, calls=%fused_computation.clone | custom fusion | bytes 884736 | tf_op jit(solution)/shard_map/jvp(jit(_take))/gather | solution.py:69
  763.3 93.0 %gather_fusion.1 = f32[24576,4]{1,0:T(8,128)} fusion(f32[4,18432]{0,1:T(8,128)} %copy.167, s32[24576]{0:T(1024)} %broadcast_clamp_fusion), kind=kCustom, calls=%fused_computation.1.clone | custom fusion | bytes 884736 | tf_op jit(solution)/shard_map/jvp(jit(_take))/gather | solution.py:69
  883.6 135.1 %scatter_custom_fusion.1 = f32[4,18432]{0,1:T(8,128)} fusion(s32[24576]{0:T(1024)} %reshape.596, f32[24576,4]{1,0:T(8,128)} %bitcast.259, f32[]{:T(128)} %constant.204.clone.1), kind=kCustom, calls=%fused_computation.51 | custom fusion | flops 98304 | bytes 295424 | tf_op jit(solution)/shard_map/transpose(jvp(jit(_take)))/scatter-add | solution.py:69
  1055.0 135.5 %scatter_custom_fusion = f32[4,18432]{0,1:T(8,128)} fusion(s32[24576]{0:T(1024)} %reshape.588, f32[24576,4]{1,0:T(8,128)} %bitcast.260, f32[]{:T(128)} %constant.204.clone.1), kind=kCustom, calls=%fused_computation.53 | custom fusion | flops 98304 | bytes 295424 | tf_op jit(solution)/shard_map/transpose(jvp(jit(_take)))/scatter-add | solution.py:69
  1302.0 31.2 %convert_bitcast_fusion.1 = bf16[1024,16,64]{0,2,1:T(8,128)(2,1)} fusion(f32[16,256,1024]{2,1,0:T(8,128)} %fusion.75, f32[16,256,1024]{2,1,0:T(8,128)} %copy-done.3, f32[16,256]{1,0:T(8,128)S(1)} %copy-done.118, pred[1024]{0:T(1024)(128)(4,1)S(1)} %copy-done.155, bf16[256,3,16,64]{0,3,2,1:T(8,128)(2,1)} %bitcast.266), kind=kOutput, calls=%fused_computation.89 | convolution fusion | flops 584061952 | bytes 69765120 | tf_op jit(solution)/shard_map/hqk,qhd->khd/dot_general | solution.py:203
  1361.0 31.7 %convert_bitcast_fusion.3 = bf16[1024,16,64]{0,2,1:T(8,128)(2,1)} fusion(f32[16,256,1024]{2,1,0:T(8,128)} %fusion.82, f32[16,256,1024]{2,1,0:T(8,128)} %copy-done.2, f32[16,256]{1,0:T(8,128)S(1)} %copy-done.116, pred[1024]{0:T(1024)(128)(4,1)S(1)} %copy-done.153, bf16[256,3,16,64]{0,3,2,1:T(8,128)(2,1)} %bitcast.263), kind=kOutput, calls=%fused_computation.91 | convolution fusion | flops 584061952 | bytes 69765120 | tf_op jit(solution)/shard_map/hqk,qhd->khd/dot_general | solution.py:203
  1410.9 29.9 %fusion.118 = bf16[256,1,16,64]{0,3,2,1:T(8,128)(2,1)S(1)} fusion(f32[16,256,1024]{2,1,0:T(8,128)} %fusion.75, f32[16,256,1024]{2,1,0:T(8,128)} %copy-done.3, f32[16,256]{1,0:T(8,128)S(1)} %copy-done.118, pred[1024]{0:T(1024)(128)(4,1)S(1)} %copy-done.155, bf16[1024,1,16,64]{0,3,2,1:T(8,128)(2,1)} %all-gather.39.cloned.1.call-done), kind=kOutput, calls=%fused_computation.122 | convolution fusion | flops 583275520 | bytes 36193280 | tf_op jit(solution)/shard_map/hqk,khd->qhd/dot_general | solution.py:197
  1440.7 30.0 %fusion.113 = bf16[256,1,16,64]{0,3,2,1:T(8,128)(2,1)S(1)} fusion(f32[16,256,1024]{2,1,0:T(8,128)} %fusion.82, f32[16,256,1024]{2,1,0:T(8,128)} %copy-done.2, f32[16,256]{1,0:T(8,128)S(1)} %copy-done.116, pred[1024]{0:T(1024)(128)(4,1)S(1)} %copy-done.153, bf16[1024,1,16,64]{0,3,2,1:T(8,128)(2,1)} %all-gather.35.cloned.1.call-done), kind=kOutput, calls=%fused_computation.121 | convolution fusion | flops 583275520 | bytes 36193280 | tf_op jit(solution)/shard_map/hqk,khd->qhd/dot_general | solution.py:197
  1473.3 40.2 %reduce-scatter.19.cloned.1.call-done = bf16[256,16,64]{0,2,1:T(8,128)(2,1)} async-done(((bf16[1024,16,64]{0,2,1:T(8,128)(2,1)}), bf16[256,16,64]{0,2,1:T(8,128)(2,1)}) %reduce-scatter.19.cloned.1.call-update) | async-done | bytes 524304 | tf_op jit(solution)/shard_map/reduce_scatter | solution.py:208
  1597.6 28.8 %reduce-scatter.25.cloned.1.call-done = bf16[144,1024]{1,0:T(8,128)(2,1)} async-done(((bf16[576,1024]{1,0:T(8,128)(2,1)}), bf16[144,1024]{1,0:T(8,128)(2,1)}) %reduce-scatter.25.cloned.1.call-update) | async-done | bytes 294928 | tf_op jit(solution)/shard_map/reduce_scatter | solution.py:352
  1628.3 109.8 %reduce-scatter.29.cloned.1.call-done = bf16[1024,768]{1,0:T(8,128)(2,1)} async-done(((bf16[1024,3072]{1,0:T(8,128)(2,1)}), bf16[1024,768]{1,0:T(8,128)(2,1)}) %reduce-scatter.29.cloned.1.call-update) | async-done | bytes 1572880 | tf_op jit(solution)/shard_map/reduce_scatter | solution.py:355
  1741.5 144.1 %reduce-scatter.37.cloned.1.call-done = bf16[1024,1024]{1,0:T(8,128)(2,1)} async-done(((bf16[1024,4096]{1,0:T(8,128)(2,1)}), bf16[1024,1024]{1,0:T(8,128)(2,1)}) %reduce-scatter.37.cloned.1.call-update) | async-done | bytes 2097168 | tf_op jit(solution)/shard_map/reduce_scatter | solution.py:361
  1890.0 143.3 %reduce-scatter.41.cloned.1.call-done = bf16[4096,256]{1,0:T(8,128)(2,1)} async-done(((bf16[4096,1024]{1,0:T(8,128)(2,1)}), bf16[4096,256]{1,0:T(8,128)(2,1)}) %reduce-scatter.41.cloned.1.call-update) | async-done | bytes 2097168 | tf_op jit(solution)/shard_map/reduce_scatter | solution.py:364
  2048.1 24.3 %reduce-scatter.47.cloned.1.call-done = f32[128,192]{0,1:T(8,128)} async-done(((f32[1024,192]{0,1:T(8,128)}), f32[128,192]{0,1:T(8,128)}) %reduce-scatter.47.cloned.1.call-update) | async-done | bytes 98320 | tf_op jit(solution)/shard_map/reduce_scatter | solution.py:377
  2074.0 37.9 %reduce-scatter.35.cloned.1.call-done = f32[128,256]{1,0:T(8,128)} async-done(((f32[1024,256]{1,0:T(8,128)}), f32[128,256]{1,0:T(8,128)}) %reduce-scatter.35.cloned.1.call-update) | async-done | bytes 131088 | tf_op jit(solution)/shard_map/reduce_scatter | solution.py:374
  2113.4 35.7 %reduce-scatter.27.cloned.1.call-done = f32[144,128]{1,0:T(8,128)} async-done(((f32[144,1024]{1,0:T(8,128)}), f32[144,128]{1,0:T(8,128)}) %reduce-scatter.27.cloned.1.call-update) | async-done | bytes 73744 | tf_op jit(solution)/shard_map/reduce_scatter | solution.py:372
  2150.6 48.4 %reduce-scatter.31.cloned.1.call-done = f32[128,768]{1,0:T(8,128)} async-done(((f32[1024,768]{1,0:T(8,128)}), f32[128,768]{1,0:T(8,128)}) %reduce-scatter.31.cloned.1.call-update) | async-done | bytes 393232 | tf_op jit(solution)/shard_map/reduce_scatter | solution.py:373
  2202.7 50.9 %reduce-scatter.39.cloned.1.call-done = f32[128,1024]{1,0:T(8,128)} async-done(((f32[1024,1024]{1,0:T(8,128)}), f32[128,1024]{1,0:T(8,128)}) %reduce-scatter.39.cloned.1.call-update) | async-done | bytes 524304 | tf_op jit(solution)/shard_map/reduce_scatter | solution.py:375
  2256.1 52.6 %reduce-scatter.43.cloned.1.call-done = f32[512,256]{1,0:T(8,128)} async-done(((f32[4096,256]{1,0:T(8,128)}), f32[512,256]{1,0:T(8,128)}) %reduce-scatter.43.cloned.1.call-update) | async-done | bytes 524304 | tf_op jit(solution)/shard_map/reduce_scatter | solution.py:376
  2311.7 40.2 %all-reduce.10 = (f32[]{:T(128)}, f32[]{:T(128)}, f32[14080]{0:T(1024)S(1)}) all-reduce(f32[]{:T(128)S(6)} %add.563, f32[]{:T(128)S(6)} %add.584, f32[14080]{0:T(1024)S(1)} %add.585), channel_id=1, replica_groups=mesh['scene'=8,'rows'=4] {'scene','rows'}, use_global_device_ids=true, to_apply=%region_28.30 | all-reduce | flops 14082 | bytes 112656 | tf_op jit(solution)/shard_map/psum | solution.py:379
  (691 shorter events, 636.9 us)
Async XLA Ops:
  7.2 42.4 %all-gather.17.cloned.1.call-start = ((), (), s32[]{:S(2)}) async-start(), calls=%async_computation.16 | async-start | bytes 1327104 | tf_op jit(solution)/shard_map/all_gather | solution.py:316
  24.1 73.0 %all-gather.19.cloned.1.call-start = ((), (), s32[]{:S(2)}) async-start(), calls=%async_computation.17 | async-start | bytes 7077888 | tf_op jit(solution)/shard_map/all_gather | solution.py:317
  43.2 94.9 %all-gather.23.cloned.1.call-start = ((), (), s32[]{:S(2)}) async-start(), calls=%async_computation.19 | async-start | bytes 1310720 | tf_op jit(solution)/shard_map/all_gather | solution.py:311
  45.0 118.0 %all-gather.27.cloned.1.call-start = ((), (), s32[]{:S(2)}) async-start(), calls=%async_computation.21 | async-start | bytes 1310720 | tf_op jit(solution)/shard_map/all_gather | solution.py:312
  45.8 165.9 %all-gather.35.cloned.1.call-start = ((), (), s32[]{:S(2)}) async-start(), calls=%async_computation.41 | async-start | bytes 2621440 | tf_op jit(solution)/shard_map/all_gather | solution.py:113
  105.8 150.8 %all-gather.33.cloned.1.call-start = ((), (), s32[]{:S(2)}) async-start(), calls=%async_computation.40 | async-start | bytes 2621440 | tf_op jit(solution)/shard_map/all_gather | solution.py:114
  106.4 178.3 %all-gather.21.cloned.1.call-start = ((), (), s32[]{:S(2)}) async-start(), calls=%async_computation.18 | async-start | bytes 2359296 | tf_op jit(solution)/shard_map/all_gather | solution.py:318
  123.3 209.7 %all-gather.39.cloned.1.call-start = ((), (), s32[]{:S(2)}) async-start(), calls=%async_computation.43 | async-start | bytes 2621440 | tf_op jit(solution)/shard_map/all_gather | solution.py:113
  137.3 242.4 %all-gather.37.cloned.1.call-start = ((), (), s32[]{:S(2)}) async-start(), calls=%async_computation.42 | async-start | bytes 2621440 | tf_op jit(solution)/shard_map/all_gather | solution.py:114
  138.0 296.1 %all-gather.25.cloned.1.call-start = ((), (), s32[]{:S(2)}) async-start(), calls=%async_computation.20 | async-start | bytes 9437184 | tf_op jit(solution)/shard_map/all_gather | solution.py:319
  138.6 351.8 %all-gather.29.cloned.1.call-start = ((), (), s32[]{:S(2)}) async-start(), calls=%async_computation.22 | async-start | bytes 9437184 | tf_op jit(solution)/shard_map/all_gather | solution.py:320
  163.1 355.0 %all-gather.31.cloned.1.call-start = ((), (), s32[]{:S(2)}) async-start(), calls=%async_computation.23 | async-start | bytes 1769472 | tf_op jit(solution)/shard_map/all_gather | solution.py:321
  178.3 1292.5 %reduce-scatter.21.cloned.1.call-start = ((), (), s32[]{:S(2)}) async-start(), calls=%async_computation.26 | async-start | bytes 2621440 | tf_op jit(solution)/shard_map/reduce_scatter | solution.py:205
  537.1 34.8 %collective-permute-start.2 = (bf16[16,768]{1,0:T(8,128)(2,1)}, bf16[16,768]{1,0:T(8,128)(2,1)}, u32[]{:S(2)}, u32[]{:S(2)}) collective-permute-start(bf16[16,768]{1,0:T(8,128)(2,1)} %get-tuple-element.172), channel_id=1, source_target_pairs={{0,1},{1,2},{2,3},{4,5},{5,6},{6,7},{8,9},{9,10},{10,11},{12,13},{... | collective-permute-start | bytes 73736 | tf_op jit(solution)/shard_map/ppermute | solution.py:29
  541.6 30.3 %collective-permute-start.3 = (bf16[16,768]{1,0:T(8,128)(2,1)}, bf16[16,768]{1,0:T(8,128)(2,1)}, u32[]{:S(2)}, u32[]{:S(2)}) collective-permute-start(bf16[16,768]{1,0:T(8,128)(2,1)} %get-tuple-element.173), channel_id=1, source_target_pairs={{1,0},{2,1},{3,2},{5,4},{6,5},{7,6},{9,8},{10,9},{11,10},{13,12},{... | collective-permute-start | bytes 73736 | tf_op jit(solution)/shard_map/ppermute | solution.py:30
  1033.9 214.8 %collective-permute-start.6 = (bf16[16,768]{1,0:T(8,128)(2,1)S(1)}, bf16[16,768]{1,0:T(8,128)(2,1)}, u32[]{:S(2)}, u32[]{:S(2)}) collective-permute-start(bf16[16,768]{1,0:T(8,128)(2,1)S(1)} %slice.327), channel_id=1, source_target_pairs={{0,1},{1,2},{2,3},{4,5},{5,6},{6,7},{8,9},{9,10},{10,11},{12,13},{... | collective-permute-start | bytes 73736 | tf_op jit(solution)/shard_map/ppermute | solution.py:29
  1042.5 206.1 %collective-permute-start.7 = (bf16[16,768]{1,0:T(8,128)(2,1)}, bf16[16,768]{1,0:T(8,128)(2,1)}, u32[]{:S(2)}, u32[]{:S(2)}) collective-permute-start(bf16[16,768]{1,0:T(8,128)(2,1)} %slice.329), channel_id=1, source_target_pairs={{1,0},{2,1},{3,2},{5,4},{6,5},{7,6},{9,8},{10,9},{11,10},{13,12},{... | collective-permute-start | bytes 73736 | tf_op jit(solution)/shard_map/ppermute | solution.py:30
  1333.2 137.6 %reduce-scatter.23.cloned.1.call-start = ((), (), s32[]{:S(2)}) async-start(), calls=%async_computation.27 | async-start | bytes 2621440 | tf_op jit(solution)/shard_map/reduce_scatter | solution.py:208
  1344.9 128.5 %reduce-scatter.17.cloned.1.call-start = ((), (), s32[]{:S(2)}) async-start(), calls=%async_computation.24 | async-start | bytes 2621440 | tf_op jit(solution)/shard_map/reduce_scatter | solution.py:205
  1392.8 120.8 %reduce-scatter.19.cloned.1.call-start = ((), (), s32[]{:S(2)}) async-start(), calls=%async_computation.25 | async-start | bytes 2621440 | tf_op jit(solution)/shard_map/reduce_scatter | solution.py:208
  1402.7 185.0 %reduce-scatter.45.cloned.1.call-start = ((), (), s32[]{:S(2)}) async-start(), calls=%async_computation.38 | async-start | bytes 1966080 | tf_op jit(solution)/shard_map/reduce_scatter | solution.py:367
  1406.8 188.6 %reduce-scatter.33.cloned.1.call-start = ((), (), s32[]{:S(2)}) async-start(), calls=%async_computation.32 | async-start | bytes 2621440 | tf_op jit(solution)/shard_map/reduce_scatter | solution.py:358
  1410.8 215.5 %reduce-scatter.25.cloned.1.call-start = ((), (), s32[]{:S(2)}) async-start(), calls=%async_computation.28 | async-start | bytes 1474560 | tf_op jit(solution)/shard_map/reduce_scatter | solution.py:352
  1530.5 207.5 %reduce-scatter.29.cloned.1.call-start = ((), (), s32[]{:S(2)}) async-start(), calls=%async_computation.30 | async-start | bytes 7864320 | tf_op jit(solution)/shard_map/reduce_scatter | solution.py:355
  1539.1 346.5 %reduce-scatter.37.cloned.1.call-start = ((), (), s32[]{:S(2)}) async-start(), calls=%async_computation.34 | async-start | bytes 10485760 | tf_op jit(solution)/shard_map/reduce_scatter | solution.py:361
  1562.0 471.3 %reduce-scatter.41.cloned.1.call-start = ((), (), s32[]{:S(2)}) async-start(), calls=%async_computation.36 | async-start | bytes 10485760 | tf_op jit(solution)/shard_map/reduce_scatter | solution.py:364
  1587.6 484.9 %reduce-scatter.47.cloned.1.call-start = ((), (), s32[]{:S(2)}) async-start(), calls=%async_computation.39 | async-start | bytes 884736 | tf_op jit(solution)/shard_map/reduce_scatter | solution.py:377
  1589.7 522.2 %reduce-scatter.35.cloned.1.call-start = ((), (), s32[]{:S(2)}) async-start(), calls=%async_computation.33 | async-start | bytes 1179648 | tf_op jit(solution)/shard_map/reduce_scatter | solution.py:374
  1597.5 551.6 %reduce-scatter.27.cloned.1.call-start = ((), (), s32[]{:S(2)}) async-start(), calls=%async_computation.29 | async-start | bytes 663552 | tf_op jit(solution)/shard_map/reduce_scatter | solution.py:372
  1628.2 570.8 %reduce-scatter.31.cloned.1.call-start = ((), (), s32[]{:S(2)}) async-start(), calls=%async_computation.31 | async-start | bytes 3538944 | tf_op jit(solution)/shard_map/reduce_scatter | solution.py:373
  1741.4 512.1 %reduce-scatter.39.cloned.1.call-start = ((), (), s32[]{:S(2)}) async-start(), calls=%async_computation.35 | async-start | bytes 4718592 | tf_op jit(solution)/shard_map/reduce_scatter | solution.py:375
  1889.7 418.9 %reduce-scatter.43.cloned.1.call-start = ((), (), s32[]{:S(2)}) async-start(), calls=%async_computation.37 | async-start | bytes 4718592 | tf_op jit(solution)/shard_map/reduce_scatter | solution.py:376
  (178 other events, 10300.8 us)
Sparse Core Ops, SparseCore 0:
  24.2 25.3 all-gather.16
  51.5 45.5 all-gather.18
  99.2 32.1 all-gather.22
  133.4 29.6 all-gather.26
  165.1 46.6 all-gather.34
  213.7 42.8 all-gather.32
  258.5 26.1 all-gather.20
  286.8 46.2 all-gather.38
  335.2 44.4 all-gather.36
  381.4 52.6 all-gather.24
  436.0 54.3 all-gather.28
  492.2 25.8 all-gather.30
  1333.3 43.6 reduce-scatter.20
  1379.3 43.2 reduce-scatter.22
  1424.7 43.3 reduce-scatter.16
  1470.3 43.1 reduce-scatter.18
  1515.7 34.6 reduce-scatter.44
  1552.5 42.8 reduce-scatter.32
  1597.8 28.4 reduce-scatter.24
  1628.6 109.4 reduce-scatter.28
  1740.6 144.9 reduce-scatter.36
  1888.1 145.1 reduce-scatter.40
  2036.8 35.6 reduce-scatter.46
  2075.8 36.0 reduce-scatter.34
  2115.4 33.7 reduce-scatter.26
  2152.7 46.2 reduce-scatter.30
  2202.2 51.3 reduce-scatter.38
  2257.3 51.3 reduce-scatter.42
where the time goes:
time: 2390 us; the launch traced here: 2370 us
  waiting for transfers between devices  1070 us (45%)
  local copies, waits for them, and re-layouts  415 us (17%)
  other arithmetic  383 us (16%)
  matrix products  349 us (15%)
  blocking collectives  106 us (4%)
  between operations  26.9 us (1%)
  starting transfers between devices  25.9 us (1%)
    scatter-add x2, other arithmetic, render_sum(): picked = jnp.take(table, index, axis=1)  271 us
    gather x4, local copies, waits for them, and re-layouts, render_sum(): picked = jnp.take(table, index, axis=1)  203 us
    reduce_scatter x1, waiting for transfers between devices, body(): lax.psum_scatter(totals[3].astype(jnp.bfloat16), 'rows', scatter_dimensio...  144 us
    reduce_scatter x1, waiting for transfers between devices, body(): lax.psum_scatter(totals[4].astype(jnp.bfloat16), 'rows', scatter_dimensio...  143 us
    reduce_scatter x1, waiting for transfers between devices, body(): lax.psum_scatter(totals[1].astype(jnp.bfloat16), 'rows', scatter_dimensio...  110 us
    all_gather x2, waiting for transfers between devices, layer_forward(): lax.all_gather(projected[:, 2], 'rows', axis=0, tiled=True)  70.8 us
    all_gather x2, waiting for transfers between devices, layer_forward(): lax.all_gather(projected[:, 1], 'rows', axis=0, tiled=True)  67.4 us
    dot_general x12, matrix products, left_product(): lax.dot_general(left, right, (((0,), (0,)), ((), ())), preferred_element_...  65.7 us
  transfers between devices with their start and end apart: 36, of which 24 were waited for; matrix products, arithmetic and copies ran while one was open for 24% of the time, Pallas kernels for 0%

commit v1 on v0

v1 whole, which is shorter than its diff:
```python
import functools

import jax
import jax.numpy as jnp
import numpy as np
from jax import lax
from jax.experimental import pallas as pl
from jax.experimental.pallas import tpu as pltpu
from jax.sharding import PartitionSpec as P

D = 1024
HEADS = 16
HD = 64
FF = 4096
POUT = 768
HT = 16
GV = 12
NG = POUT // GV

EPSILON = 1e-05
CLIP_NORM = 0.002
STEP_RATE = 1250.0
MOMENTUM = 0.9
AVERAGE_DECAY = 0.9

F32 = jnp.float32
BF16 = jnp.bfloat16
HIGHEST = lax.Precision.HIGHEST
BLOCKS = 8
WIDE = D // BLOCKS
VMEM_MB = 1024 * 1024
TABLE = NG + 8


def nn(a, b):
    return lax.dot_general(a, b, (((1,), (0,)), ((), ())), preferred_element_type=F32)


def nt(a, b):
    return lax.dot_general(a, b, (((1,), (1,)), ((), ())), preferred_element_type=F32)


def tn(a, b):
    return lax.dot_general(a, b, (((0,), (0,)), ((), ())), preferred_element_type=F32)


def params(mb, n=1):
    return pltpu.CompilerParams(
        vmem_limit_bytes=mb * VMEM_MB, dimension_semantics=("arbitrary",) * n
    )


def lane_block(index, width):
    return pl.ds(pl.multiple_of(index * width, width), width)


def norm_store(perm, h_ref, g_ref, s_ref, a_ref, chunk):
    def step(i, carry):
        rows = pl.ds(pl.multiple_of(i * chunk, chunk), chunk)
        h = h_ref[rows, :]
        c = h - jnp.mean(h, axis=1, keepdims=True)
        var = jnp.mean(c * c, axis=1, keepdims=True)
        a = (c * lax.rsqrt(var + EPSILON) * g_ref[...] + s_ref[...]).astype(BF16)
        for b in range(BLOCKS):
            a_ref[rows, lane_block(perm[8 + b], WIDE)] = a[:, b * WIDE : (b + 1) * WIDE]
        return carry

    lax.fori_loop(0, h_ref.shape[0] // chunk, step, 0)


def embed_kernel(perm, x_ref, w_ref, b_ref, g_ref, s_ref, h_ref, a_ref):
    hr = nt(x_ref[...], w_ref[...])
    for j in range(BLOCKS):
        cols = lane_block(perm[j], WIDE)
        h_ref[:, cols] = hr[:, j * WIDE : (j + 1) * WIDE] + b_ref[:, cols]
    norm_store(perm, h_ref, g_ref, s_ref, a_ref, 32)


def embed(perm, x, w, b, g, s):
    rows, pin = x.shape
    part = 256
    full = lambda shape: pl.BlockSpec(shape, lambda i, p: (0, 0))
    tile = lambda n: pl.BlockSpec((part, n), lambda i, p: (i, 0))
    return pl.pallas_call(
        embed_kernel,
        grid_spec=pltpu.PrefetchScalarGridSpec(
            num_scalar_prefetch=1,
            grid=(rows // part,),
            in_specs=[tile(pin), full((D, pin)), full((1, D)), full((1, D)), full((1, D))],
            out_specs=[tile(D), tile(D)],
        ),
        out_shape=[jax.ShapeDtypeStruct((rows, D), F32), jax.ShapeDtypeStruct((rows, D), BF16)],
        compiler_params=params(32),
        cost_estimate=pl.CostEstimate(
            flops=2 * rows * D * pin, bytes_accessed=rows * D * 6 + 4 * D * pin, transcendentals=0
        ),
        name="embed_norm",
    )(perm, x, w, b, g, s)


def project_kernel(perm, a_ref, w_ref, r_ref, b_ref, g_ref, s_ref, h_ref, n_ref):
    k = pl.program_id(0)

    @pl.when(k == 0)
    def _():
        h_ref[...] = r_ref[...] + b_ref[...] + nn(a_ref[...], w_ref[...])

    @pl.when(k > 0)
    def _():
        h_ref[...] = h_ref[...] + nn(a_ref[...], w_ref[...])

    @pl.when(k == pl.num_programs(0) - 1)
    def _():
        norm_store(perm, h_ref, g_ref, s_ref, n_ref, 32)


def project(perm, a, w, res, b, g, s):
    rows, depth = a.shape
    part = 512
    full = lambda shape: pl.BlockSpec(shape, lambda k, p: (0, 0))
    return pl.pallas_call(
        project_kernel,
        grid_spec=pltpu.PrefetchScalarGridSpec(
            num_scalar_prefetch=1,
            grid=(depth // part,),
            in_specs=[
                pl.BlockSpec((rows, part), lambda k, p: (0, k)),
                pl.BlockSpec((part, D), lambda k, p: (k, 0)),
                full((rows, D)),
                full((1, D)),
                full((1, D)),
                full((1, D)),
            ],
            out_specs=[full((rows, D)), full((rows, D))],
        ),
        out_shape=[jax.ShapeDtypeStruct((rows, D), F32), jax.ShapeDtypeStruct((rows, D), BF16)],
        compiler_params=params(40),
        cost_estimate=pl.CostEstimate(
            flops=2 * rows * D * depth,
            bytes_accessed=rows * D * 10 + 2 * D * depth + 2 * rows * depth,
            transcendentals=0,
        ),
        name="project_norm",
    )(perm, a, w, res, b, g, s)


GELU_C = float(np.sqrt(2.0 / np.pi))


def up_kernel(perm, a_ref, w_ref, b_ref, u_ref, g_ref):
    u = nn(a_ref[...], w_ref[...]) + b_ref[...]
    u_ref[...] = u
    t = jnp.tanh(GELU_C * (u + 0.044715 * (u * u * u)))
    g_ref[...] = (u * (0.5 * (1.0 + t))).astype(BF16)


def up_project(perm, a, w, b):
    rows = a.shape[0]
    part = FF // BLOCKS
    return pl.pallas_call(
        up_kernel,
        grid_spec=pltpu.PrefetchScalarGridSpec(
            num_scalar_prefetch=1,
            grid=(BLOCKS,),
            in_specs=[
                pl.BlockSpec((rows, D), lambda n, p: (0, 0)),
                pl.BlockSpec((D, part), lambda n, p: (0, n)),
                pl.BlockSpec((1, part), lambda n, p: (0, n)),
            ],
            out_specs=[
                pl.BlockSpec((rows, part), lambda n, p: (0, n)),
                pl.BlockSpec((rows, part), lambda n, p: (0, p[8 + n])),
            ],
        ),
        out_shape=[jax.ShapeDtypeStruct((rows, FF), F32), jax.ShapeDtypeStruct((rows, FF), BF16)],
        compiler_params=params(32),
        cost_estimate=pl.CostEstimate(
            flops=2 * rows * D * FF, bytes_accessed=rows * FF * 6 + 2 * D * FF, transcendentals=rows * FF
        ),
        name="up_gelu",
    )(perm, a, w, b)


def down_back_kernel(perm, d_ref, w_ref, u_ref, du_ref, sum_ref):
    dg = nt(d_ref[...], w_ref[...])
    u = u_ref[...]
    u2 = u * u
    t = jnp.tanh(GELU_C * (u + 0.044715 * (u2 * u)))
    slope = 0.5 * (1.0 + t) + (0.5 * GELU_C) * u * (1.0 - t * t) * (1.0 + (3 * 0.044715) * u2)
    du = slope * dg
    du_ref[...] = du.astype(BF16)
    sum_ref[...] = jnp.sum(du, axis=0, keepdims=True)


def down_back(perm, d, w, u):
    rows = d.shape[0]
    part = FF // BLOCKS
    return pl.pallas_call(
        down_back_kernel,
        grid_spec=pltpu.PrefetchScalarGridSpec(
            num_scalar_prefetch=1,
            grid=(BLOCKS,),
            in_specs=[
                pl.BlockSpec((rows, D), lambda j, p: (0, 0)),
                pl.BlockSpec((part, D), lambda j, p: (j, 0)),
                pl.BlockSpec((rows, part), lambda j, p: (0, p[j])),
            ],
            out_specs=[
                pl.BlockSpec((rows, part), lambda j, p: (0, p[j])),
                pl.BlockSpec((1, part), lambda j, p: (0, p[j])),
            ],
        ),
        out_shape=[jax.ShapeDtypeStruct((rows, FF), BF16), jax.ShapeDtypeStruct((1, FF), F32)],
        compiler_params=params(32),
        cost_estimate=pl.CostEstimate(
            flops=2 * rows * D * FF, bytes_accessed=rows * FF * 6 + 2 * D * FF, transcendentals=rows * FF
        ),
        name="down_back_gelu",
    )(perm, d, w, u)


def back_kernel(has_res, placed, perm, *refs):
    if has_res:
        d_ref, w_ref, h_ref, g_ref, r_ref, *outs = refs
    else:
        d_ref, w_ref, h_ref, g_ref, *outs = refs
        r_ref = None
    if placed:
        low_ref, sums_ref, acc_ref, part_ref = outs
        dh_ref = None
    else:
        dh_ref, low_ref, sums_ref, acc_ref, part_ref = outs
    n = pl.program_id(0)

    @pl.when(n == 0)
    def _():
        acc_ref[...] = nt(d_ref[...], w_ref[...])

    @pl.when(n > 0)
    def _():
        acc_ref[...] = acc_ref[...] + nt(d_ref[...], w_ref[...])

    @pl.when(n == pl.num_programs(0) - 1)
    def _():
        chunk = 32
        part_ref[...] = jnp.zeros_like(part_ref)

        def fold(x):
            return jnp.sum(x.reshape(chunk // 8, 8, D), axis=0)

        def step(i, carry):
            rows = pl.ds(pl.multiple_of(i * chunk, chunk), chunk)
            h = h_ref[rows, :]
            c = h - jnp.mean(h, axis=1, keepdims=True)
            var = jnp.mean(c * c, axis=1, keepdims=True)
            rstd = lax.rsqrt(var + EPSILON)
            xh = c * rstd
            da = jnp.concatenate(
                [acc_ref[rows, lane_block(perm[8 + b], WIDE)] for b in range(BLOCKS)], axis=1
            )
            dxh = da * xh
            part_ref[0] += fold(dxh)
            part_ref[1] += fold(da)
            dy = da * g_ref[...]
            first = jnp.mean(dy, axis=1, keepdims=True)
            second = jnp.mean(dy * xh, axis=1, keepdims=True)
            dh = rstd * (dy - first - xh * second)
            if has_res:
                dh = dh + r_ref[rows, :]
            part_ref[2] += fold(dh)
            low = dh.astype(BF16)
            if placed:
                for b in range(BLOCKS):
                    low_ref[rows, lane_block(perm[8 + b], WIDE)] = low[:, b * WIDE : (b + 1) * WIDE]
            else:
                dh_ref[rows, :] = dh
                low_ref[rows, :] = low
            return carry

        lax.fori_loop(0, h_ref.shape[0] // chunk, step, 0)
        sums_ref[...] = jnp.concatenate(
            [jnp.sum(part_ref[i], axis=0, keepdims=True) for i in range(3)]
            + [jnp.zeros((5, D), F32)],
            axis=0,
        )


def norm_back(perm, d, w, h, g, res, placed):
    rows, wide = d.shape
    part = 768 if wide % 1024 else 1024
    full = lambda shape: pl.BlockSpec(shape, lambda n, p: (0, 0))
    args = [d, w, h, g]
    specs = [
        pl.BlockSpec((rows, part), lambda n, p: (0, n)),
        pl.BlockSpec((D, part), lambda n, p: (0, n)),
        full((rows, D)),
        full((1, D)),
    ]
    if res is not None:
        args.append(res)
        specs.append(full((rows, D)))
    out_specs = [full((rows, D)), full((8, D))]
    out_shape = [jax.ShapeDtypeStruct((rows, D), BF16), jax.ShapeDtypeStruct((8, D), F32)]
    if not placed:
        out_specs = [full((rows, D))] + out_specs
        out_shape = [jax.ShapeDtypeStruct((rows, D), F32)] + out_shape
    return pl.pallas_call(
        functools.partial(back_kernel, res is not None, placed),
        grid_spec=pltpu.PrefetchScalarGridSpec(
            num_scalar_prefetch=1,
            grid=(wide // part,),
            in_specs=specs,
            out_specs=out_specs,
            scratch_shapes=[pltpu.VMEM((rows, D), F32), pltpu.VMEM((3, 8, D), F32)],
        ),
        out_shape=out_shape,
        compiler_params=params(40),
        cost_estimate=pl.CostEstimate(
            flops=2 * rows * D * wide,
            bytes_accessed=rows * D * 14 + 2 * D * wide + 2 * rows * wide,
            transcendentals=0,
        ),
        name="norm_back",
    )(perm, *args)


SCALE = HD ** (-0.5)
PAIR = 2 * HD
PAIRS = HEADS // 2


def attend_kernel(perm, lens, q_ref, k0_ref, k1_ref, v0_ref, v1_ref, o_ref, l_ref):
    half = k0_ref.shape[0]
    lane = lax.broadcasted_iota(jnp.int32, (1, PAIR), 1)
    spot = lax.broadcasted_iota(jnp.int32, (1, half), 1)
    see = [spot < lens[0], spot < lens[1]]
    k0, k1, v0, v1 = k0_ref[...], k1_ref[...], v0_ref[...], v1_ref[...]
    chunk = 256
    for i in range(q_ref.shape[0] // chunk):
        rows = slice(i * chunk, (i + 1) * chunk)
        q = q_ref[rows, :] * SCALE
        outs = []
        logs = []
        for side in range(2):
            qm = jnp.where((lane < HD) == (side == 0), q, 0.0).astype(BF16)
            s0 = jnp.where(see[0], nt(qm, k0), -1e30)
            s1 = jnp.where(see[1], nt(qm, k1), -1e30)
            top = jnp.maximum(
                jnp.max(s0, axis=1, keepdims=True), jnp.max(s1, axis=1, keepdims=True)
            )
            e0 = jnp.exp(s0 - top)
            e1 = jnp.exp(s1 - top)
            total = jnp.sum(e0, axis=1, keepdims=True) + jnp.sum(e1, axis=1, keepdims=True)
            inv = 1.0 / total
            outs.append(nn((e0 * inv).astype(BF16), v0) + nn((e1 * inv).astype(BF16), v1))
            logs.append(top + jnp.log(total))
        o_ref[rows, :] = jnp.where(lane < HD, outs[0], outs[1]).astype(BF16)
        flat = jnp.where(lane < HD, logs[0], logs[1])
        turned = flat.T
        l_ref[0, 0:1, rows] = turned[0:1, :]
        l_ref[0, 1:2, rows] = turned[HD : HD + 1, :]


def attend(perm, lens, p, kv):
    rows = p.shape[0]
    block = lambda first: pl.BlockSpec((rows, PAIR), lambda h, m, n: (0, first + h))
    return pl.pallas_call(
        attend_kernel,
        grid_spec=pltpu.PrefetchScalarGridSpec(
            num_scalar_prefetch=2,
            grid=(PAIRS,),
            in_specs=[block(0), block(PAIRS), block(0), block(2 * PAIRS), block(PAIRS)],
            out_specs=[
                pl.BlockSpec((rows, PAIR), lambda h, m, n: (0, m[8 + h])),
                pl.BlockSpec((1, 8, rows), lambda h, m, n: (h, 0, 0)),
            ],
        ),
        out_shape=[
            jax.ShapeDtypeStruct((rows, D), BF16),
            jax.ShapeDtypeStruct((PAIRS, 8, rows), F32),
        ],
        compiler_params=params(40),
        cost_estimate=pl.CostEstimate(
            flops=8 * rows * rows * D,
            bytes_accessed=12 * rows * D,
            transcendentals=2 * rows * rows * HEADS,
        ),
        name="attend",
    )(perm, lens, p, p, kv, p, kv)


def attend_back_kernel(
    perm, lens, q_ref, k0_ref, k1_ref, v0_ref, v1_ref, do_ref, l_ref, dq_ref, own_ref, far_ref
):
    half = k0_ref.shape[0]
    lane = lax.broadcasted_iota(jnp.int32, (1, PAIR), 1)
    spot = lax.broadcasted_iota(jnp.int32, (half, 1), 0)
    see = [spot < lens[0], spot < lens[1]]
    keys = [k0_ref[...], k1_ref[...]]
    values = [v0_ref[...], v1_ref[...]]
    q_all, do_all = q_ref[...], do_ref[...]
    chunk = 256
    dk = [None, None]
    dv = [None, None]
    for i in range(q_ref.shape[0] // chunk):
        rows = slice(i * chunk, (i + 1) * chunk)
        dq = None
        for side in range(2):
            mine = (lane < HD) == (side == 0)
            qm = jnp.where(mine, q_all[rows, :], 0.0).astype(BF16)
            dom = jnp.where(mine, do_all[rows, :], 0.0).astype(BF16)
            qs = qm * SCALE
            logs = l_ref[0, side : side + 1, rows]
            probs = [
                jnp.exp(jnp.where(see[j], nt(keys[j], qs), -1e30) - logs) for j in range(2)
            ]
            da = [nt(values[j], dom) for j in range(2)]
            delta = sum(jnp.sum(probs[j] * da[j], axis=0, keepdims=True) for j in range(2))
            for j in range(2):
                ds = (probs[j] * (da[j] - delta) * SCALE).astype(BF16)
                km = jnp.where(mine, keys[j], 0.0).astype(BF16)
                term = tn(ds, km)
                dq = term if dq is None else dq + term
                term = nn(ds, qm)
                dk[j] = term if dk[j] is None else dk[j] + term
                term = nn(probs[j].astype(BF16), dom)
                dv[j] = term if dv[j] is None else dv[j] + term
        dq_ref[rows, :] = dq.astype(BF16)
    own_ref[0] = dk[0]
    own_ref[1] = dv[0]
    far_ref[0] = dk[1].astype(BF16)
    far_ref[1] = dv[1].astype(BF16)


def attend_back(perm, lens, p, kv, do, logs):
    rows = p.shape[0]
    block = lambda first: pl.BlockSpec((rows, PAIR), lambda h, m, n: (0, first + h))
    both = pl.BlockSpec((2, rows, PAIR), lambda h, m, n: (0, 0, h))
    return pl.pallas_call(
        attend_back_kernel,
        grid_spec=pltpu.PrefetchScalarGridSpec(
            num_scalar_prefetch=2,
            grid=(PAIRS,),
            in_specs=[
                block(0),
                block(PAIRS),
                block(0),
                block(2 * PAIRS),
                block(PAIRS),
                pl.BlockSpec((rows, PAIR), lambda h, m, n: (0, m[8 + h])),
                pl.BlockSpec((1, 8, rows), lambda h, m, n: (h, 0, 0)),
            ],
            out_specs=[block(0), both, both],
        ),
        out_shape=[
            jax.ShapeDtypeStruct((rows, D), BF16),
            jax.ShapeDtypeStruct((2, rows, D), F32),
            jax.ShapeDtypeStruct((2, rows, D), BF16),
        ],
        compiler_params=params(48),
        cost_estimate=pl.CostEstimate(
            flops=20 * rows * rows * D,
            bytes_accessed=28 * rows * D,
            transcendentals=2 * rows * rows * HEADS,
        ),
        name="attend_back",
    )(perm, lens, p, p, kv, p, kv, do, logs)


def iota(shape, dim):
    return lax.broadcasted_iota(jnp.int32, shape, dim)


def render_kernel(
    terms, views_ref, inv_ref, z_ref, zx_ref, rd_ref, mc_ref, dz_ref, dzx_ref, loss_ref,
    tf_ref, hi_ref, lo_ref, o_ref, wm_ref, a_ref, b_ref, dt_ref, tok_ref, edge_ref, zs_ref,
):
    width = 256
    pixels = rd_ref.shape[-1]
    kg = 8

    lanes = 128
    parts = z_ref.shape[1] // lanes
    for i in range(parts):
        zs_ref[i] = z_ref[:, i * lanes : (i + 1) * lanes]
    zs_ref[parts] = zx_ref[...]

    def values(i):
        return [zs_ref[i, pl.ds(v, NG, stride=GV), :] for v in range(GV)]

    def shade(z):
        colour = [jax.nn.sigmoid(z[i]) for i in range(3)]
        gate = jax.nn.sigmoid(z[3])
        square = z[4] * z[4]
        for i in range(5, GV):
            square = square + z[i] * z[i]
        opacity = gate * jnp.exp(-0.5 * (square / (GV - 4)))
        return colour, gate, opacity

    own_group = iota((NG, width), 0) % 16 == iota((NG, width), 1) // 16

    def spread(base):
        return (iota((128, width), 0) == base + iota((128, width), 1) % 16).astype(F32)

    def rim_rows(table, base):
        wide = lax.dot_general(
            table, spread(base), (((1,), (0,)), ((), ())), precision=HIGHEST,
            preferred_element_type=F32,
        )
        return jnp.sum(jnp.where(own_group, wide, 0.0).reshape(4, 16, width), axis=1)

    def rim_back(rows, base):
        wide = jnp.concatenate(
            [jnp.broadcast_to(rows[j : j + 1, :], (16, width)) for j in range(4)], axis=0
        )
        return lax.dot_general(
            jnp.where(own_group, wide, 0.0), spread(base), (((1,), (1,)), ((), ())),
            precision=HIGHEST, preferred_element_type=F32,
        )

    def place(i):
        if i == parts:
            return edge_ref, slice(0, lanes)
        return tok_ref, slice(i * lanes, (i + 1) * lanes)

    for i in range(parts + 1):
        out_ref, cols = place(i)
        colour, gate, opacity = shade(values(i))
        for ch in range(3):
            out_ref[ch * NG : (ch + 1) * NG, cols] = colour[ch] * opacity
        out_ref[3 * NG : 4 * NG, cols] = opacity

    for ch in range(4):
        rows = slice(ch * NG, (ch + 1) * NG)
        at = ch * TABLE
        tf_ref[0, at : at + NG, :] = tok_ref[rows, 0:width]
        tf_ref[1, at : at + NG, :] = tok_ref[rows, width : 2 * width]
        tf_ref[0, at + NG : at + NG + 4, :] = rim_rows(edge_ref[rows, :], 0)
        tf_ref[0, at + NG + 4 : at + NG + 8, :] = rim_rows(tok_ref[rows, width : width + 128], 0)
        tf_ref[1, at + NG : at + NG + 4, :] = rim_rows(tok_ref[rows, width - 128 : width], 112)
        tf_ref[1, at + NG + 4 : at + NG + 8, :] = rim_rows(edge_ref[rows, :], 16)
    for block in range(2):
        table = tf_ref[block]
        high = table.astype(BF16)
        hi_ref[block] = high
        lo_ref[block] = (table - high.astype(F32)).astype(BF16)
    dt_ref[...] = jnp.zeros_like(dt_ref)
    inverse = inv_ref[0]
    row_hi = iota((width, pixels), 0)
    row_lo = iota((TABLE, pixels), 0)

    def features(c):
        return jnp.tanh(mc_ref[0] * c[0] + mc_ref[1] * c[1] + mc_ref[2] * c[2])

    def view(t, loss):
        for block in range(2):
            r = rd_ref[block, t, 0:kg, :].astype(jnp.int32)
            weight = rd_ref[block, t, kg : 2 * kg, :]
            token = lax.shift_right_logical(r, 6)
            g = jnp.bitwise_and(r, NG - 1)
            after = token >= HT + width
            inside = jnp.logical_and(token >= HT, jnp.logical_not(after))
            rim = jnp.where(after, token - (HT + width), token)
            high = jnp.where(inside, token - HT, jnp.bitwise_and(g, 15) * 16 + rim)
            low = jnp.where(
                inside, g, NG + lax.shift_right_logical(g, 4) + jnp.where(after, 4, 0)
            )
            sums = [jnp.zeros((8, pixels), F32) for _ in range(4)]
            t_hi = hi_ref[block]
            t_lo = lo_ref[block]
            for k in range(kg):
                cols = slice(k * pixels, (k + 1) * pixels)
                one = jnp.where(row_hi == high[k : k + 1, :], 1.0, 0.0).astype(BF16)
                o_ref[:, cols] = one
                wm = jnp.where(row_lo == low[k : k + 1, :], weight[k : k + 1, :], 0.0)
                wm_ref[:, cols] = wm
                picked = nn(t_hi, one) + nn(t_lo, one)
                for ch in range(4):
                    part = picked[ch * TABLE : (ch + 1) * TABLE, :] * wm
                    sums[ch] = sums[ch] + jnp.sum(part.reshape(TABLE // 8, 8, pixels), axis=0)
            sums = [jnp.sum(s, axis=0, keepdims=True) for s in sums]
            scale = 1.0 / (1.0 + sums[3])
            seen = [sums[i] * scale for i in range(3)]
            goal = [rd_ref[block, t, 2 * kg + i : 2 * kg + i + 1, :] for i in range(3)]
            f_seen = features(seen)
            gap = f_seen - features(goal)
            diff = [seen[i] - goal[i] for i in range(3)]
            loss = loss + diff[0] * diff[0] + diff[1] * diff[1] + diff[2] * diff[2]
            loss = loss + 0.5 * jnp.sum(gap * gap, axis=0, keepdims=True)
            pull = gap * (1.0 - f_seen * f_seen)
            d_seen = [
                inverse * (2.0 * diff[i] + jnp.sum(pull * mc_ref[i], axis=0, keepdims=True))
                for i in range(3)
            ]
            d_sum = [d * scale for d in d_seen]
            d_sum.append(
                -(d_seen[0] * seen[0] + d_seen[1] * seen[1] + d_seen[2] * seen[2]) * scale
            )
            for k in range(kg):
                cols = slice(k * pixels, (k + 1) * pixels)
                wm = wm_ref[:, cols]
                full = jnp.concatenate([wm * d_sum[ch] for ch in range(4)], axis=0)
                first = full.astype(BF16)
                a_ref[:, cols] = first
                if terms > 1:
                    b_ref[:, cols] = (full - first.astype(F32)).astype(BF16)
            ones = o_ref[...]
            grad = nt(a_ref[...], ones)
            if terms > 1:
                grad = grad + nt(b_ref[...], ones)
            dt_ref[block] += grad
        return loss

    loss = lax.fori_loop(0, views_ref[0], view, jnp.zeros((1, pixels), F32))
    loss_ref[...] = jnp.broadcast_to(jnp.sum(loss, axis=1, keepdims=True), loss_ref.shape)

    for ch in range(4):
        rows = slice(ch * NG, (ch + 1) * NG)
        at = ch * TABLE + NG
        tok_ref[rows, 0:width] = dt_ref[0, at - NG : at, :]
        tok_ref[rows, width : 2 * width] = dt_ref[1, at - NG : at, :]
        tok_ref[rows, width : width + 128] += rim_back(dt_ref[0, at + 4 : at + 8, :], 0)
        tok_ref[rows, width - 128 : width] += rim_back(dt_ref[1, at : at + 4, :], 112)
        edge_ref[rows, :] = rim_back(dt_ref[0, at : at + 4, :], 0) + rim_back(
            dt_ref[1, at + 4 : at + 8, :], 16
        )

    for part in range(parts + 1):
        grad_ref, cols = place(part)
        z = values(part)
        colour, gate, opacity = shade(z)
        d = [grad_ref[i * NG : (i + 1) * NG, cols] for i in range(4)]
        d_opacity = d[3]
        for i in range(3):
            d_opacity = d_opacity + d[i] * colour[i]
            zs_ref[part, pl.ds(i, NG, stride=GV), :] = d[i] * opacity * colour[i] * (1.0 - colour[i])
        both = d_opacity * opacity
        zs_ref[part, pl.ds(3, NG, stride=GV), :] = both * (1.0 - gate)
        for i in range(4, GV):
            zs_ref[part, pl.ds(i, NG, stride=GV), :] = both * z[i] * (-1.0 / (GV - 4))
    for i in range(parts):
        dz_ref[:, i * lanes : (i + 1) * lanes] = zs_ref[i]
    dzx_ref[...] = zs_ref[parts]


def render(views, inverse, zt, zx, rd, terms):
    tokens = zt.shape[1]
    pixels = rd.shape[-1]
    slots = 8 * pixels
    counter = np.arange(48, dtype=np.float32).reshape(16, 3)
    mix = (np.float32(0.8) * np.cos(np.float32(1.7) * counter + np.float32(0.3))).astype(np.float32)
    mix = jnp.broadcast_to(jnp.asarray(mix.T)[:, :, None], (3, 16, pixels))
    whole = lambda x: pl.BlockSpec(x.shape, lambda: (0,) * x.ndim)
    smem = pl.BlockSpec(memory_space=pltpu.SMEM)
    shape = jax.ShapeDtypeStruct
    return pl.pallas_call(
        functools.partial(render_kernel, terms),
        in_specs=[smem, smem, whole(zt), whole(zx), whole(rd), whole(mix)],
        out_specs=[whole(zt), whole(zx), pl.BlockSpec((8, 128), lambda: (0, 0))],
        out_shape=[shape(zt.shape, F32), shape(zx.shape, F32), shape((8, 128), F32)],
        scratch_shapes=[
            pltpu.VMEM((2, 4 * TABLE, 256), F32),
            pltpu.VMEM((2, 4 * TABLE, 256), BF16),
            pltpu.VMEM((2, 4 * TABLE, 256), BF16),
            pltpu.VMEM((256, slots), BF16),
            pltpu.VMEM((TABLE, slots), F32),
            pltpu.VMEM((4 * TABLE, slots), BF16),
            pltpu.VMEM((4 * TABLE, slots), BF16),
            pltpu.VMEM((2, 4 * TABLE, 256), F32),
            pltpu.VMEM((4 * NG, tokens), F32),
            pltpu.VMEM((4 * NG, 128), F32),
            pltpu.VMEM((tokens // 128 + 1, POUT, 128), F32),
        ],
        compiler_params=pltpu.CompilerParams(vmem_limit_bytes=48 * VMEM_MB),
        cost_estimate=pl.CostEstimate(
            flops=24 * slots * 4 * TABLE * 256 * 6, bytes_accessed=4 * 1024 * 1024, transcendentals=0
        ),
        name="render",
    )(views, inverse, zt, zx, rd, mix)


def flip_pairs(n, bit):
    return [(i, i ^ bit) for i in range(n)]


def swap(x, axis, bit):
    return lax.ppermute(x, axis, flip_pairs(lax.axis_size(axis), bit))


def total_sum(x):
    for axis in ("scene", "rows"):
        bit = 1
        while bit < lax.axis_size(axis):
            x = x + swap(x, axis, bit)
            bit = 2 * bit
    return x


def gather_plain(shard):
    return lax.all_gather(
        lax.all_gather(shard, "rows", axis=1, tiled=True), "scene", axis=0, tiled=True
    )


def scatter_plain(grad):
    part = lax.psum_scatter(grad, "scene", scatter_dimension=0, tiled=True)
    return lax.psum_scatter(part, "rows", scatter_dimension=1, tiled=True).astype(F32)


def to_items(x):
    scenes, rows = lax.axis_size("scene"), lax.axis_size("rows")
    z = lax.axis_index("rows")
    pairs = [[], []]
    for s in range(scenes):
        for b in range(rows):
            for turn in range(2):
                m = (b % 2) ^ turn
                to = ((s // 2) * 2 + b // 2) * rows + 2 * m + s % 2
                pairs[turn].append((s * rows + b, to))
    even = z % 2 == 0
    first = lax.ppermute(jnp.where(even, x[0], x[1]), ("scene", "rows"), pairs[0])
    second = lax.ppermute(jnp.where(even, x[1], x[0]), ("scene", "rows"), pairs[1])
    early = z // 2 == 0
    return jnp.stack([jnp.where(early, first, second), jnp.where(early, second, first)])


def body(patches, scene_length, target_views, gauss_index, raster_weight, target_color, *state):
    masters, moments, averages = state[:7], state[7:14], state[14:]
    vectors = masters[6]
    scene, row = lax.axis_index("scene"), lax.axis_index("rows")
    side = scene % 2
    item_m, item_s = row // 2, (scene // 2) * 2 + row % 2
    block_rows = patches.shape[2]
    tokens = 2 * block_rows
    length = scene_length[item_m, item_s]
    views = target_views[item_m, item_s].reshape(1)
    lens = jnp.stack([length - side * tokens, length - (1 - side) * tokens])
    pixel_count = jnp.sum(target_views).astype(F32) * (
        raster_weight.shape[-1] * lax.axis_size("rows")
    )
    perm = jnp.concatenate([jnp.arange(8, dtype=jnp.int32)] * 2)

    gains = [vectors[None, i * D : (i + 1) * D] for i in range(9)]
    bias_up = vectors[None, 9 * D : 9 * D + FF]
    bias_gauss = vectors[9 * D + FF :]

    low = [w.astype(BF16) for w in masters[:6]]
    low[0] = low[0].T
    weights = [gather_plain(w) for w in low]
    w_patch, w_joint, w_out, w_up, w_down, w_gauss = weights

    x = to_items(patches[:, 0]).reshape(tokens, -1)
    drawn = jnp.concatenate(
        [gauss_index[:, 0].astype(F32), raster_weight[:, 0], target_color[:, 0]], axis=1
    )
    rd = to_items(jnp.transpose(drawn, (0, 2, 1, 3)))

    h0, a1 = embed(perm, x, w_patch, gains[6], gains[0], gains[3])
    p = nn(a1, w_joint).astype(BF16)
    kv = swap(p[:, D:], "scene", 1)
    mixed, logs = attend(perm, lens, p, kv)
    h1, a2 = project(perm, mixed, w_out, h0, gains[7], gains[1], gains[4])
    u, act = up_project(perm, a2, w_up, bias_up)
    h2, a3 = project(perm, act, w_down, h1, gains[8], gains[2], gains[5])
    zt = lax.dot_general(w_gauss, a3, (((0,), (1,)), ((), ())), preferred_element_type=F32)
    zt = zt + bias_gauss[:, None]

    edge = swap(jnp.where(side == 0, zt[:, tokens - HT :], zt[:, :HT]), "scene", 1)
    before = jnp.where(side == 0, 0.0, edge)
    after = jnp.where(side == 0, edge, 0.0)
    zx = jnp.concatenate([before, after, jnp.zeros((POUT, 128 - 2 * HT), F32)], axis=1)
    dzt, dzx, loss = render(views, (1.0 / pixel_count).reshape(1), zt, zx, rd, 2)
    back = swap(jnp.where(side == 0, dzx[:, HT : 2 * HT], dzx[:, :HT]), "scene", 1)
    dzt = jnp.concatenate(
        [
            dzt[:, :HT] + jnp.where(side == 0, 0.0, back),
            dzt[:, HT : tokens - HT],
            dzt[:, tokens - HT :] + jnp.where(side == 0, back, 0.0),
        ],
        axis=1,
    )
    d_bias_gauss = jnp.sum(dzt, axis=1)
    dz = dzt.astype(BF16).T

    dw_gauss = tn(a3, dz).astype(BF16)
    dh2, dh2_low, sums3 = norm_back(perm, dz, w_gauss, h2, gains[2], None, False)
    dw_down = tn(act, dh2_low).astype(BF16)
    du, d_bias_up = down_back(perm, dh2_low, w_down, u)
    dw_up = tn(a2, du).astype(BF16)
    dh1, dh1_low, sums2 = norm_back(perm, du, w_up, h1, gains[1], dh2, False)
    dw_out = tn(mixed, dh1_low).astype(BF16)
    do = nt(dh1_low, w_out).astype(BF16)
    dq, own, far = attend_back(perm, lens, p, kv, do, logs)
    got = swap(far, "scene", 1)
    dkv = (own + got.astype(F32)).astype(BF16)
    dp = jnp.concatenate([dq, dkv[0], dkv[1]], axis=1)
    dw_joint = tn(a1, dp).astype(BF16)
    dh0_low, sums1 = norm_back(perm, dp, w_joint, h0, gains[0], dh1, True)
    dw_patch = tn(dh0_low, x).astype(BF16)

    reduced = [
        scatter_plain(g) for g in (dw_patch, dw_joint, dw_out, dw_up, dw_down, dw_gauss)
    ]
    reduced[0] = reduced[0].T
    vector_part = jnp.concatenate(
        [sums1[0], sums2[0], sums3[0], sums1[1], sums2[1], sums3[1], sums1[2], sums2[2], sums3[2]]
        + [d_bias_up[0], d_bias_gauss, loss[0]]
    )
    squares = sum(jnp.sum(item * item) for item in reduced)
    totals = total_sum(jnp.concatenate([vector_part, jnp.broadcast_to(squares, (128,))]).reshape(-1, 128))
    totals = totals.reshape(-1)
    vec = vectors.shape[0]
    vector_grad, loss_sum, square_sum = totals[:vec], totals[vec], totals[vec + 128]
    grad_norm = jnp.sqrt(square_sum + jnp.sum(vector_grad * vector_grad))
    factor = jnp.minimum(1.0, CLIP_NORM / (grad_norm + 1e-06))
    next_moments, next_weights, next_averages = ([], [], [])
    for grad, moment, master, average in zip(reduced + [vector_grad], moments, masters, averages):
        clipped = grad * factor
        moment_new = MOMENTUM * moment + clipped
        weight_new = master - STEP_RATE * (clipped + MOMENTUM * moment_new)
        next_moments.append(moment_new)
        next_weights.append(weight_new)
        next_averages.append(AVERAGE_DECAY * average + (1.0 - AVERAGE_DECAY) * weight_new)
    return (loss_sum, pixel_count, grad_norm, *next_moments, *next_weights, *next_averages)


def solution(mesh):
    item = P(None, "scene", None, None, "rows")
    weight_specs = (P("rows", "scene"),) + (P("scene", "rows"),) * 5 + (P(),)
    in_specs = (P(None, "scene", "rows", None), P(), P(), item, item, item) + 3 * weight_specs
    out_specs = (P(), P(), P()) + 3 * weight_specs
    return jax.shard_map(body, mesh=mesh, in_specs=in_specs, out_specs=out_specs, check_vma=False)
```

time: 2390 us -> 984 us (0.41)
  waiting for transfers between devices: 1070 us -> 547 us
  other arithmetic: 383 us -> 32.5 us
  local copies, waits for them, and re-layouts: 415 us -> 74.9 us
  matrix products: 349 us -> 41.8 us
  Pallas kernels: 0 us -> 170 us
  blocking collectives: 106 us -> 71.9 us
    reduce_scatter x16 -> x10, waiting for transfers between devices: 722 us -> 329 us  [the longest x5 219 us: scatter_plain(): part = lax.psum_scatter(grad, 'scene', scatter_dimension=0, tiled=True)]
    dot_general x52 -> x9, matrix products: 349 us -> 41.8 us  [the longest x6 31.5 us: tn(): lax.dot_general(a, b, (((0,), (0,)), ((), ())), preferred_element_type=F32)]
    scatter-add x6 -> x0, other arithmetic: 276 us -> none  [the longest x2 271 us: render_sum(): picked = jnp.take(table, index, axis=1)]
    all_gather x12 -> x8, waiting for transfers between devices: 342 us -> 127 us  [the longest x6 115 us: gather_plain(): lax.all_gather(lax.all_gather(shard, 'rows', axis=1, tiled=True), 'scene'...]
    gather x4 -> x0, local copies, waits for them, and re-layouts: 203 us -> none  [render_sum(): picked = jnp.take(table, index, axis=1)]
    pallas_call x0 -> x11, Pallas kernels: none -> 170 us  [the longest x1 37.6 us: render(): pl.pallas_call(functools.partial(render_kernel, terms), in_specs=[smem, s...]
    slice x28 -> x10, local copies, waits for them, and re-layouts: 77.2 us -> 4.21 us  [the longest x1 1.49 us: body(): kv = swap(p[:, D:], 'scene', 1)]
    unnamed x28 -> x22, waiting for transfers between devices: 2.13 us -> 63.6 us
  transfers between devices with their start and end apart: 36 -> 33, of which waited for: 24 -> 25; matrix products, arithmetic and copies ran while one was open for 24% -> 7% of each run, Pallas kernels for 0% -> 14%
where the time goes in v1:
time: 984 us; the launch traced here: 977 us
  waiting for transfers between devices  547 us (56%)
  Pallas kernels  170 us (17%)
  local copies, waits for them, and re-layouts  74.9 us (8%)
  blocking collectives  71.9 us (7%)
  matrix products  41.8 us (4%)
  other arithmetic  32.5 us (3%)
  between operations  25.3 us (3%)
  starting transfers between devices  13.9 us (1%)
    reduce_scatter x5, waiting for transfers between devices, scatter_plain(): part = lax.psum_scatter(grad, 'scene', scatter_dimension=0, tiled=True)  219 us
    all_gather x6, waiting for transfers between devices, gather_plain(): lax.all_gather(lax.all_gather(shard, 'rows', axis=1, tiled=True), 'scene'...  115 us
    reduce_scatter x5, waiting for transfers between devices, scatter_plain(): lax.psum_scatter(part, 'rows', scatter_dimension=1, tiled=True).astype(F32)  111 us
    all_gather x4, blocking collectives, gather_plain(): lax.all_gather(shard, 'rows', axis=1, tiled=True)  71.9 us
    unnamed x22, waiting for transfers between devices  63.6 us
    unnamed x178, local copies, waits for them, and re-layouts  59.2 us
    pallas_call x1, Pallas kernels, render(): pl.pallas_call(functools.partial(render_kernel, terms), in_specs=[smem, s...  37.6 us
    pallas_call x1, Pallas kernels, attend_back(): pl.pallas_call(attend_back_kernel, grid_spec=pltpu.PrefetchScalarGridSpec...  35.5 us
  transfers between devices with their start and end apart: 33, of which 25 were waited for; matrix products, arithmetic and copies ran while one was open for 7% of the time, Pallas kernels for 14%

profile of v1, /device:TPU:0, one launch (start us, length us, event | category | flops | bytes accessed | tf_op | source)
XLA Modules:
  0.0 977.4 jit_solution(9788758370512061042)
XLA Ops:
  12.0 15.6 %all_gather.36 = bf16[128,576]{0,1:T(8,128)(2,1)S(1)} all-gather(bf16[128,144]{0,1:T(8,128)(2,1)S(1)} %convert_bitcast_fusion), channel_id=1, replica_groups=mesh['scene'=8,'rows'=4] {'rows'}, dimensions={1}, use_global_device_ids=true | all-gather | bytes 184320 | tf_op jit(solution)/shard_map/all_gather | solution.py:701
  28.5 26.7 %all_gather.38 = bf16[128,3072]{1,0:T(8,128)(2,1)} all-gather(bf16[128,768]{1,0:T(8,128)(2,1)S(1)} %convert_element_type.77), channel_id=1, replica_groups=mesh['scene'=8,'rows'=4] {'rows'}, dimensions={1}, use_global_device_ids=true | all-gather | bytes 983040 | tf_op jit(solution)/shard_map/all_gather | solution.py:701
  55.3 15.9 %all_gather.40 = bf16[128,1024]{1,0:T(8,128)(2,1)} all-gather(bf16[128,256]{1,0:T(8,128)(2,1)S(1)} %convert_element_type.80), channel_id=1, replica_groups=mesh['scene'=8,'rows'=4] {'rows'}, dimensions={1}, use_global_device_ids=true | all-gather | bytes 327680 | tf_op jit(solution)/shard_map/all_gather | solution.py:701
  71.8 12.6 %all-gather.19.cloned.1.call-done = bf16[512,1024]{1,0:T(8,128)(2,1)} async-done(((bf16[512,256]{1,0:T(8,128)(2,1)}), bf16[512,1024]{1,0:T(8,128)(2,1)}) %all-gather.19.cloned.1.call-update) | async-done | bytes 1048592 | tf_op jit(solution)/shard_map/all_gather | solution.py:701
  88.3 7.8 collective-permute-done.1
  96.5 13.9 %all-gather.9.cloned.1.call-done.w_ref = bf16[1024,576]{1,0:T(8,128)(2,1)} async-done(((bf16[128,576]{1,0:T(8,128)(2,1)}), bf16[1024,576]{1,0:T(8,128)(2,1)}) %all-gather.9.cloned.1.call-update) | async-done | bytes 1179664 | tf_op jit(solution)/shard_map/all_gather | solution.py:700
  117.9 39.8 %all-gather.11.cloned.1.call-done.refs_1_ = bf16[1024,3072]{1,0:T(8,128)(2,1)} async-done(((bf16[128,3072]{1,0:T(8,128)(2,1)}), bf16[1024,3072]{1,0:T(8,128)(2,1)}) %all-gather.11.cloned.1.call-update) | async-done | bytes 6291472 | tf_op jit(solution)/shard_map/all_gather | solution.py:700
  167.7 13.7 %all_gather.46 = bf16[128,768]{0,1:T(8,128)(2,1)S(1)} all-gather(bf16[128,192]{0,1:T(8,128)(2,1)S(1)} %convert_element_type.83), channel_id=1, replica_groups=mesh['scene'=8,'rows'=4] {'rows'}, dimensions={1}, use_global_device_ids=true | all-gather | bytes 245760 | tf_op jit(solution)/shard_map/all_gather | solution.py:701
  196.8 23.1 %attend.1 = (bf16[512,1024]{1,0:T(8,128)(2,1)S(1)}, f32[8,8,512]{2,1,0:T(8,128)S(1)}) custom-call(s32[16]{0:T(128)S(1)} %pad_add_fusion.perm, s32[2]{0:T(128)S(1)} %pad_add_fusion.1.lens, bf16[512,3072]{1,0:T(8,128)(2,1)S(1)} %copy-done.20, bf16[512,3072]{1,0:T(8,128)(2,1)S(1)} %copy-done.20, bf16[512,2048]{1,0:T(8,128)(2,1)} %collective-permute-done.2.k1_ref.v1_ref, ...), custom_call_target="tpu_custom_call" | custom-call | flops 2147483648 | bytes 6291456 | tf_op jit(solution)/shard_map/attend/pallas_call | solution.py:367
  229.6 13.9 %all-gather.17.cloned.1.call-done.w_ref.refs_1_ = bf16[1024,4096]{1,0:T(8,128)(2,1)} async-done(((bf16[128,4096]{1,0:T(8,128)(2,1)}), bf16[1024,4096]{1,0:T(8,128)(2,1)}) %all-gather.17.cloned.1.call-update) | async-done | bytes 8388624 | tf_op jit(solution)/shard_map/all_gather | solution.py:700
  248.1 9.7 up_gelu.1
  263.2 36.7 %all-gather.21.cloned.1.call-done.w_ref = bf16[4096,1024]{1,0:T(8,128)(2,1)} async-done(((bf16[512,1024]{1,0:T(8,128)(2,1)}), bf16[4096,1024]{1,0:T(8,128)(2,1)}) %all-gather.21.cloned.1.call-update) | async-done | bytes 8388624 | tf_op jit(solution)/shard_map/all_gather | solution.py:700
  303.6 12.8 %project_norm.3 = (f32[512,1024]{1,0:T(8,128)S(1)}, bf16[512,1024]{1,0:T(8,128)(2,1)S(1)}) custom-call(s32[16]{0:T(128)S(1)} %pad_add_fusion.perm, bf16[512,4096]{1,0:T(8,128)(2,1)S(1)} %copy-done.34, bf16[4096,1024]{1,0:T(8,128)(2,1)} %all-gather.21.cloned.1.call-done.w_ref, f32[512,1024]{1,0:T(8,128)S(1)} %copy-done.12, f32[1,1024]{1,0:T(1,128)S(1)} %bitcast.126, ...), custom_call_target="tpu_custom_call" | custom-call | flops 4294967296 | bytes 17825792 | tf_op jit(solution)/shard_map/project_norm/pallas_call | solution.py:121
  317.8 10.4 %all-gather.23.cloned.1.call-done.refs_1_ = bf16[1024,768]{1,0:T(8,128)(2,1)} async-done(((bf16[128,768]{1,0:T(8,128)(2,1)}), bf16[1024,768]{1,0:T(8,128)(2,1)}) %all-gather.23.cloned.1.call-update) | async-done | bytes 1572880 | tf_op jit(solution)/shard_map/all_gather | solution.py:700
  338.6 37.6 %render.1 = (f32[768,512]{1,0:T(8,128)S(1)}, f32[768,128]{1,0:T(8,128)S(1)}, f32[8,128]{1,0:T(8,128)S(1)}) custom-call(s32[1]{0:T(128)} %bitcast.12.views_ref, f32[1]{0:T(128)} %bitcast.13.inv_ref, f32[768,512]{1,0:T(8,128)S(1)} %copy-done.16, f32[768,128]{1,0:T(8,128)S(1)} %maximum_maximum_fusion.zx_ref, f32[2,12,19,256]{3,2,1,0:T(8,128)S(1)} %pad_maximum_fusion.3.rd_ref, ...), custom_call_target="tpu_custom_call" | custom-call | flops 21743271936 | bytes 4194304 | tf_op jit(solution)/shard_map/render/pallas_call | solution.py:656
  406.7 10.8 %down_back_gelu.1 = (bf16[512,4096]{1,0:T(8,128)(2,1)S(1)}, f32[1,4096]{1,0:T(1,128)S(1)}) custom-call(s32[16]{0:T(128)S(1)} %pad_add_fusion.perm, bf16[512,1024]{1,0:T(8,128)(2,1)S(1)} %get-tuple-element.60.d_ref, bf16[4096,1024]{1,0:T(8,128)(2,1)S(1)} %copy-done, f32[512,4096]{1,0:T(8,128)S(1)} %copy-done.2), custom_call_target="tpu_custom_call" | custom-call | flops 4294967296 | bytes 20971520 | tf_op jit(solution)/shard_map/down_back_gelu/pallas_call | solution.py:198
  422.2 12.7 %norm_back.4 = (f32[512,1024]{1,0:T(8,128)S(1)}, bf16[512,1024]{1,0:T(8,128)(2,1)S(1)}, f32[8,1024]{1,0:T(8,128)S(1)}) custom-call(s32[16]{0:T(128)S(1)} %pad_add_fusion.perm, bf16[512,4096]{1,0:T(8,128)(2,1)S(1)} %get-tuple-element.62.refs_0_, bf16[1024,4096]{1,0:T(8,128)(2,1)} %all-gather.17.cloned.1.call-done.w_ref.refs_1_, f32[512,1024]{1,0:T(8,128)S(1)} %copy-done.13, ...), custom_call_target="tpu_custom_call" | custom-call | flops 4294967296 | bytes 19922944 | tf_op jit(solution)/shard_map/norm_back/pallas_call | solution.py:307
  436.3 35.5 %attend_back.1 = (bf16[512,1024]{1,0:T(8,128)(2,1)S(1)}, f32[2,512,1024]{2,1,0:T(8,128)}, bf16[2,512,1024]{2,1,0:T(8,128)(2,1)}) custom-call(s32[16]{0:T(128)S(1)} %pad_add_fusion.perm, s32[2]{0:T(128)S(1)} %pad_add_fusion.1.lens, bf16[512,3072]{1,0:T(8,128)(2,1)} %copy-done.19, bf16[512,3072]{1,0:T(8,128)(2,1)} %copy-done.19, ...), custom_call_target="tpu_custom_call" | custom-call | flops 5368709120 | bytes 14680064 | tf_op jit(solution)/shard_map/attend_back/pallas_call | solution.py:439
  482.5 11.3 %norm_back.5 = (bf16[512,1024]{1,0:T(8,128)(2,1)S(1)}, f32[8,1024]{1,0:T(8,128)S(1)}) custom-call(s32[16]{0:T(128)S(1)} %pad_add_fusion.perm, bf16[512,3072]{1,0:T(8,128)(2,1)S(1)} %pad_maximum_fusion.refs_0_, bf16[1024,3072]{1,0:T(8,128)(2,1)} %all-gather.11.cloned.1.call-done.refs_1_, f32[512,1024]{1,0:T(8,128)S(1)} %get-tuple-element.52.r_ref.refs_2_, ...), custom_call_target="tpu_custom_call" | custom-call | flops 3221225472 | bytes 16777216 | tf_op jit(solution)/shard_map/norm_back/pallas_call | solution.py:307
  498.2 6.7 convolution_convert_fusion.2
  506.1 9.0 convolution_convert_fusion.1
  516.3 9.1 convolution_convert_fusion
  533.4 40.9 %reduce-scatter.37.cloned.1.call-done = bf16[128,576]{1,0:T(8,128)(2,1)} async-done(((bf16[1024,576]{1,0:T(8,128)(2,1)}), bf16[128,576]{1,0:T(8,128)(2,1)}) %reduce-scatter.37.cloned.1.call-update) | async-done | bytes 147472
  576.0 63.6 %reduce-scatter.19.cloned.1.call-done = bf16[128,3072]{1,0:T(8,128)(2,1)} async-done(((bf16[1024,3072]{1,0:T(8,128)(2,1)}), bf16[128,3072]{1,0:T(8,128)(2,1)}) %reduce-scatter.19.cloned.1.call-update) | async-done | bytes 786448 | tf_op jit(solution)/shard_map/reduce_scatter | solution.py:706
  639.7 74.7 %reduce-scatter.27.cloned.1.call-done = bf16[128,4096]{1,0:T(8,128)(2,1)} async-done(((bf16[1024,4096]{1,0:T(8,128)(2,1)}), bf16[128,4096]{1,0:T(8,128)(2,1)}) %reduce-scatter.27.cloned.1.call-update) | async-done | bytes 1048592 | tf_op jit(solution)/shard_map/reduce_scatter | solution.py:706
  714.9 74.5 %reduce-scatter.31.cloned.1.call-done = bf16[512,1024]{1,0:T(8,128)(2,1)} async-done(((bf16[4096,1024]{1,0:T(8,128)(2,1)}), bf16[512,1024]{1,0:T(8,128)(2,1)}) %reduce-scatter.31.cloned.1.call-update) | async-done | bytes 1048592 | tf_op jit(solution)/shard_map/reduce_scatter | solution.py:706
  789.6 21.9 %reduce-scatter.39.cloned.1.call-done = bf16[192,128]{1,0:T(8,128)(2,1)} async-done(((bf16[768,128]{1,0:T(8,128)(2,1)}), bf16[192,128]{1,0:T(8,128)(2,1)}) %reduce-scatter.39.cloned.1.call-update) | async-done | bytes 49168
  813.0 18.6 %reduce-scatter.25.cloned.1.call-done = bf16[128,256]{1,0:T(8,128)(2,1)} async-done(((bf16[128,1024]{1,0:T(8,128)(2,1)}), bf16[128,256]{1,0:T(8,128)(2,1)}) %reduce-scatter.25.cloned.1.call-update) | async-done | bytes 65552 | tf_op jit(solution)/shard_map/reduce_scatter | solution.py:707
  833.1 18.7 %reduce-scatter.17.cloned.1.call-done = bf16[128,144]{0,1:T(8,128)(2,1)} async-done(((bf16[128,576]{0,1:T(8,128)(2,1)}), bf16[128,144]{0,1:T(8,128)(2,1)}) %reduce-scatter.17.cloned.1.call-update) | async-done | bytes 36880 | tf_op jit(solution)/shard_map/reduce_scatter | solution.py:707
  853.2 22.4 %reduce-scatter.21.cloned.1.call-done = bf16[128,768]{1,0:T(8,128)(2,1)} async-done(((bf16[128,3072]{1,0:T(8,128)(2,1)}), bf16[128,768]{1,0:T(8,128)(2,1)}) %reduce-scatter.21.cloned.1.call-update) | async-done | bytes 196624 | tf_op jit(solution)/shard_map/reduce_scatter | solution.py:707
  879.2 25.3 %reduce-scatter.29.cloned.1.call-done = bf16[128,1024]{1,0:T(8,128)(2,1)} async-done(((bf16[128,4096]{1,0:T(8,128)(2,1)}), bf16[128,1024]{1,0:T(8,128)(2,1)}) %reduce-scatter.29.cloned.1.call-update) | async-done | bytes 262160 | tf_op jit(solution)/shard_map/reduce_scatter | solution.py:707
  906.8 25.6 %reduce-scatter.33.cloned.1.call-done = bf16[512,256]{1,0:T(8,128)(2,1)} async-done(((bf16[512,1024]{1,0:T(8,128)(2,1)}), bf16[512,256]{1,0:T(8,128)(2,1)}) %reduce-scatter.33.cloned.1.call-update) | async-done | bytes 262160 | tf_op jit(solution)/shard_map/reduce_scatter | solution.py:707
  (328 shorter events, 181.0 us)
Async XLA Ops:
  7.2 64.1 %all-gather.15.cloned.1.call-start = ((), (), s32[]{:S(2)}) async-start(), calls=%async_computation.15 | async-start | bytes 1310720 | tf_op jit(solution)/shard_map/all_gather | solution.py:701
  9.1 75.3 %all-gather.19.cloned.1.call-start = ((), (), s32[]{:S(2)}) async-start(), calls=%async_computation.17 | async-start | bytes 1310720 | tf_op jit(solution)/shard_map/all_gather | solution.py:701
  11.0 99.4 %all-gather.9.cloned.1.call-start = ((), (), s32[]{:S(2)}) async-start(), calls=%async_computation.12 | async-start | bytes 1474560 | tf_op jit(solution)/shard_map/all_gather | solution.py:700
  28.4 129.3 %all-gather.11.cloned.1.call-start = ((), (), s32[]{:S(2)}) async-start(), calls=%async_computation.13 | async-start | bytes 7077888 | tf_op jit(solution)/shard_map/all_gather | solution.py:700
  55.2 164.8 %all-gather.13.cloned.1.call-start = ((), (), s32[]{:S(2)}) async-start(), calls=%async_computation.14 | async-start | bytes 2359296 | tf_op jit(solution)/shard_map/all_gather | solution.py:700
  71.2 172.3 %all-gather.17.cloned.1.call-start = ((), (), s32[]{:S(2)}) async-start(), calls=%async_computation.16 | async-start | bytes 9437184 | tf_op jit(solution)/shard_map/all_gather | solution.py:700
  71.8 228.1 %all-gather.21.cloned.1.call-start = ((), (), s32[]{:S(2)}) async-start(), calls=%async_computation.18 | async-start | bytes 9437184 | tf_op jit(solution)/shard_map/all_gather | solution.py:700
  84.4 243.7 %all-gather.23.cloned.1.call-start = ((), (), s32[]{:S(2)}) async-start(), calls=%async_computation.19 | async-start | bytes 1769472 | tf_op jit(solution)/shard_map/all_gather | solution.py:700
  84.6 3.7 collective-permute-start
  85.2 10.9 %collective-permute-start.1 = (bf16[256,576]{0,1:T(8,128)(2,1)S(1)}, bf16[256,576]{0,1:T(8,128)(2,1)S(1)}, u32[]{:S(2)}, u32[]{:S(2)}) collective-permute-start(bf16[256,576]{0,1:T(8,128)(2,1)S(1)} %get-tuple-element.181), channel_id=1, source_target_pairs={{0,2},{1,0},{2,6},{3,4},{4,3},{5,1},{6,7},{7,5},{8,10},{9,8},{10,1... | collective-permute-start | bytes 884744 | tf_op jit(solution)/shard_map/ppermute | solution.py:722
  167.5 27.1 %collective-permute-start.2 = (bf16[512,2048]{1,0:T(8,128)(2,1)}, bf16[512,2048]{1,0:T(8,128)(2,1)}, u32[]{:S(2)}, u32[]{:S(2)}) collective-permute-start(bf16[512,2048]{1,0:T(8,128)(2,1)} %slice.159), channel_id=1, source_target_pairs={{0,4},{4,0},{8,12},{12,8},{16,20},{20,16},{24,28},{28,24},{1,5},{5... | collective-permute-start | bytes 6291464 | tf_op jit(solution)/shard_map/ppermute | solution.py:687
  182.3 343.2 %reduce-scatter.35.cloned.1.call-start = ((), (), s32[]{:S(2)}) async-start(), calls=%async_computation.29 | async-start | bytes 1769472 | tf_op jit(solution)/shard_map/reduce_scatter | solution.py:706
  182.5 7.5 collective-permute-start.4
  183.2 10.5 %collective-permute-start.5 = (f32[12,19,256]{2,1,0:T(8,128)S(1)}, f32[12,19,256]{2,1,0:T(8,128)S(1)}, u32[]{:S(2)}, u32[]{:S(2)}) collective-permute-start(f32[12,19,256]{2,1,0:T(8,128)S(1)} %get-tuple-element.177), channel_id=1, source_target_pairs={{0,2},{1,0},{2,6},{3,4},{4,3},{5,1},{6,7},{7,5},{8,10},{9,8},{10,1... | collective-permute-start | bytes 700424 | tf_op jit(solution)/shard_map/ppermute | solution.py:722
  330.6 4.2 collective-permute-start.3
  379.2 4.8 collective-permute-start.6
  388.5 144.8 %reduce-scatter.23.cloned.1.call-start = ((), (), s32[]{:S(2)}) async-start(), calls=%async_computation.23 | async-start | bytes 2359296 | tf_op jit(solution)/shard_map/reduce_scatter | solution.py:706
  471.8 4.5 collective-permute-start.7
  474.7 99.5 %reduce-scatter.37.cloned.1.call-start = ((), (), s32[]{:S(2)}) async-start(), calls=%async_computation.30 | async-start | bytes 1474560
  498.1 141.6 %reduce-scatter.19.cloned.1.call-start = ((), (), s32[]{:S(2)}) async-start(), calls=%async_computation.21 | async-start | bytes 7077888 | tf_op jit(solution)/shard_map/reduce_scatter | solution.py:706
  504.9 209.5 %reduce-scatter.27.cloned.1.call-start = ((), (), s32[]{:S(2)}) async-start(), calls=%async_computation.25 | async-start | bytes 9437184 | tf_op jit(solution)/shard_map/reduce_scatter | solution.py:706
  515.1 274.3 %reduce-scatter.31.cloned.1.call-start = ((), (), s32[]{:S(2)}) async-start(), calls=%async_computation.27 | async-start | bytes 9437184 | tf_op jit(solution)/shard_map/reduce_scatter | solution.py:706
  525.4 286.0 %reduce-scatter.39.cloned.1.call-start = ((), (), s32[]{:S(2)}) async-start(), calls=%async_computation.31 | async-start | bytes 245760
  527.4 304.2 %reduce-scatter.25.cloned.1.call-start = ((), (), s32[]{:S(2)}) async-start(), calls=%async_computation.24 | async-start | bytes 327680 | tf_op jit(solution)/shard_map/reduce_scatter | solution.py:707
  533.3 318.4 %reduce-scatter.17.cloned.1.call-start = ((), (), s32[]{:S(2)}) async-start(), calls=%async_computation.20 | async-start | bytes 184320 | tf_op jit(solution)/shard_map/reduce_scatter | solution.py:707
  576.0 299.6 %reduce-scatter.21.cloned.1.call-start = ((), (), s32[]{:S(2)}) async-start(), calls=%async_computation.22 | async-start | bytes 983040 | tf_op jit(solution)/shard_map/reduce_scatter | solution.py:707
  639.7 264.7 %reduce-scatter.29.cloned.1.call-start = ((), (), s32[]{:S(2)}) async-start(), calls=%async_computation.26 | async-start | bytes 1310720 | tf_op jit(solution)/shard_map/reduce_scatter | solution.py:707
  714.5 217.9 %reduce-scatter.33.cloned.1.call-start = ((), (), s32[]{:S(2)}) async-start(), calls=%async_computation.28 | async-start | bytes 1310720 | tf_op jit(solution)/shard_map/reduce_scatter | solution.py:707
  936.8 4.2 collective-permute-start.9
  941.1 4.2 collective-permute-start.10
  945.3 4.2 collective-permute-start.11
  949.6 5.2 collective-permute-start.12
  (80 other events, 3090.3 us)
Sparse Core Ops, SparseCore 0:
  10.2 41.8 all-gather.14
  54.2 30.1 all-gather.18
  86.9 23.4 all-gather.8
  112.1 45.5 all-gather.10
  159.4 27.8 all-gather.12
  189.1 54.3 all-gather.16
  245.4 54.3 all-gather.20
  302.3 25.7 all-gather.22
  388.6 55.5 reduce-scatter.34
  474.9 58.4 reduce-scatter.22
  536.9 37.2 reduce-scatter.36
  577.9 61.7 reduce-scatter.18
  643.1 71.2 reduce-scatter.26
  718.1 71.2 reduce-scatter.30
  792.1 19.3 reduce-scatter.38
  813.7 17.8 reduce-scatter.24
  834.3 17.4 reduce-scatter.16
  854.0 21.5 reduce-scatter.20
  878.0 26.3 reduce-scatter.28
  906.6 25.7 reduce-scatter.32

commit v2 on v1

--- a/solution.py
+++ b/solution.py
@@ -29,6 +29,7 @@
 BLOCKS = 8
 WIDE = D // BLOCKS
 VMEM_MB = 1024 * 1024
+VMEM = 28
 TABLE = NG + 8
 
 
@@ -52,6 +53,16 @@
 
 def lane_block(index, width):
     return pl.ds(pl.multiple_of(index * width, width), width)
+
+
+PATCH = 144
+GAUSS = POUT // 4
+
+
+def side_rows(w_ref, place, first, count):
+    return jnp.concatenate(
+        [w_ref[j, place, first : first + count, :] for j in range(4)], axis=1
+    )
 
 
 def norm_store(perm, h_ref, g_ref, s_ref, a_ref, chunk):
@@ -68,95 +79,298 @@
     lax.fori_loop(0, h_ref.shape[0] // chunk, step, 0)
 
 
-def embed_kernel(perm, x_ref, w_ref, b_ref, g_ref, s_ref, h_ref, a_ref):
-    hr = nt(x_ref[...], w_ref[...])
-    for j in range(BLOCKS):
-        cols = lane_block(perm[j], WIDE)
-        h_ref[:, cols] = hr[:, j * WIDE : (j + 1) * WIDE] + b_ref[:, cols]
+def rows_of(w_ref, z, width):
+    block = w_ref[:, z]
+    if block.shape[-1] != width:
+        block = block[:, :, :width]
+    return block.reshape(block.shape[0] * block.shape[1], width)
+
+
+def embed_kernel(perm, x_ref, w0_ref, w1_ref, b_ref, g_ref, s_ref, h_ref, a_ref):
+    x = x_ref[...]
+    for i, w_ref in enumerate((w0_ref, w1_ref)):
+        weight = jnp.concatenate(
+            [side_rows(w_ref, perm[16 + z], 0, PATCH) for z in range(4)], axis=0
+        )
+        hr = nn(x, weight)
+        for j in range(BLOCKS // 2):
+            cols = lane_block(perm[i * BLOCKS // 2 + j], WIDE)
+            h_ref[:, cols] = hr[:, j * WIDE : (j + 1) * WIDE] + b_ref[:, cols]
     norm_store(perm, h_ref, g_ref, s_ref, a_ref, 32)
 
 
-def embed(perm, x, w, b, g, s):
-    rows, pin = x.shape
+def embed(perm, x, chunk, b, g, s):
+    rows = x.shape[0]
     part = 256
     full = lambda shape: pl.BlockSpec(shape, lambda i, p: (0, 0))
     tile = lambda n: pl.BlockSpec((part, n), lambda i, p: (i, 0))
+    weight = pl.BlockSpec((4, 4, PATCH + GAUSS, WIDE), lambda i, p: (0, 0, 0, 0))
     return pl.pallas_call(
         embed_kernel,
         grid_spec=pltpu.PrefetchScalarGridSpec(
             num_scalar_prefetch=1,
             grid=(rows // part,),
-            in_specs=[tile(pin), full((D, pin)), full((1, D)), full((1, D)), full((1, D))],
+            in_specs=[tile(x.shape[1]), weight, weight]
+            + [full((1, D))] * 3,
             out_specs=[tile(D), tile(D)],
         ),
         out_shape=[jax.ShapeDtypeStruct((rows, D), F32), jax.ShapeDtypeStruct((rows, D), BF16)],
-        compiler_params=params(32),
+        compiler_params=params(VMEM),
         cost_estimate=pl.CostEstimate(
-            flops=2 * rows * D * pin, bytes_accessed=rows * D * 6 + 4 * D * pin, transcendentals=0
+            flops=2 * rows * D * 576, bytes_accessed=rows * D * 6 + 4 * D * 576, transcendentals=0
         ),
         name="embed_norm",
-    )(perm, x, w, b, g, s)
-
-
-def project_kernel(perm, a_ref, w_ref, r_ref, b_ref, g_ref, s_ref, h_ref, n_ref):
-    k = pl.program_id(0)
-
-    @pl.when(k == 0)
-    def _():
-        h_ref[...] = r_ref[...] + b_ref[...] + nn(a_ref[...], w_ref[...])
-
-    @pl.when(k > 0)
-    def _():
-        h_ref[...] = h_ref[...] + nn(a_ref[...], w_ref[...])
-
-    @pl.when(k == pl.num_programs(0) - 1)
+    )(perm, x, *chunk, b, g, s)
+
+
+def first_of(chunk):
+    return (0, 0) if chunk[0].shape[0] == 4 else (0, 1)
+
+
+def project_kernel(perm, a_ref, w0_ref, w1_ref, r_ref, b_ref, g_ref, s_ref, h_ref, n_ref):
+    z = pl.program_id(0)
+    middle = a_ref.shape[1] // 2
+    width = D // 4
+    cols = lane_block(z, width)
+    h_ref[:, cols] = (
+        r_ref[...]
+        + b_ref[...]
+        + nn(a_ref[:, :middle], rows_of(w0_ref, 0, width))
+        + nn(a_ref[:, middle:], rows_of(w1_ref, 0, width))
+    )
+
+    @pl.when(z == pl.num_programs(0) - 1)
     def _():
         norm_store(perm, h_ref, g_ref, s_ref, n_ref, 32)
 
 
-def project(perm, a, w, res, b, g, s):
+def project(perm, a, chunk, at, res, b, g, s):
     rows, depth = a.shape
-    part = 512
-    full = lambda shape: pl.BlockSpec(shape, lambda k, p: (0, 0))
+    width = D // 4
+    full = lambda shape: pl.BlockSpec(shape, lambda z, p: (0, 0))
+    weights = [
+        pl.BlockSpec((4, 1, depth // 8, width), lambda z, p, i=i: (i, p[16 + z], 0, at))
+        for i in first_of(chunk)
+    ]
     return pl.pallas_call(
         project_kernel,
         grid_spec=pltpu.PrefetchScalarGridSpec(
             num_scalar_prefetch=1,
-            grid=(depth // part,),
+            grid=(4,),
             in_specs=[
-                pl.BlockSpec((rows, part), lambda k, p: (0, k)),
-                pl.BlockSpec((part, D), lambda k, p: (k, 0)),
-                full((rows, D)),
-                full((1, D)),
+                full((rows, depth)),
+                *weights,
+                pl.BlockSpec((rows, width), lambda z, p: (0, z)),
+                pl.BlockSpec((1, width), lambda z, p: (0, z)),
                 full((1, D)),
                 full((1, D)),
             ],
             out_specs=[full((rows, D)), full((rows, D))],
         ),
         out_shape=[jax.ShapeDtypeStruct((rows, D), F32), jax.ShapeDtypeStruct((rows, D), BF16)],
-        compiler_params=params(40),
+        compiler_params=params(VMEM),
         cost_estimate=pl.CostEstimate(
             flops=2 * rows * D * depth,
             bytes_accessed=rows * D * 10 + 2 * D * depth + 2 * rows * depth,
             transcendentals=0,
         ),
         name="project_norm",
-    )(perm, a, w, res, b, g, s)
+    )(perm, a, *chunk, res, b, g, s)
+
+
+def halves(a_ref, w0_ref, w1_ref, width):
+    middle = a_ref.shape[1] // 2
+    return nn(a_ref[:, :middle], rows_of(w0_ref, 0, width)) + nn(
+        a_ref[:, middle:], rows_of(w1_ref, 0, width)
+    )
+
+
+def joint_kernel(perm, a_ref, w0_ref, w1_ref, p_ref):
+    p_ref[...] = halves(a_ref, w0_ref, w1_ref, p_ref.shape[1]).astype(BF16)
+
+
+def joint(perm, a, chunk):
+    rows = a.shape[0]
+    part = 3 * D // 4
+    weight = pl.BlockSpec((4, 1, WIDE, part), lambda z, p: (0, p[16 + z], 0, 0))
+    return pl.pallas_call(
+        joint_kernel,
+        grid_spec=pltpu.PrefetchScalarGridSpec(
+            num_scalar_prefetch=1,
+            grid=(4,),
+            in_specs=[pl.BlockSpec((rows, D), lambda z, p: (0, 0)), weight, weight],
+            out_specs=pl.BlockSpec((rows, part), lambda z, p: (0, z)),
+        ),
+        out_shape=jax.ShapeDtypeStruct((rows, 3 * D), BF16),
+        compiler_params=params(VMEM),
+        cost_estimate=pl.CostEstimate(
+            flops=6 * rows * D * D, bytes_accessed=rows * D * 8 + 6 * D * D, transcendentals=0
+        ),
+        name="joint",
+    )(perm, a, *chunk)
+
+
+def gauss_kernel(perm, a_ref, w0_ref, w1_ref, b_ref, z_ref):
+    half = D // 2
+    z_ref[...] = (
+        nt(side_rows(w0_ref, 0, PATCH, GAUSS), a_ref[:, :half])
+        + nt(side_rows(w1_ref, 0, PATCH, GAUSS), a_ref[:, half:])
+        + b_ref[...]
+    )
+
+
+def gauss(perm, a, chunk, b):
+    rows = a.shape[0]
+    weight = pl.BlockSpec((4, 1, PATCH + GAUSS, WIDE), lambda z, p: (0, p[16 + z], 0, 0))
+    return pl.pallas_call(
+        gauss_kernel,
+        grid_spec=pltpu.PrefetchScalarGridSpec(
+            num_scalar_prefetch=1,
+            grid=(4,),
+            in_specs=[
+                pl.BlockSpec((rows, D), lambda z, p: (0, 0)),
+                weight,
+                weight,
+                pl.BlockSpec((GAUSS, 1), lambda z, p: (z, 0)),
+            ],
+            out_specs=pl.BlockSpec((GAUSS, rows), lambda z, p: (z, 0)),
+        ),
+        out_shape=jax.ShapeDtypeStruct((POUT, rows), F32),
+        compiler_params=params(VMEM),
+        cost_estimate=pl.CostEstimate(
+            flops=2 * rows * D * POUT, bytes_accessed=rows * D * 5 + 2 * D * POUT, transcendentals=0
+        ),
+        name="gauss",
+    )(perm, a, *chunk, b[:, None])
+
+
+def out_back_kernel(perm, d_ref, w0_ref, w1_ref, o_ref):
+    width = D // 4
+    for i, w_ref in enumerate((w0_ref, w1_ref)):
+        total = sum(
+            nt(d_ref[:, z * width : (z + 1) * width], rows_of(w_ref, perm[16 + z], width))
+            for z in range(4)
+        )
+        o_ref[:, i * D // 2 : (i + 1) * D // 2] = total.astype(BF16)
+
+
+def out_back(perm, d, chunk):
+    rows = d.shape[0]
+    part = 256
+    weight = pl.BlockSpec((4, 4, WIDE, D // 4), lambda i, p: (0, 0, 0, 4))
+    tile = pl.BlockSpec((part, D), lambda i, p: (i, 0))
+    return pl.pallas_call(
+        out_back_kernel,
+        grid_spec=pltpu.PrefetchScalarGridSpec(
+            num_scalar_prefetch=1,
+            grid=(rows // part,),
+            in_specs=[tile, weight, weight],
+            out_specs=tile,
+        ),
+        out_shape=jax.ShapeDtypeStruct((rows, D), BF16),
+        compiler_params=params(VMEM),
+        cost_estimate=pl.CostEstimate(
+            flops=2 * rows * D * D, bytes_accessed=rows * D * 4 + 2 * D * D, transcendentals=0
+        ),
+        name="out_back",
+    )(perm, d, *chunk)
+
+
+def grad_kernel(perm, a_ref, d_ref, *refs):
+    *outs, turned_ref = refs
+    middle = a_ref.shape[1] // 2
+
+    @pl.when(pl.program_id(0) == 0)
+    def _():
+        turned_ref[...] = a_ref[...].T
+
+    for i in (1, 0):
+        g = nn(turned_ref[i * middle : (i + 1) * middle, :], d_ref[...]).astype(BF16)
+        g = g.reshape(4, 1, middle // 4, g.shape[1])
+        if len(outs) == 2:
+            outs[i][...] = g
+        else:
+            for j in range(4):
+                outs[0][perm[4 * i + j]] = g[j]
+
+
+def weight_grad(perm, a, d, whole=False):
+    tokens, depth = a.shape
+    n = d.shape[1] // 4
+    right = pl.BlockSpec((tokens, n), lambda z, p: (0, z))
+    count = 8 if whole else 4
+    out = pl.BlockSpec((count, 1, depth // 8, n), lambda z, p: (0, p[16 + z], 0, 0))
+    shape = jax.ShapeDtypeStruct((count, 4, depth // 8, n), BF16)
+    return pl.pallas_call(
+        grad_kernel,
+        grid_spec=pltpu.PrefetchScalarGridSpec(
+            num_scalar_prefetch=1,
+            grid=(4,),
+            in_specs=[pl.BlockSpec((tokens, depth), lambda z, p: (0, 0)), right],
+            out_specs=[out] * (8 // count),
+            scratch_shapes=[pltpu.VMEM((depth, tokens), BF16)],
+        ),
+        out_shape=[shape] * (8 // count),
+        compiler_params=params(VMEM),
+        cost_estimate=pl.CostEstimate(
+            flops=8 * tokens * depth * n,
+            bytes_accessed=2 * tokens * (depth + 4 * n) + 8 * depth * n,
+            transcendentals=0,
+        ),
+        name="weight_grad",
+    )(perm, a, d)
+
+
+def side_grad_kernel(perm, d_ref, a_ref, *outs):
+    g = nn(d_ref[...], a_ref[...]).astype(BF16)
+    for j in range(BLOCKS):
+        block = g[:, j * WIDE : (j + 1) * WIDE]
+        if len(outs) == 2:
+            outs[j // 4][j % 4, 0] = block
+        else:
+            outs[0][perm[j], 0] = block
+
+
+def side_grad(perm, d, a, whole=False):
+    tokens = a.shape[0]
+    n = d.shape[0] // 4
+    count = 8 if whole else 4
+    out = pl.BlockSpec((count, 1, n, WIDE), lambda z, p: (0, p[16 + z], 0, 0))
+    shape = jax.ShapeDtypeStruct((count, 4, n, WIDE), BF16)
+    return pl.pallas_call(
+        side_grad_kernel,
+        grid_spec=pltpu.PrefetchScalarGridSpec(
+            num_scalar_prefetch=1,
+            grid=(4,),
+            in_specs=[
+                pl.BlockSpec((n, tokens), lambda z, p: (z, 0)),
+                pl.BlockSpec((tokens, D), lambda z, p: (0, 0)),
+            ],
+            out_specs=[out] * (8 // count),
+        ),
+        out_shape=[shape] * (8 // count),
+        compiler_params=params(VMEM),
+        cost_estimate=pl.CostEstimate(
+            flops=8 * tokens * D * n, bytes_accessed=2 * tokens * D + 16 * D * n, transcendentals=0
+        ),
+        name="side_grad",
+    )(perm, d, a)
 
 
 GELU_C = float(np.sqrt(2.0 / np.pi))
 
 
-def up_kernel(perm, a_ref, w_ref, b_ref, u_ref, g_ref):
-    u = nn(a_ref[...], w_ref[...]) + b_ref[...]
+def up_kernel(perm, a_ref, w0_ref, w1_ref, b_ref, u_ref, g_ref):
+    u = halves(a_ref, w0_ref, w1_ref, u_ref.shape[1]) + b_ref[...]
     u_ref[...] = u
     t = jnp.tanh(GELU_C * (u + 0.044715 * (u * u * u)))
     g_ref[...] = (u * (0.5 * (1.0 + t))).astype(BF16)
 
 
-def up_project(perm, a, w, b):
+def up_project(perm, a, chunk, b):
     rows = a.shape[0]
     part = FF // BLOCKS
+    weight = pl.BlockSpec((4, 1, WIDE, part), lambda n, p: (0, p[16 + n // 2], 0, n % 2))
     return pl.pallas_call(
         up_kernel,
         grid_spec=pltpu.PrefetchScalarGridSpec(
@@ -164,7 +378,8 @@
             grid=(BLOCKS,),
             in_specs=[
                 pl.BlockSpec((rows, D), lambda n, p: (0, 0)),
-                pl.BlockSpec((D, part), lambda n, p: (0, n)),
+                weight,
+                weight,
                 pl.BlockSpec((1, part), lambda n, p: (0, n)),
             ],
             out_specs=[
@@ -173,16 +388,27 @@
             ],
         ),
         out_shape=[jax.ShapeDtypeStruct((rows, FF), F32), jax.ShapeDtypeStruct((rows, FF), BF16)],
-        compiler_params=params(32),
+        compiler_params=params(VMEM),
         cost_estimate=pl.CostEstimate(
             flops=2 * rows * D * FF, bytes_accessed=rows * FF * 6 + 2 * D * FF, transcendentals=rows * FF
         ),
         name="up_gelu",
-    )(perm, a, w, b)
-
-
-def down_back_kernel(perm, d_ref, w_ref, u_ref, du_ref, sum_ref):
-    dg = nt(d_ref[...], w_ref[...])
+    )(perm, a, *chunk, b)
+
+
+def down_back_kernel(perm, d_ref, w0_ref, w1_ref, u_ref, du_ref, sum_ref, dg_ref):
+    width = D // 4
+
+    def product(w_ref):
+        dg_ref[...] = sum(
+            nt(d_ref[:, z * width : (z + 1) * width], rows_of(w_ref, perm[16 + z], width))
+            for z in range(4)
+        )
+
+    first = pl.program_id(0) < pl.num_programs(0) // 2
+    pl.when(first)(lambda: product(w0_ref))
+    pl.when(jnp.logical_not(first))(lambda: product(w1_ref))
+    dg = dg_ref[...]
     u = u_ref[...]
     u2 = u * u
     t = jnp.tanh(GELU_C * (u + 0.044715 * (u2 * u)))
@@ -192,8 +418,9 @@
     sum_ref[...] = jnp.sum(du, axis=0, keepdims=True)
 
 
-def down_back(perm, d, w, u):
+def down_back(perm, d, chunk, u):
     rows = d.shape[0]
+    second = 4 * first_of(chunk)[1]
     part = FF // BLOCKS
     return pl.pallas_call(
         down_back_kernel,
@@ -202,28 +429,32 @@
             grid=(BLOCKS,),
             in_specs=[
                 pl.BlockSpec((rows, D), lambda j, p: (0, 0)),
-                pl.BlockSpec((part, D), lambda j, p: (j, 0)),
+                pl.BlockSpec((1, 4, part, D // 4), lambda j, p: (jnp.minimum(j, 3), 0, 0, 0)),
+                pl.BlockSpec(
+                    (1, 4, part, D // 4), lambda j, p: (jnp.maximum(j - 4, 0) + second, 0, 0, 0)
+                ),
                 pl.BlockSpec((rows, part), lambda j, p: (0, p[j])),
             ],
             out_specs=[
                 pl.BlockSpec((rows, part), lambda j, p: (0, p[j])),
                 pl.BlockSpec((1, part), lambda j, p: (0, p[j])),
             ],
+            scratch_shapes=[pltpu.VMEM((rows, part), F32)],
         ),
         out_shape=[jax.ShapeDtypeStruct((rows, FF), BF16), jax.ShapeDtypeStruct((1, FF), F32)],
-        compiler_params=params(32),
+        compiler_params=params(VMEM),
         cost_estimate=pl.CostEstimate(
             flops=2 * rows * D * FF, bytes_accessed=rows * FF * 6 + 2 * D * FF, transcendentals=rows * FF
         ),
         name="down_back_gelu",
-    )(perm, d, w, u)
-
-
-def back_kernel(has_res, placed, perm, *refs):
+    )(perm, d, *chunk, u)
+
+
+def back_kernel(has_res, placed, turned, perm, *refs):
     if has_res:
-        d_ref, w_ref, h_ref, g_ref, r_ref, *outs = refs
+        d_ref, w0_ref, w1_ref, h_ref, g_ref, r_ref, *outs = refs
     else:
-        d_ref, w_ref, h_ref, g_ref, *outs = refs
+        d_ref, w0_ref, w1_ref, h_ref, g_ref, *outs = refs
         r_ref = None
     if placed:
         low_ref, sums_ref, acc_ref, part_ref = outs
@@ -232,13 +463,26 @@
         dh_ref, low_ref, sums_ref, acc_ref, part_ref = outs
     n = pl.program_id(0)
 
-    @pl.when(n == 0)
-    def _():
-        acc_ref[...] = nt(d_ref[...], w_ref[...])
-
-    @pl.when(n > 0)
-    def _():
-        acc_ref[...] = acc_ref[...] + nt(d_ref[...], w_ref[...])
+    if turned:
+        d = d_ref[...].T
+        for i, w_ref in enumerate((w0_ref, w1_ref)):
+            weight = jnp.concatenate(
+                [side_rows(w_ref, perm[16 + z], PATCH, GAUSS) for z in range(4)], axis=0
+            )
+            acc_ref[:, i * D // 2 : (i + 1) * D // 2] = nn(d, weight)
+    else:
+        d = d_ref[...]
+        width = d.shape[1]
+
+        @pl.when(n == 0)
+        def _():
+            acc_ref[:, : D // 2] = nt(d, rows_of(w0_ref, 0, width))
+            acc_ref[:, D // 2 :] = nt(d, rows_of(w1_ref, 0, width))
+
+        @pl.when(n > 0)
+        def _():
+            acc_ref[:, : D // 2] += nt(d, rows_of(w0_ref, 0, width))
+            acc_ref[:, D // 2 :] += nt(d, rows_of(w1_ref, 0, width))
 
     @pl.when(n == pl.num_programs(0) - 1)
     def _():
@@ -285,17 +529,19 @@
         )
 
 
-def norm_back(perm, d, w, h, g, res, placed):
-    rows, wide = d.shape
-    part = 768 if wide % 1024 else 1024
+def norm_back(perm, d, chunk, turned, h, g, res, placed):
     full = lambda shape: pl.BlockSpec(shape, lambda n, p: (0, 0))
-    args = [d, w, h, g]
-    specs = [
-        pl.BlockSpec((rows, part), lambda n, p: (0, n)),
-        pl.BlockSpec((D, part), lambda n, p: (0, n)),
-        full((rows, D)),
-        full((1, D)),
-    ]
+    rows = h.shape[0]
+    wide = d.size // rows
+    if turned:
+        left = full(d.shape)
+        weight = pl.BlockSpec((4, 4, PATCH + GAUSS, WIDE), lambda n, p: (0, 0, 0, 0))
+    else:
+        part = wide // 4
+        left = pl.BlockSpec((rows, part), lambda n, p: (0, n))
+        weight = pl.BlockSpec((4, 1, WIDE, part), lambda n, p: (0, p[16 + n], 0, 0))
+    args = [d, *chunk, h, g]
+    specs = [left, weight, weight, full((rows, D)), full((1, D))]
     if res is not None:
         args.append(res)
         specs.append(full((rows, D)))
@@ -305,16 +551,16 @@
         out_specs = [full((rows, D))] + out_specs
         out_shape = [jax.ShapeDtypeStruct((rows, D), F32)] + out_shape
     return pl.pallas_call(
-        functools.partial(back_kernel, res is not None, placed),
+        functools.partial(back_kernel, res is not None, placed, turned),
         grid_spec=pltpu.PrefetchScalarGridSpec(
             num_scalar_prefetch=1,
-            grid=(wide // part,),
+            grid=(1 if turned else 4,),
             in_specs=specs,
             out_specs=out_specs,
             scratch_shapes=[pltpu.VMEM((rows, D), F32), pltpu.VMEM((3, 8, D), F32)],
         ),
         out_shape=out_shape,
-        compiler_params=params(40),
+        compiler_params=params(VMEM),
         cost_estimate=pl.CostEstimate(
             flops=2 * rows * D * wide,
             bytes_accessed=rows * D * 14 + 2 * D * wide + 2 * rows * wide,
@@ -329,36 +575,49 @@
 PAIRS = HEADS // 2
 
 
+def lanes_of(side):
+    lane = lax.broadcasted_iota(jnp.int32, (1, PAIR), 1)
+    mine = (lane < HD) == (side == 0)
+    return lane, mine, HD * (1 - side)
+
+
+def masked_keys(keys, first, length, extra):
+    lane, mine, free = first
+    spot = lax.broadcasted_iota(jnp.int32, (keys.shape[0], 1), 0)
+    hidden = jnp.where(spot < length, 0.0, -1e30).astype(BF16)
+    rest = jnp.where(lane == free, hidden, 0.0).astype(BF16)
+    if extra:
+        ones = jnp.logical_and(lane > free, lane <= free + extra)
+        rest = jnp.where(ones, 1.0, rest).astype(BF16)
+    return jnp.where(mine, keys, rest)
+
+
 def attend_kernel(perm, lens, q_ref, k0_ref, k1_ref, v0_ref, v1_ref, o_ref, l_ref):
-    half = k0_ref.shape[0]
-    lane = lax.broadcasted_iota(jnp.int32, (1, PAIR), 1)
-    spot = lax.broadcasted_iota(jnp.int32, (1, half), 1)
-    see = [spot < lens[0], spot < lens[1]]
-    k0, k1, v0, v1 = k0_ref[...], k1_ref[...], v0_ref[...], v1_ref[...]
+    v0, v1 = v0_ref[...], v1_ref[...]
+    sides = [lanes_of(side) for side in range(2)]
+    keys = [
+        [masked_keys(ref[...], where, lens[j], 0) for j, ref in enumerate((k0_ref, k1_ref))]
+        for where in sides
+    ]
     chunk = 256
     for i in range(q_ref.shape[0] // chunk):
         rows = slice(i * chunk, (i + 1) * chunk)
-        q = q_ref[rows, :] * SCALE
+        q = (q_ref[rows, :] * SCALE).astype(BF16)
         outs = []
         logs = []
-        for side in range(2):
-            qm = jnp.where((lane < HD) == (side == 0), q, 0.0).astype(BF16)
-            s0 = jnp.where(see[0], nt(qm, k0), -1e30)
-            s1 = jnp.where(see[1], nt(qm, k1), -1e30)
-            top = jnp.maximum(
-                jnp.max(s0, axis=1, keepdims=True), jnp.max(s1, axis=1, keepdims=True)
-            )
+        for (lane, mine, free), (k0, k1) in zip(sides, keys):
+            qm = jnp.where(mine, q, jnp.where(lane == free, 1.0, 0.0).astype(BF16))
+            s0 = nt(qm, k0)
+            s1 = nt(qm, k1)
+            top = jnp.max(jnp.maximum(s0, s1), axis=1, keepdims=True)
             e0 = jnp.exp(s0 - top)
             e1 = jnp.exp(s1 - top)
-            total = jnp.sum(e0, axis=1, keepdims=True) + jnp.sum(e1, axis=1, keepdims=True)
-            inv = 1.0 / total
-            outs.append(nn((e0 * inv).astype(BF16), v0) + nn((e1 * inv).astype(BF16), v1))
+            total = jnp.sum(e0 + e1, axis=1, keepdims=True)
+            outs.append((nn(e0.astype(BF16), v0) + nn(e1.astype(BF16), v1)) * (1.0 / total))
             logs.append(top + jnp.log(total))
+        lane = sides[0][0]
         o_ref[rows, :] = jnp.where(lane < HD, outs[0], outs[1]).astype(BF16)
-        flat = jnp.where(lane < HD, logs[0], logs[1])
-        turned = flat.T
-        l_ref[0, 0:1, rows] = turned[0:1, :]
-        l_ref[0, 1:2, rows] = turned[HD : HD + 1, :]
+        l_ref[rows, :] = jnp.where(lane < HD, logs[1], logs[0])
 
 
 def attend(perm, lens, p, kv):
@@ -372,14 +631,14 @@
             in_specs=[block(0), block(PAIRS), block(0), block(2 * PAIRS), block(PAIRS)],
             out_specs=[
                 pl.BlockSpec((rows, PAIR), lambda h, m, n: (0, m[8 + h])),
-                pl.BlockSpec((1, 8, rows), lambda h, m, n: (h, 0, 0)),
+                block(0),
             ],
         ),
         out_shape=[
             jax.ShapeDtypeStruct((rows, D), BF16),
-            jax.ShapeDtypeStruct((PAIRS, 8, rows), F32),
+            jax.ShapeDtypeStruct((rows, D), F32),
         ],
-        compiler_params=params(40),
+        compiler_params=params(VMEM),
         cost_estimate=pl.CostEstimate(
             flops=8 * rows * rows * D,
             bytes_accessed=12 * rows * D,
@@ -392,43 +651,49 @@
 def attend_back_kernel(
     perm, lens, q_ref, k0_ref, k1_ref, v0_ref, v1_ref, do_ref, l_ref, dq_ref, own_ref, far_ref
 ):
-    half = k0_ref.shape[0]
-    lane = lax.broadcasted_iota(jnp.int32, (1, PAIR), 1)
-    spot = lax.broadcasted_iota(jnp.int32, (half, 1), 0)
-    see = [spot < lens[0], spot < lens[1]]
-    keys = [k0_ref[...], k1_ref[...]]
     values = [v0_ref[...], v1_ref[...]]
     q_all, do_all = q_ref[...], do_ref[...]
+    sides = [lanes_of(side) for side in range(2)]
+    keys = [
+        [masked_keys(ref[...], where, lens[j], 3) for j, ref in enumerate((k0_ref, k1_ref))]
+        for where in sides
+    ]
     chunk = 256
     dk = [None, None]
     dv = [None, None]
     for i in range(q_ref.shape[0] // chunk):
         rows = slice(i * chunk, (i + 1) * chunk)
-        dq = None
-        for side in range(2):
-            mine = (lane < HD) == (side == 0)
+        logs = l_ref[rows, :]
+        first = logs.astype(BF16)
+        left = logs - first.astype(F32)
+        second = left.astype(BF16)
+        third = (left - second.astype(F32)).astype(BF16)
+        dqs = []
+        for (lane, mine, free), (k0, k1) in zip(sides, keys):
             qm = jnp.where(mine, q_all[rows, :], 0.0).astype(BF16)
             dom = jnp.where(mine, do_all[rows, :], 0.0).astype(BF16)
-            qs = qm * SCALE
-            logs = l_ref[0, side : side + 1, rows]
-            probs = [
-                jnp.exp(jnp.where(see[j], nt(keys[j], qs), -1e30) - logs) for j in range(2)
-            ]
-            da = [nt(values[j], dom) for j in range(2)]
-            delta = sum(jnp.sum(probs[j] * da[j], axis=0, keepdims=True) for j in range(2))
-            for j in range(2):
-                ds = (probs[j] * (da[j] - delta) * SCALE).astype(BF16)
-                km = jnp.where(mine, keys[j], 0.0).astype(BF16)
-                term = tn(ds, km)
+            rest = jnp.where(lane == free, 1.0, 0.0).astype(BF16)
+            for at, part in enumerate((first, second, third)):
+                rest = jnp.where(lane == free + 1 + at, -part, rest)
+            qs = jnp.where(mine, (q_all[rows, :] * SCALE).astype(BF16), rest)
+            probs = [jnp.exp(nt(k, qs)) for k in (k0, k1)]
+            da = [nt(v, dom) for v in values]
+            delta = jnp.sum(probs[0] * da[0] + probs[1] * da[1], axis=0, keepdims=True)
+            dq = None
+            for j, k in enumerate((k0, k1)):
+                ds = (probs[j] * (da[j] - delta)).astype(BF16)
+                term = tn(ds, k)
                 dq = term if dq is None else dq + term
                 term = nn(ds, qm)
                 dk[j] = term if dk[j] is None else dk[j] + term
                 term = nn(probs[j].astype(BF16), dom)
                 dv[j] = term if dv[j] is None else dv[j] + term
-        dq_ref[rows, :] = dq.astype(BF16)
-    own_ref[0] = dk[0]
+            dqs.append(dq)
+        lane = sides[0][0]
+        dq_ref[rows, :] = (jnp.where(lane < HD, dqs[0], dqs[1]) * SCALE).astype(BF16)
+    own_ref[0] = dk[0] * SCALE
     own_ref[1] = dv[0]
-    far_ref[0] = dk[1].astype(BF16)
+    far_ref[0] = (dk[1] * SCALE).astype(BF16)
     far_ref[1] = dv[1].astype(BF16)
 
 
@@ -448,7 +713,7 @@
                 block(2 * PAIRS),
                 block(PAIRS),
                 pl.BlockSpec((rows, PAIR), lambda h, m, n: (0, m[8 + h])),
-                pl.BlockSpec((1, 8, rows), lambda h, m, n: (h, 0, 0)),
+                block(0),
             ],
             out_specs=[block(0), both, both],
         ),
@@ -457,7 +722,7 @@
             jax.ShapeDtypeStruct((2, rows, D), F32),
             jax.ShapeDtypeStruct((2, rows, D), BF16),
         ],
-        compiler_params=params(48),
+        compiler_params=params(VMEM),
         cost_estimate=pl.CostEstimate(
             flops=20 * rows * rows * D,
             bytes_accessed=28 * rows * D,
@@ -472,8 +737,8 @@
 
 
 def render_kernel(
-    terms, views_ref, inv_ref, z_ref, zx_ref, rd_ref, mc_ref, dz_ref, dzx_ref, loss_ref,
-    tf_ref, hi_ref, lo_ref, o_ref, wm_ref, a_ref, b_ref, dt_ref, tok_ref, edge_ref, zs_ref,
+    views_ref, inv_ref, z_ref, zx_ref, rd_ref, mc_ref, dz_ref, dzx_ref, loss_ref,
+    tf_ref, both_ref, o_ref, wm_ref, a_ref, dt_ref, tok_ref, edge_ref, zs_ref,
 ):
     width = 256
     pixels = rd_ref.shape[-1]
@@ -542,12 +807,13 @@
     for block in range(2):
         table = tf_ref[block]
         high = table.astype(BF16)
-        hi_ref[block] = high
-        lo_ref[block] = (table - high.astype(F32)).astype(BF16)
+        both_ref[block, : 4 * TABLE] = high
+        both_ref[block, 4 * TABLE :] = (table - high.astype(F32)).astype(BF16)
     dt_ref[...] = jnp.zeros_like(dt_ref)
     inverse = inv_ref[0]
-    row_hi = iota((width, pixels), 0)
+    row_hi = iota((width, pixels), 0).astype(F32).astype(BF16)
     row_lo = iota((TABLE, pixels), 0)
+    one_low, zero_low = jnp.ones((), BF16), jnp.zeros((), BF16)
 
     def features(c):
         return jnp.tanh(mc_ref[0] * c[0] + mc_ref[1] * c[1] + mc_ref[2] * c[2])
@@ -566,15 +832,16 @@
                 inside, g, NG + lax.shift_right_logical(g, 4) + jnp.where(after, 4, 0)
             )
             sums = [jnp.zeros((8, pixels), F32) for _ in range(4)]
-            t_hi = hi_ref[block]
-            t_lo = lo_ref[block]
+            high = high.astype(F32).astype(BF16)
+            table = both_ref[block]
             for k in range(kg):
                 cols = slice(k * pixels, (k + 1) * pixels)
-                one = jnp.where(row_hi == high[k : k + 1, :], 1.0, 0.0).astype(BF16)
-                o_ref[:, cols] = one
+                one = jnp.where(row_hi == high[k : k + 1, :], one_low, zero_low)
+                o_ref[block, :, cols] = one
                 wm = jnp.where(row_lo == low[k : k + 1, :], weight[k : k + 1, :], 0.0)
-                wm_ref[:, cols] = wm
-                picked = nn(t_hi, one) + nn(t_lo, one)
+                wm_ref[block, :, cols] = wm
+                picked = nn(table, one)
+                picked = picked[: 4 * TABLE] + picked[4 * TABLE :]
                 for ch in range(4):
                     part = picked[ch * TABLE : (ch + 1) * TABLE, :] * wm
                     sums[ch] = sums[ch] + jnp.sum(part.reshape(TABLE // 8, 8, pixels), axis=0)
@@ -598,17 +865,10 @@
             )
             for k in range(kg):
                 cols = slice(k * pixels, (k + 1) * pixels)
-                wm = wm_ref[:, cols]
+                wm = wm_ref[block, :, cols]
                 full = jnp.concatenate([wm * d_sum[ch] for ch in range(4)], axis=0)
-                first = full.astype(BF16)
-                a_ref[:, cols] = first
-                if terms > 1:
-                    b_ref[:, cols] = (full - first.astype(F32)).astype(BF16)
-            ones = o_ref[...]
-            grad = nt(a_ref[...], ones)
-            if terms > 1:
-                grad = grad + nt(b_ref[...], ones)
-            dt_ref[block] += grad
+                a_ref[block, :, cols] = full.astype(BF16)
+            dt_ref[block] += nt(a_ref[block], o_ref[block])
         return loss
 
     loss = lax.fori_loop(0, views_ref[0], view, jnp.zeros((1, pixels), F32))
@@ -643,7 +903,7 @@
     dzx_ref[...] = zs_ref[parts]
 
 
-def render(views, inverse, zt, zx, rd, terms):
+def render(views, inverse, zt, zx, rd):
     tokens = zt.shape[1]
     pixels = rd.shape[-1]
     slots = 8 * pixels
@@ -654,24 +914,22 @@
     smem = pl.BlockSpec(memory_space=pltpu.SMEM)
     shape = jax.ShapeDtypeStruct
     return pl.pallas_call(
-        functools.partial(render_kernel, terms),
+        render_kernel,
         in_specs=[smem, smem, whole(zt), whole(zx), whole(rd), whole(mix)],
         out_specs=[whole(zt), whole(zx), pl.BlockSpec((8, 128), lambda: (0, 0))],
         out_shape=[shape(zt.shape, F32), shape(zx.shape, F32), shape((8, 128), F32)],
         scratch_shapes=[
             pltpu.VMEM((2, 4 * TABLE, 256), F32),
-            pltpu.VMEM((2, 4 * TABLE, 256), BF16),
-            pltpu.VMEM((2, 4 * TABLE, 256), BF16),
-            pltpu.VMEM((256, slots), BF16),
-            pltpu.VMEM((TABLE, slots), F32),
-            pltpu.VMEM((4 * TABLE, slots), BF16),
-            pltpu.VMEM((4 * TABLE, slots), BF16),
+            pltpu.VMEM((2, 8 * TABLE, 256), BF16),
+            pltpu.VMEM((2, 256, slots), BF16),
+            pltpu.VMEM((2, TABLE, slots), F32),
+            pltpu.VMEM((2, 4 * TABLE, slots), BF16),
             pltpu.VMEM((2, 4 * TABLE, 256), F32),
             pltpu.VMEM((4 * NG, tokens), F32),
             pltpu.VMEM((4 * NG, 128), F32),
             pltpu.VMEM((tokens // 128 + 1, POUT, 128), F32),
         ],
-        compiler_params=pltpu.CompilerParams(vmem_limit_bytes=48 * VMEM_MB),
+        compiler_params=pltpu.CompilerParams(vmem_limit_bytes=VMEM * VMEM_MB),
         cost_estimate=pl.CostEstimate(
             flops=24 * slots * 4 * TABLE * 256 * 6, bytes_accessed=4 * 1024 * 1024, transcendentals=0
         ),
@@ -696,15 +954,156 @@
     return x
 
 
-def gather_plain(shard):
-    return lax.all_gather(
-        lax.all_gather(shard, "rows", axis=1, tiled=True), "scene", axis=0, tiled=True
-    )
-
-
-def scatter_plain(grad):
-    part = lax.psum_scatter(grad, "scene", scatter_dimension=0, tiled=True)
-    return lax.psum_scatter(part, "rows", scatter_dimension=1, tiled=True).astype(F32)
+def gather_whole(shard):
+    whole = lax.all_gather(shard, ("scene", "rows"), axis=0)
+    return (whole.reshape((BLOCKS, 4) + shard.shape),) * 2
+
+
+def scatter_whole(grad):
+    part = lax.psum_scatter(grad[0], "scene", scatter_dimension=0)
+    return lax.psum_scatter(part, "rows", scatter_dimension=0).astype(F32)
+
+
+def gather_plain(shards, turned):
+    parts = []
+    for shard in shards:
+        if turned:
+            wide = lax.all_gather(shard, "rows", axis=0, tiled=True)
+            full = lax.all_gather(wide, "scene", axis=1, tiled=True)
+            parts.append(jnp.transpose(full.reshape(4, -1, BLOCKS, WIDE), (2, 0, 1, 3)))
+        else:
+            wide = lax.all_gather(shard, "rows", axis=1, tiled=True)
+            full = lax.all_gather(wide, "scene", axis=0, tiled=True)
+            blocks = full.reshape(BLOCKS, full.shape[0] // BLOCKS, 4, -1)
+            parts.append(jnp.transpose(blocks, (0, 2, 1, 3)))
+    chunk = jnp.concatenate(parts, axis=2 if turned else 3)
+    return chunk[:4], chunk[4:]
+
+
+def scatter_plain(grad, turned):
+    both = jnp.concatenate(grad, axis=0)
+    if turned:
+        full = jnp.transpose(both, (1, 2, 0, 3)).reshape(-1, D)
+    else:
+        full = jnp.transpose(both, (0, 2, 1, 3)).reshape(both.shape[0] * both.shape[2], -1)
+    part = lax.psum_scatter(full, "scene", scatter_dimension=int(turned), tiled=True)
+    return lax.psum_scatter(part, "rows", scatter_dimension=1 - turned, tiled=True).astype(F32)
+
+
+CORE, XBIT, YBIT = 1, 2, 4
+PLACES = np.array([0, 2, 4, 6, 1, 3, 5, 7], np.int32)
+
+
+def stack_kernel(*refs):
+    *parts, out_ref = refs
+    for i, ref in enumerate(parts):
+        out_ref[i] = ref[...]
+
+
+def stack(parts):
+    shape = parts[0].shape
+    lead = shape[:-2]
+    steps = lead[0] if lead else 1
+    block = (1,) * len(lead) + shape[-2:]
+    rest = (0,) * (len(shape) - 1) if lead else (0, 0)
+    place = lambda i: ((i,) + rest) if lead else rest
+    return pl.pallas_call(
+        stack_kernel,
+        grid=(steps,),
+        in_specs=[pl.BlockSpec(block, place)] * len(parts),
+        out_specs=pl.BlockSpec((len(parts),) + block, lambda i: (0,) + place(i)),
+        out_shape=jax.ShapeDtypeStruct((len(parts),) + shape, parts[0].dtype),
+        compiler_params=params(VMEM),
+        cost_estimate=pl.CostEstimate(
+            flops=0, bytes_accessed=4 * len(parts) * parts[0].size, transcendentals=0
+        ),
+        name="stack",
+    )(*parts)
+
+
+def tie(x, *earlier):
+    return lax.optimization_barrier((x,) + earlier)[0]
+
+
+def share_rows(x):
+    return lax.all_to_all(x, "rows", 0, 0)
+
+
+class Gather:
+    def __init__(self, shard, order):
+        self.shard = shard
+        self.first, self.second = (XBIT, YBIT) if order == "xy" else (YBIT, XBIT)
+
+    def rows(self, *earlier):
+        shard = tie(self.shard, *earlier)
+        self.own = share_rows(jnp.broadcast_to(shard[None], (4,) + shard.shape))
+
+    def near(self, *earlier):
+        self.own = tie(self.own, *earlier)
+        self.one = swap(self.own, "scene", self.first)
+        self.two = swap(self.own, "scene", self.second)
+        return self.own
+
+    def cross(self, *earlier):
+        self.one = tie(self.one, *earlier)
+        self.both = swap(self.one, "scene", self.second)
+        return self.one
+
+    def core(self, *earlier):
+        x, y = (self.one, self.two) if self.first == XBIT else (self.two, self.one)
+        self.half = stack([tie(self.own, *earlier), x, y, self.both])
+        return self.half
+
+    def get(self):
+        return self.half, swap(self.half, "scene", CORE)
+
+
+class Scatter:
+    def __init__(self, grad, streams):
+        self.keep, send = grad
+        self.streams = streams
+        self.got = swap(send, "scene", CORE)
+
+    def near(self, *earlier):
+        keep = tie(self.keep, *earlier)
+        shape = (2, 2) + keep.shape[1:]
+        total = keep.reshape(shape).astype(F32) + self.got.reshape(shape).astype(F32)
+        count = 4 // len(self.streams)
+        self.sums, self.moved = [], []
+        for i, order in enumerate(self.streams):
+            part = total[:, :, i * count : (i + 1) * count]
+            if order == "xy":
+                near, far, bit = part[:, 0], part[:, 1], XBIT
+            else:
+                near, far, bit = part[0], part[1], YBIT
+            self.sums.append(near)
+            self.moved.append(swap(far.astype(BF16), "scene", bit))
+        return self.moved[0]
+
+    def cross(self, *earlier):
+        for i, order in enumerate(self.streams):
+            near = self.sums[i] + tie(self.moved[i], *earlier).astype(F32)
+            self.sums[i] = near[0]
+            self.moved[i] = swap(near[1].astype(BF16), "scene", YBIT if order == "xy" else XBIT)
+        return self.moved[0]
+
+    def rows(self, *earlier):
+        mine = [
+            (near + tie(moved, *earlier).astype(F32)).astype(BF16)
+            for near, moved in zip(self.sums, self.moved)
+        ]
+        self.sums = share_rows(mine[0] if len(mine) == 1 else jnp.concatenate(mine, axis=0))
+        return mine[0]
+
+    def get(self, *earlier):
+        return jnp.sum(tie(self.sums, *earlier).astype(F32), axis=0)
+
+
+def weight_step(grad, factor, moment, master, average):
+    clipped = grad * factor
+    moment_new = MOMENTUM * moment + clipped
+    weight_new = master - STEP_RATE * (clipped + MOMENTUM * moment_new)
+    return moment_new, weight_new, AVERAGE_DECAY * average + (1.0 - AVERAGE_DECAY) * weight_new
 
 
 def to_items(x):
@@ -738,38 +1137,78 @@
     pixel_count = jnp.sum(target_views).astype(F32) * (
         raster_weight.shape[-1] * lax.axis_size("rows")
     )
-    perm = jnp.concatenate([jnp.arange(8, dtype=jnp.int32)] * 2)
+    natural = jnp.arange(BLOCKS, dtype=jnp.int32)
+    plain = jnp.concatenate([natural, natural, natural[:4]])
+    placed = lax.axis_size("scene") == BLOCKS and lax.axis_size("rows") == 4
+    if placed:
+        apart = jnp.bitwise_xor(natural, scene.astype(jnp.int32))
+        at = jnp.bitwise_xor(jnp.asarray(PLACES), scene.astype(jnp.int32))
+        spots = jnp.bitwise_and(apart, 1) * 4 + lax.shift_right_logical(apart, 1)
+        perm = jnp.concatenate([at, spots, natural[:4]])
+    else:
+        perm = plain
 
     gains = [vectors[None, i * D : (i + 1) * D] for i in range(9)]
     bias_up = vectors[None, 9 * D : 9 * D + FF]
     bias_gauss = vectors[9 * D + FF :]
 
     low = [w.astype(BF16) for w in masters[:6]]
-    low[0] = low[0].T
-    weights = [gather_plain(w) for w in low]
-    w_patch, w_joint, w_out, w_up, w_down, w_gauss = weights
-
-    x = to_items(patches[:, 0]).reshape(tokens, -1)
+    low[5] = low[5].T
+    x_in = patches[:, 0]
     drawn = jnp.concatenate(
         [gauss_index[:, 0].astype(F32), raster_weight[:, 0], target_color[:, 0]], axis=1
     )
-    rd = to_items(jnp.transpose(drawn, (0, 2, 1, 3)))
-
-    h0, a1 = embed(perm, x, w_patch, gains[6], gains[0], gains[3])
-    p = nn(a1, w_joint).astype(BF16)
+    drawn = jnp.transpose(drawn, (0, 2, 1, 3))
+    if placed:
+        side_w = Gather(jnp.concatenate([low[0], low[5]], axis=0), "yx")
+        first_w = Gather(low[1], "xy")
+        second_w = Gather(jnp.concatenate([low[3], low[2]], axis=1), "yx")
+        side_w.rows()
+        x = to_items(x_in)
+        first_w.rows(side_w.own)
+        own = side_w.near()
+        one = side_w.cross(own, x)
+        own = first_w.near(one)
+        second_w.rows(own)
+        w_third = gather_whole(tie(low[4], own))
+        half = side_w.core(own)
+        w_side = side_w.get()
+        one = first_w.cross(half)
+        x = tie(x, one)
+    else:
+        w_side = gather_plain([low[0], low[5]], True)
+        w_first = gather_plain([low[1]], False)
+        w_second = gather_plain([low[3], low[2]], False)
+        w_third = gather_plain([low[4]], False)
+    if not placed:
+        x = to_items(x_in)
+    x = x.reshape(tokens, -1)
+    h0, a1 = embed(perm, x, w_side, gains[6], gains[0], gains[3])
+    if placed:
+        own = second_w.near(a1)
+        first_w.core(own)
+        w_first = first_w.get()
+    p = joint(perm, a1, w_first)
     kv = swap(p[:, D:], "scene", 1)
+    if placed:
+        second_w.cross(p)
+        drawn = tie(drawn, second_w.one)
     mixed, logs = attend(perm, lens, p, kv)
-    h1, a2 = project(perm, mixed, w_out, h0, gains[7], gains[1], gains[4])
-    u, act = up_project(perm, a2, w_up, bias_up)
-    h2, a3 = project(perm, act, w_down, h1, gains[8], gains[2], gains[5])
-    zt = lax.dot_general(w_gauss, a3, (((0,), (1,)), ((), ())), preferred_element_type=F32)
-    zt = zt + bias_gauss[:, None]
+    if placed:
+        second_w.core(mixed)
+        w_second = second_w.get()
+    rd = to_items(drawn)
+    h1, a2 = project(perm, mixed, w_second, 4, h0, gains[7], gains[1], gains[4])
+    u, act = up_project(plain, a2, w_second, bias_up)
+    h2, a3 = project(perm, act, w_third, 0, h1, gains[8], gains[2], gains[5])
+    zt = gauss(perm, a3, w_side, bias_gauss)
+    rd = tie(rd, zt)
 
     edge = swap(jnp.where(side == 0, zt[:, tokens - HT :], zt[:, :HT]), "scene", 1)
     before = jnp.where(side == 0, 0.0, edge)
     after = jnp.where(side == 0, edge, 0.0)
     zx = jnp.concatenate([before, after, jnp.zeros((POUT, 128 - 2 * HT), F32)], axis=1)
-    dzt, dzx, loss = render(views, (1.0 / pixel_count).reshape(1), zt, zx, rd, 2)
+    dzt, dzx, loss = render(views, (1.0 / pixel_count).reshape(1), zt, zx, rd)
     back = swap(jnp.where(side == 0, dzx[:, HT : 2 * HT], dzx[:, :HT]), "scene", 1)
     dzt = jnp.concatenate(
         [
@@ -780,28 +1219,68 @@
         axis=1,
     )
     d_bias_gauss = jnp.sum(dzt, axis=1)
-    dz = dzt.astype(BF16).T
-
-    dw_gauss = tn(a3, dz).astype(BF16)
-    dh2, dh2_low, sums3 = norm_back(perm, dz, w_gauss, h2, gains[2], None, False)
-    dw_down = tn(act, dh2_low).astype(BF16)
-    du, d_bias_up = down_back(perm, dh2_low, w_down, u)
-    dw_up = tn(a2, du).astype(BF16)
-    dh1, dh1_low, sums2 = norm_back(perm, du, w_up, h1, gains[1], dh2, False)
-    dw_out = tn(mixed, dh1_low).astype(BF16)
-    do = nt(dh1_low, w_out).astype(BF16)
+    dz = dzt.astype(BF16)
+
+    streams = ("xy", "yx")
+    dw_gauss = side_grad(perm, dz, a3, placed)
+    if placed:
+        r_gauss = scatter_whole(dw_gauss)
+        dz = tie(dz, dw_gauss[0])
+    dh2, dh2_low, sums3 = norm_back(perm, dz, w_side, True, h2, gains[2], None, False)
+    dw_down = weight_grad(plain, act, dh2_low, placed)
+    d_low = dh2_low
+    if placed:
+        r_down = scatter_whole(dw_down)
+        d_low = tie(dh2_low, dw_down[0])
+    du, d_bias_up = down_back(plain, d_low, w_third, u)
+    dw_up = weight_grad(perm, a2, du)
+    if placed:
+        su = Scatter(dw_up, streams)
+        du = tie(du, dw_up[0])
+    dh1, dh1_low, sums2 = norm_back(perm, du, w_second, False, h1, gains[1], dh2, False)
+    d_low = dh1_low
+    if placed:
+        su.near(dh1_low)
+        d_low = tie(dh1_low, su.sums[0])
+    dw_out = weight_grad(perm, mixed, d_low)
+    if placed:
+        so = Scatter(dw_out, ("xy",))
+        d_low = tie(dh1_low, dw_out[0])
+    do = out_back(perm, d_low, w_second)
     dq, own, far = attend_back(perm, lens, p, kv, do, logs)
     got = swap(far, "scene", 1)
+    if placed:
+        su.cross(dq)
+        so.near(su.sums[0])
+        got = tie(got, so.sums[0])
     dkv = (own + got.astype(F32)).astype(BF16)
     dp = jnp.concatenate([dq, dkv[0], dkv[1]], axis=1)
-    dw_joint = tn(a1, dp).astype(BF16)
-    dh0_low, sums1 = norm_back(perm, dp, w_joint, h0, gains[0], dh1, True)
-    dw_patch = tn(dh0_low, x).astype(BF16)
-
-    reduced = [
-        scatter_plain(g) for g in (dw_patch, dw_joint, dw_out, dw_up, dw_down, dw_gauss)
-    ]
-    reduced[0] = reduced[0].T
+    dw_joint = weight_grad(perm, a1, dp)
+    dp_last = dp
+    if placed:
+        sj = Scatter(dw_joint, streams)
+        dp_last = tie(dp, dw_joint[0])
+    dh0_low, sums1 = norm_back(perm, dp_last, w_first, False, h0, gains[0], dh1, True)
+    d_low = dh0_low
+    if placed:
+        sj.near(dh0_low)
+        d_low = tie(dh0_low, sj.sums[0])
+    dw_patch = side_grad(perm, x.T, d_low)
+    if placed:
+        sp = Scatter(dw_patch, ("yx",))
+        so.cross(dw_patch[0], r_gauss)
+        moved = su.rows(so.sums[0])
+        sp.near(moved)
+        sj.cross(sp.sums[0], r_down)
+        moved = so.rows(sj.sums[0])
+        sp.cross(moved)
+        moved = sj.rows(sp.sums[0])
+        sp.rows(moved)
+        reduced = [t.get() for t in (sp, sj, so, su)] + [r_down, r_gauss]
+    else:
+        grads = [dw_patch, dw_joint, dw_out, dw_up, dw_down, dw_gauss]
+        reduced = [scatter_plain(g, i in (0, 5)) for i, g in enumerate(grads)]
+    reduced[5] = reduced[5].T
     vector_part = jnp.concatenate(
         [sums1[0], sums2[0], sums3[0], sums1[1], sums2[1], sums3[1], sums1[2], sums2[2], sums3[2]]
         + [d_bias_up[0], d_bias_gauss, loss[0]]
@@ -815,12 +1294,10 @@
     factor = jnp.minimum(1.0, CLIP_NORM / (grad_norm + 1e-06))
     next_moments, next_weights, next_averages = ([], [], [])
     for grad, moment, master, average in zip(reduced + [vector_grad], moments, masters, averages):
-        clipped = grad * factor
-        moment_new = MOMENTUM * moment + clipped
-        weight_new = master - STEP_RATE * (clipped + MOMENTUM * moment_new)
-        next_moments.append(moment_new)
-        next_weights.append(weight_new)
-        next_averages.append(AVERAGE_DECAY * average + (1.0 - AVERAGE_DECAY) * weight_new)
+        moment, weight, mean = weight_step(grad, factor, moment, master, average)
+        next_moments.append(moment)
+        next_weights.append(weight)
+        next_averages.append(mean)
     return (loss_sum, pixel_count, grad_norm, *next_moments, *next_weights, *next_averages)
 
 

time: 984 us -> 690 us (0.70)
  waiting for transfers between devices: 547 us -> 217 us
  starting transfers between devices: 13.9 us -> 98.2 us
  blocking collectives: 71.9 us -> 0 us
  matrix products: 41.8 us -> 0 us
  Pallas kernels: 170 us -> 211 us
  other arithmetic: 32.5 us -> 57.5 us
    reduce_scatter x10 -> x4, waiting for transfers between devices: 329 us -> 0.01 us  [the longest x2 0.01 us: scatter_whole(): part = lax.psum_scatter(grad[0], 'scene', scatter_dimension=0)]
    ppermute x9 -> x37, waiting for transfers between devices: 15.5 us -> 164 us  [swap(): return lax.ppermute(x, axis, flip_pairs(lax.axis_size(axis), bit))]
    all_gather x8 -> x1, waiting for transfers between devices: 127 us -> 0.01 us  [gather_whole(): whole = lax.all_gather(shard, ('scene', 'rows'), axis=0)]
    all_gather x4 -> x0, blocking collectives: 71.9 us -> none  [gather_plain(): lax.all_gather(shard, 'rows', axis=1, tiled=True)]
    unnamed x22 -> x5, waiting for transfers between devices: 63.6 us -> 0.63 us
    ppermute x9 -> x37, starting transfers between devices: 5.88 us -> 51 us  [swap(): return lax.ppermute(x, axis, flip_pairs(lax.axis_size(axis), bit))]
    pallas_call x4 -> x16, Pallas kernels: 67.8 us -> 110 us  [the longest x1 30.3 us: render(): pl.pallas_call(render_kernel, in_specs=[smem, smem, whole(zt), whole(zx),...]
    dot_general x9 -> x0, matrix products: 41.8 us -> none  [the longest x6 31.5 us: tn(): lax.dot_general(a, b, (((0,), (0,)), ((), ())), preferred_element_type=F32)]
  transfers between devices with their start and end apart: 33 -> 53, of which waited for: 25 -> 28; matrix products, arithmetic and copies ran while one was open for 7% -> 8% of each run, Pallas kernels for 14% -> 22%
where the time goes in v2:
time: 690 us; the launch traced here: 682 us
  waiting for transfers between devices  217 us (31%)
  Pallas kernels  211 us (31%)
  starting transfers between devices  98.2 us (14%)
  local copies, waits for them, and re-layouts  73.8 us (11%)
  other arithmetic  57.5 us (8%)
  between operations  25 us (4%)
    ppermute x37, waiting for transfers between devices, swap(): return lax.ppermute(x, axis, flip_pairs(lax.axis_size(axis), bit))  164 us
    unnamed x224, local copies, waits for them, and re-layouts  58.1 us
    ppermute x37, starting transfers between devices, swap(): return lax.ppermute(x, axis, flip_pairs(lax.axis_size(axis), bit))  51 us
    all_to_all x7, starting transfers between devices, share_rows(): return lax.all_to_all(x, 'rows', 0, 0)  36.4 us
    all_to_all x7, waiting for transfers between devices, share_rows(): return lax.all_to_all(x, 'rows', 0, 0)  35.5 us
    pallas_call x1, Pallas kernels, attend_back(): pl.pallas_call(attend_back_kernel, grid_spec=pltpu.PrefetchScalarGridSpec...  35.4 us
    pallas_call x1, Pallas kernels, render(): pl.pallas_call(render_kernel, in_specs=[smem, smem, whole(zt), whole(zx),...  30.3 us
    pallas_call x3, Pallas kernels, norm_back(): pl.pallas_call(functools.partial(back_kernel, res is not None, placed, tu...  29.9 us
  transfers between devices with their start and end apart: 53, of which 28 were waited for; matrix products, arithmetic and copies ran while one was open for 8% of the time, Pallas kernels for 22%

profile of v2, /device:TPU:0, one launch (start us, length us, event | category | flops | bytes accessed | tf_op | source)
XLA Modules:
  0.0 682.4 jit_solution(10917346993840484603)
XLA Ops:
  9.8 6.3 all-to-all-start
  17.2 9.6 %all-to-all-done.refs_0_ = bf16[4,336,128]{2,1,0:T(8,128)(2,1)S(1)} async-done(((bf16[4,336,128]{2,1,0:T(8,128)(2,1)}), bf16[4,336,128]{2,1,0:T(8,128)(2,1)S(1)}, u32[]{:S(2)}, u32[]{:S(2)}) %all-to-all-start) | async-done | bytes 344096 | tf_op jit(solution)/shard_map/all_to_all | solution.py:1029
  39.3 12.3 %collective-permute-done.1 = bf16[256,576]{0,1:T(8,128)(2,1)} collective-permute-done((bf16[256,576]{0,1:T(8,128)(2,1)S(1)}, bf16[256,576]{0,1:T(8,128)(2,1)}, u32[]{:S(2)}, u32[]{:S(2)}) %collective-permute-start.1) | collective-permute-done | bytes 294944 | tf_op jit(solution)/shard_map/ppermute | solution.py:1121
  58.3 9.0 %all-to-all-start.2 = ((bf16[4,128,1280]{2,1,0:T(8,128)(2,1)}), bf16[4,128,1280]{2,1,0:T(8,128)(2,1)}, u32[]{:S(2)}, u32[]{:S(2)}) async-start(bf16[4,128,1280]{2,1,0:T(8,128)(2,1)} %broadcast_in_dim.76), calls=%async_computation.2 | async-start | bytes 2621440 | tf_op jit(solution)/shard_map/all_to_all | solution.py:1029
  70.9 7.8 %collective-permute-done.4.refs_1_ = bf16[4,336,128]{2,1,0:T(8,128)(2,1)S(1)} collective-permute-done((bf16[4,336,128]{2,1,0:T(8,128)(2,1)S(1)}, bf16[4,336,128]{2,1,0:T(8,128)(2,1)S(1)}, u32[]{:S(2)}, u32[]{:S(2)}) %collective-permute-start.4) | collective-permute-done | bytes 344096 | tf_op jit(solution)/shard_map/ppermute | solution.py:945
  78.7 7.4 %collective-permute-done.5.refs_3_ = bf16[4,336,128]{2,1,0:T(8,128)(2,1)S(1)} collective-permute-done((bf16[4,336,128]{2,1,0:T(8,128)(2,1)S(1)}, bf16[4,336,128]{2,1,0:T(8,128)(2,1)S(1)}, u32[]{:S(2)}, u32[]{:S(2)}) %collective-permute-start.5) | collective-permute-done | bytes 344096 | tf_op jit(solution)/shard_map/ppermute | solution.py:945
  93.0 10.0 %collective-permute-done.3.refs_1_ = bf16[4,128,768]{2,1,0:T(8,128)(2,1)} collective-permute-done((bf16[4,128,768]{2,1,0:T(8,128)(2,1)S(1)}, bf16[4,128,768]{2,1,0:T(8,128)(2,1)}, u32[]{:S(2)}, u32[]{:S(2)}) %collective-permute-start.3) | collective-permute-done | bytes 786464 | tf_op jit(solution)/shard_map/ppermute | solution.py:945
  121.2 14.6 %collective-permute-done.8.refs_3_ = bf16[4,128,768]{2,1,0:T(8,128)(2,1)} collective-permute-done((bf16[4,128,768]{2,1,0:T(8,128)(2,1)}, bf16[4,128,768]{2,1,0:T(8,128)(2,1)}, u32[]{:S(2)}, u32[]{:S(2)}) %collective-permute-start.8) | collective-permute-done | bytes 786464 | tf_op jit(solution)/shard_map/ppermute | solution.py:945
  153.2 21.6 %collective-permute-done.12.refs_2_ = bf16[4,128,1280]{2,1,0:T(8,128)(2,1)} collective-permute-done((bf16[4,128,1280]{2,1,0:T(8,128)(2,1)}, bf16[4,128,1280]{2,1,0:T(8,128)(2,1)}, u32[]{:S(2)}, u32[]{:S(2)}) %collective-permute-start.12) | collective-permute-done | bytes 1310752 | tf_op jit(solution)/shard_map/ppermute | solution.py:945
  180.1 19.9 %attend.1 = (bf16[512,1024]{1,0:T(8,128)(2,1)S(1)}, f32[512,1024]{1,0:T(8,128)S(1)}) custom-call(s32[20]{0:T(128)S(1)} %get-tuple-element.232.perm, s32[2]{0:T(128)S(1)} %pad_add_fusion.lens, bf16[512,3072]{1,0:T(8,128)(2,1)S(1)} %copy-done.32, bf16[512,3072]{1,0:T(8,128)(2,1)S(1)} %copy-done.32, bf16[512,2048]{1,0:T(8,128)(2,1)} %collective-permute-done.10.k1_ref.v1_ref, ...), custom_call_target="tpu_custom_call" | custom-call | flops 2147483648 | bytes 6291456 | tf_op jit(solution)/shard_map/attend/pallas_call | solution.py:626
  202.3 9.2 %collective-permute-done.13.refs_3_ = bf16[4,128,1280]{2,1,0:T(8,128)(2,1)} collective-permute-done((bf16[4,128,1280]{2,1,0:T(8,128)(2,1)}, bf16[4,128,1280]{2,1,0:T(8,128)(2,1)}, u32[]{:S(2)}, u32[]{:S(2)}) %collective-permute-start.13) | collective-permute-done | bytes 1310752 | tf_op jit(solution)/shard_map/ppermute | solution.py:945
  235.5 7.3 %project_norm.2 = (f32[512,1024]{1,0:T(8,128)S(1)}, bf16[512,1024]{1,0:T(8,128)(2,1)S(1)}) custom-call(s32[20]{0:T(128)S(1)} %get-tuple-element.232.perm, bf16[512,1024]{1,0:T(8,128)(2,1)S(1)} %copy-done.37, bf16[4,4,128,1280]{3,2,1,0:T(8,128)(2,1)} %stack.41.w0_ref.refs_1_, bf16[4,4,128,1280]{3,2,1,0:T(8,128)(2,1)} %collective-permute-done.14.w1_ref.refs_2_, ...), custom_call_target="tpu_custom_call" | custom-call | flops 1073741824 | bytes 8388608 | tf_op jit(solution)/shard_map/project_norm/pallas_call | solution.py:155
  244.1 10.9 %up_gelu.1 = (f32[512,4096]{1,0:T(8,128)S(1)}, bf16[512,4096]{1,0:T(8,128)(2,1)S(1)}) custom-call(s32[20]{0:T(128)S(1)} %copy-done.52, bf16[512,1024]{1,0:T(8,128)(2,1)S(1)} %get-tuple-element.110.a_ref, bf16[4,4,128,1280]{3,2,1,0:T(8,128)(2,1)} %stack.41.w0_ref.refs_1_, bf16[4,4,128,1280]{3,2,1,0:T(8,128)(2,1)} %collective-permute-done.14.w1_ref.refs_2_, ...), custom_call_target="tpu_custom_call" | custom-call | flops 4294967296 | bytes 20971520 | tf_op jit(solution)/shard_map/up_gelu/pallas_call | solution.py:374
  268.7 9.6 %project_norm.3 = (f32[512,1024]{1,0:T(8,128)S(1)}, bf16[512,1024]{1,0:T(8,128)(2,1)S(1)}) custom-call(s32[20]{0:T(128)S(1)} %get-tuple-element.232.perm, bf16[512,4096]{1,0:T(8,128)(2,1)S(1)} %copy-done.16, bf16[8,4,512,256]{3,2,1,0:T(8,128)(2,1)S(1)} %bitcast.186, bf16[8,4,512,256]{3,2,1,0:T(8,128)(2,1)S(1)} %bitcast.187, f32[512,1024]{1,0:T(8,128)S(1)} %copy-done.5, ...), custom_call_target="tpu_custom_call" | custom-call | flops 4294967296 | bytes 17825792 | tf_op jit(solution)/shard_map/project_norm/pallas_call | solution.py:155
  281.4 6.1 collective-permute-start.15
  289.1 30.3 %render.1 = (f32[768,512]{1,0:T(8,128)S(1)}, f32[768,128]{1,0:T(8,128)S(1)}, f32[8,128]{1,0:T(8,128)S(1)}) custom-call(s32[1]{0:T(128)} %bitcast.11.views_ref, f32[1]{0:T(128)} %bitcast.12.inv_ref, f32[768,512]{1,0:T(8,128)S(1)} %gauss.1.z_ref, f32[768,128]{1,0:T(8,128)S(1)} %maximum_maximum_fusion.zx_ref, f32[2,12,19,256]{3,2,1,0:T(8,128)S(1)} %pad_maximum_fusion.5.rd_ref, ...), custom_call_target="tpu_custom_call" | custom-call | flops 21743271936 | bytes 4194304 | tf_op jit(solution)/shard_map/render/pallas_call | solution.py:916
  327.8 6.2 norm_back.3
  336.0 7.8 %weight_grad.4 = bf16[8,4,512,256]{3,2,1,0:T(8,128)(2,1)S(1)} custom-call(s32[20]{0:T(128)S(1)} %copy-done.53, bf16[512,4096]{1,0:T(8,128)(2,1)S(1)} %copy-done.17, bf16[512,1024]{1,0:T(8,128)(2,1)S(1)} %get-tuple-element.122.d_ref), custom_call_target="tpu_custom_call" | custom-call | flops 4294967296 | bytes 13631488 | tf_op jit(solution)/shard_map/weight_grad/pallas_call | solution.py:304
  356.1 12.6 %down_back_gelu.1 = (bf16[512,4096]{1,0:T(8,128)(2,1)S(1)}, f32[1,4096]{1,0:T(1,128)S(1)}) custom-call(s32[20]{0:T(128)S(1)} %copy-done.54, bf16[512,1024]{1,0:T(8,128)(2,1)S(1)} %copy-done.40, bf16[8,4,512,256]{3,2,1,0:T(8,128)(2,1)S(1)} %bitcast.188, bf16[8,4,512,256]{3,2,1,0:T(8,128)(2,1)S(1)} %bitcast.189, f32[512,4096]{1,0:T(8,128)S(1)} %copy-done.9), custom_call_target="tpu_custom_call" | custom-call | flops 4294967296 | bytes 20971520 | tf_op jit(solution)/shard_map/down_back_gelu/pallas_call | solution.py:425
  368.7 6.8 weight_grad.5
  379.6 13.2 %norm_back.4 = (f32[512,1024]{1,0:T(8,128)S(1)}, bf16[512,1024]{1,0:T(8,128)(2,1)S(1)}, f32[8,1024]{1,0:T(8,128)S(1)}) custom-call(s32[20]{0:T(128)S(1)} %get-tuple-element.232.perm, bf16[512,4096]{1,0:T(8,128)(2,1)S(1)} %get-tuple-element.126.d_ref.refs_0_, bf16[4,4,128,1280]{3,2,1,0:T(8,128)(2,1)} %stack.41.w0_ref.refs_1_, ...), custom_call_target="tpu_custom_call" | custom-call | flops 4294967296 | bytes 19922944 | tf_op jit(solution)/shard_map/norm_back/pallas_call | solution.py:553
  400.1 35.4 %attend_back.1 = (bf16[512,1024]{1,0:T(8,128)(2,1)S(1)}, f32[2,512,1024]{2,1,0:T(8,128)S(1)}, bf16[2,512,1024]{2,1,0:T(8,128)(2,1)}) custom-call(s32[20]{0:T(128)S(1)} %get-tuple-element.232.perm, s32[2]{0:T(128)S(1)} %copy-done.64, bf16[512,3072]{1,0:T(8,128)(2,1)S(1)} %copy-done.33, bf16[512,3072]{1,0:T(8,128)(2,1)S(1)} %copy-done.33, ...), custom_call_target="tpu_custom_call" | custom-call | flops 5368709120 | bytes 14680064 | tf_op jit(solution)/shard_map/attend_back/pallas_call | solution.py:704
  446.4 10.1 %collective-permute-start.25 = (bf16[2,4,128,256]{3,2,1,0:T(8,128)(2,1)S(1)}, bf16[2,4,128,256]{3,2,1,0:T(8,128)(2,1)}, u32[]{:S(2)}, u32[]{:S(2)}) collective-permute-start(bf16[2,4,128,256]{3,2,1,0:T(8,128)(2,1)S(1)} %fusion.7), channel_id=1, source_target_pairs={{0,8},{4,12},{8,0},{12,4},{16,24},{20,28},{24,16},{28,20},{1,9},{5... | collective-permute-start | bytes 1572872 | tf_op jit(solution)/shard_map/ppermute | solution.py:945
  467.8 10.4 %norm_back.5 = (bf16[512,1024]{1,0:T(8,128)(2,1)S(1)}, f32[8,1024]{1,0:T(8,128)S(1)}) custom-call(s32[20]{0:T(128)S(1)} %get-tuple-element.232.perm, bf16[512,3072]{1,0:T(8,128)(2,1)S(1)} %pad_maximum_fusion.d_ref.refs_0_, bf16[4,4,128,768]{3,2,1,0:T(8,128)(2,1)S(1)} %copy-done.3, bf16[4,4,128,768]{3,2,1,0:T(8,128)(2,1)S(1)} %copy-done.22, ...), custom_call_target="tpu_custom_call" | custom-call | flops 3221225472 | bytes 16777216 | tf_op jit(solution)/shard_map/norm_back/pallas_call | solution.py:553
  484.5 10.1 %collective-permute-done.28 = bf16[4,128,256]{2,1,0:T(8,128)(2,1)S(1)} collective-permute-done((bf16[4,128,256]{2,1,0:T(8,128)(2,1)S(1)}, bf16[4,128,256]{2,1,0:T(8,128)(2,1)S(1)}, u32[]{:S(2)}, u32[]{:S(2)}) %collective-permute-start.28) | collective-permute-done | bytes 262176 | tf_op jit(solution)/shard_map/ppermute | solution.py:945
  495.4 6.0 all-to-all-start.5
  501.9 5.6 convert_add_fusion
  515.1 18.8 %collective-permute-done.21 = bf16[2,2,128,1024]{3,2,1,0:T(8,128)(2,1)S(1)} collective-permute-done((bf16[2,2,128,1024]{3,2,1,0:T(8,128)(2,1)S(1)}, bf16[2,2,128,1024]{3,2,1,0:T(8,128)(2,1)S(1)}, u32[]{:S(2)}, u32[]{:S(2)}) %collective-permute-start.21) | collective-permute-done | bytes 1048608 | tf_op jit(solution)/shard_map/ppermute | solution.py:945
  537.7 24.1 %collective-permute-done.24 = bf16[2,128,1024]{2,1,0:T(8,128)(2,1)S(1)} collective-permute-done((bf16[2,128,1024]{2,1,0:T(8,128)(2,1)S(1)}, bf16[2,128,1024]{2,1,0:T(8,128)(2,1)S(1)}, u32[]{:S(2)}, u32[]{:S(2)}) %collective-permute-start.24) | collective-permute-done | bytes 524320 | tf_op jit(solution)/shard_map/ppermute | solution.py:945
  587.5 6.4 collective-permute-done.30
  595.4 7.1 %all-to-all-done.6 = bf16[4,128,1024]{2,1,0:T(8,128)(2,1)} async-done(((bf16[4,128,1024]{2,1,0:T(8,128)(2,1)}), bf16[4,128,1024]{2,1,0:T(8,128)(2,1)}, u32[]{:S(2)}, u32[]{:S(2)}) %all-to-all-start.6) | async-done | bytes 1048608 | tf_op jit(solution)/shard_map/all_to_all | solution.py:1029
  622.5 11.4 %all-to-all-done.4 = bf16[4,128,768]{2,1,0:T(8,128)(2,1)S(1)} async-done(((bf16[4,128,768]{2,1,0:T(8,128)(2,1)}), bf16[4,128,768]{2,1,0:T(8,128)(2,1)S(1)}, u32[]{:S(2)}, u32[]{:S(2)}) %all-to-all-start.4) | async-done | bytes 786464 | tf_op jit(solution)/shard_map/all_to_all | solution.py:1029
  (434 shorter events, 273.6 us)
Async XLA Ops:
  9.8 17.0 %all-to-all-start = ((bf16[4,336,128]{2,1,0:T(8,128)(2,1)}), bf16[4,336,128]{2,1,0:T(8,128)(2,1)S(1)}, u32[]{:S(2)}, u32[]{:S(2)}) async-start(bf16[4,336,128]{2,1,0:T(8,128)(2,1)} %broadcast_in_dim.71), calls=%async_computation | async-start | bytes 688128 | tf_op jit(solution)/shard_map/all_to_all | solution.py:1029
  27.7 29.3 %all-to-all-start.1 = ((bf16[4,128,768]{2,1,0:T(8,128)(2,1)}), bf16[4,128,768]{2,1,0:T(8,128)(2,1)S(1)}, u32[]{:S(2)}, u32[]{:S(2)}) async-start(bf16[4,128,768]{2,1,0:T(8,128)(2,1)} %broadcast_in_dim.72), calls=%async_computation.1 | async-start | bytes 1572864 | tf_op jit(solution)/shard_map/all_to_all | solution.py:1029
  31.2 230.2 %all-gather.3.cloned.1.call-start = ((), (), s32[]{:S(2)}) async-start(), calls=%async_computation.15 | async-start | bytes 8650752 | tf_op jit(solution)/shard_map/all_gather | solution.py:958
  33.8 17.7 %collective-permute-start.1 = (bf16[256,576]{0,1:T(8,128)(2,1)S(1)}, bf16[256,576]{0,1:T(8,128)(2,1)}, u32[]{:S(2)}, u32[]{:S(2)}) collective-permute-start(bf16[256,576]{0,1:T(8,128)(2,1)S(1)} %get-tuple-element.208), channel_id=1, source_target_pairs={{0,2},{1,0},{2,6},{3,4},{4,3},{5,1},{6,7},{7,5},{8,10},{9,8},{10,1... | collective-permute-start | bytes 884744 | tf_op jit(solution)/shard_map/ppermute | solution.py:1121
  58.3 62.9 %all-to-all-start.2 = ((bf16[4,128,1280]{2,1,0:T(8,128)(2,1)}), bf16[4,128,1280]{2,1,0:T(8,128)(2,1)}, u32[]{:S(2)}, u32[]{:S(2)}) async-start(bf16[4,128,1280]{2,1,0:T(8,128)(2,1)} %broadcast_in_dim.76), calls=%async_computation.2 | async-start | bytes 2621440 | tf_op jit(solution)/shard_map/all_to_all | solution.py:1029
  67.3 414.8 %reduce-scatter.9.cloned.1.call-start = ((), (), s32[]{:S(2)}) async-start(), calls=%async_computation.13 | async-start | bytes 9437184 | tf_op jit(solution)/shard_map/reduce_scatter | solution.py:963
  68.9 17.2 %collective-permute-start.5 = (bf16[4,336,128]{2,1,0:T(8,128)(2,1)S(1)}, bf16[4,336,128]{2,1,0:T(8,128)(2,1)S(1)}, u32[]{:S(2)}, u32[]{:S(2)}) collective-permute-start(bf16[4,336,128]{2,1,0:T(8,128)(2,1)S(1)} %collective-permute-done.2.refs_2_), channel_id=1, source_target_pairs={{0,8},{4,12},{8,0},{12,4},{16,24},{20,28},{24,16},{28,20},{1,9},{5... | collective-permute-start | bytes 1032200 | tf_op jit(solution)/shard_map/ppermute | solution.py:945
  69.4 33.7 %collective-permute-start.3 = (bf16[4,128,768]{2,1,0:T(8,128)(2,1)S(1)}, bf16[4,128,768]{2,1,0:T(8,128)(2,1)}, u32[]{:S(2)}, u32[]{:S(2)}) collective-permute-start(bf16[4,128,768]{2,1,0:T(8,128)(2,1)S(1)} %all-to-all-done.1.refs_0_), channel_id=1, source_target_pairs={{0,8},{4,12},{8,0},{12,4},{16,24},{20,28},{24,16},{28,20},{1,9},{5... | collective-permute-start | bytes 2359304 | tf_op jit(solution)/shard_map/ppermute | solution.py:945
  88.3 23.0 %collective-permute-start.6 = (bf16[4,4,336,128]{3,2,1,0:T(8,128)(2,1)S(1)}, bf16[4,4,336,128]{3,2,1,0:T(8,128)(2,1)S(1)}, u32[]{:S(2)}, u32[]{:S(2)}) collective-permute-start(bf16[4,4,336,128]{3,2,1,0:T(8,128)(2,1)S(1)} %stack.39.w0_ref.refs_1_), channel_id=1, source_target_pairs={{0,4},{4,0},{8,12},{12,8},{16,20},{20,16},{24,28},{28,24},{1,5},{5... | collective-permute-start | bytes 4128776 | tf_op jit(solution)/shard_map/ppermute | solution.py:945
  91.5 29.7 %collective-permute-start.7 = (bf16[4,128,768]{2,1,0:T(8,128)(2,1)S(1)}, bf16[4,128,768]{2,1,0:T(8,128)(2,1)}, u32[]{:S(2)}, u32[]{:S(2)}) collective-permute-start(bf16[4,128,768]{2,1,0:T(8,128)(2,1)S(1)} %all-to-all-done.1.refs_0_), channel_id=1, source_target_pairs={{0,16},{4,20},{8,24},{12,28},{16,0},{20,4},{24,8},{28,12},{1,17},{... | collective-permute-start | bytes 2359304 | tf_op jit(solution)/shard_map/ppermute | solution.py:945
  103.1 32.7 %collective-permute-start.8 = (bf16[4,128,768]{2,1,0:T(8,128)(2,1)}, bf16[4,128,768]{2,1,0:T(8,128)(2,1)}, u32[]{:S(2)}, u32[]{:S(2)}) collective-permute-start(bf16[4,128,768]{2,1,0:T(8,128)(2,1)} %collective-permute-done.3.refs_1_), channel_id=1, source_target_pairs={{0,16},{4,20},{8,24},{12,28},{16,0},{20,4},{24,8},{28,12},{1,17},{... | collective-permute-start | bytes 2359304 | tf_op jit(solution)/shard_map/ppermute | solution.py:945
  138.5 36.2 %collective-permute-start.12 = (bf16[4,128,1280]{2,1,0:T(8,128)(2,1)}, bf16[4,128,1280]{2,1,0:T(8,128)(2,1)}, u32[]{:S(2)}, u32[]{:S(2)}) collective-permute-start(bf16[4,128,1280]{2,1,0:T(8,128)(2,1)} %all-to-all-done.2.refs_0_), channel_id=1, source_target_pairs={{0,16},{4,20},{8,24},{12,28},{16,0},{20,4},{24,8},{28,12},{1,17},{... | collective-permute-start | bytes 3932168 | tf_op jit(solution)/shard_map/ppermute | solution.py:945
  151.9 26.4 %collective-permute-start.10 = (bf16[512,2048]{1,0:T(8,128)(2,1)}, bf16[512,2048]{1,0:T(8,128)(2,1)}, u32[]{:S(2)}, u32[]{:S(2)}) collective-permute-start(bf16[512,2048]{1,0:T(8,128)(2,1)} %slice.288), channel_id=1, source_target_pairs={{0,4},{4,0},{8,12},{12,8},{16,20},{20,16},{24,28},{28,24},{1,5},{5... | collective-permute-start | bytes 6291464 | tf_op jit(solution)/shard_map/ppermute | solution.py:945
  152.0 50.3 %collective-permute-start.11 = (bf16[4,128,1280]{2,1,0:T(8,128)(2,1)}, bf16[4,128,1280]{2,1,0:T(8,128)(2,1)}, u32[]{:S(2)}, u32[]{:S(2)}) collective-permute-start(bf16[4,128,1280]{2,1,0:T(8,128)(2,1)} %all-to-all-done.2.refs_0_), channel_id=1, source_target_pairs={{0,8},{4,12},{8,0},{12,4},{16,24},{20,28},{24,16},{28,20},{1,9},{5... | collective-permute-start | bytes 3932168 | tf_op jit(solution)/shard_map/ppermute | solution.py:945
  174.8 36.7 %collective-permute-start.13 = (bf16[4,128,1280]{2,1,0:T(8,128)(2,1)}, bf16[4,128,1280]{2,1,0:T(8,128)(2,1)}, u32[]{:S(2)}, u32[]{:S(2)}) collective-permute-start(bf16[4,128,1280]{2,1,0:T(8,128)(2,1)} %collective-permute-done.12.refs_2_), channel_id=1, source_target_pairs={{0,8},{4,12},{8,0},{12,4},{16,24},{20,28},{24,16},{28,20},{1,9},{5... | collective-permute-start | bytes 3932168 | tf_op jit(solution)/shard_map/ppermute | solution.py:945
  348.1 153.2 %reduce-scatter.5.cloned.1.call-start = ((), (), s32[]{:S(2)}) async-start(), calls=%async_computation.11 | async-start | bytes 1769472 | tf_op jit(solution)/shard_map/reduce_scatter | solution.py:963
  437.5 19.0 %collective-permute-start.20 = (bf16[2,512,1024]{2,1,0:T(8,128)(2,1)}, bf16[2,512,1024]{2,1,0:T(8,128)(2,1)}, u32[]{:S(2)}, u32[]{:S(2)}) collective-permute-start(bf16[2,512,1024]{2,1,0:T(8,128)(2,1)} %get-tuple-element.137), channel_id=1, source_target_pairs={{0,4},{4,0},{8,12},{12,8},{16,20},{20,16},{24,28},{28,24},{1,5},{5... | collective-permute-start | bytes 6291464 | tf_op jit(solution)/shard_map/ppermute | solution.py:945
  438.7 133.8 %reduce-scatter.11.cloned.1.call-start = ((), (), s32[]{:S(2)}) async-start(), calls=%async_computation.14 | async-start | bytes 1310720 | tf_op jit(solution)/shard_map/reduce_scatter | solution.py:964
  438.9 63.0 %collective-permute-start.19 = (bf16[4,4,128,1024]{3,2,1,0:T(8,128)(2,1)}, bf16[4,4,128,1024]{3,2,1,0:T(8,128)(2,1)}, u32[]{:S(2)}, u32[]{:S(2)}) collective-permute-start(bf16[4,4,128,1024]{3,2,1,0:T(8,128)(2,1)} %copy-done.55), channel_id=1, source_target_pairs={{0,4},{4,0},{8,12},{12,8},{16,20},{20,16},{24,28},{28,24},{1,5},{5... | collective-permute-start | bytes 12582920 | tf_op jit(solution)/shard_map/ppermute | solution.py:945
  446.4 35.6 %collective-permute-start.25 = (bf16[2,4,128,256]{3,2,1,0:T(8,128)(2,1)S(1)}, bf16[2,4,128,256]{3,2,1,0:T(8,128)(2,1)}, u32[]{:S(2)}, u32[]{:S(2)}) collective-permute-start(bf16[2,4,128,256]{3,2,1,0:T(8,128)(2,1)S(1)} %fusion.7), channel_id=1, source_target_pairs={{0,8},{4,12},{8,0},{12,4},{16,24},{20,28},{24,16},{28,20},{1,9},{5... | collective-permute-start | bytes 1572872 | tf_op jit(solution)/shard_map/ppermute | solution.py:945
  483.6 27.3 %collective-permute-start.23 = (bf16[4,4,128,768]{3,2,1,0:T(8,128)(2,1)}, bf16[4,4,128,768]{3,2,1,0:T(8,128)(2,1)}, u32[]{:S(2)}, u32[]{:S(2)}) collective-permute-start(bf16[4,4,128,768]{3,2,1,0:T(8,128)(2,1)} %copy-done.56), channel_id=1, source_target_pairs={{0,4},{4,0},{8,12},{12,8},{16,20},{20,16},{24,28},{28,24},{1,5},{5... | collective-permute-start | bytes 9437192 | tf_op jit(solution)/shard_map/ppermute | solution.py:945
  483.8 78.2 %collective-permute-start.26 = (bf16[4,4,144,128]{3,2,1,0:T(8,128)(2,1)}, bf16[4,4,144,128]{3,2,1,0:T(8,128)(2,1)}, u32[]{:S(2)}, u32[]{:S(2)}) collective-permute-start(bf16[4,4,144,128]{3,2,1,0:T(8,128)(2,1)} %get-tuple-element.158), channel_id=1, source_target_pairs={{0,4},{4,0},{8,12},{12,8},{16,20},{20,16},{24,28},{28,24},{1,5},{5... | collective-permute-start | bytes 1769480 | tf_op jit(solution)/shard_map/ppermute | solution.py:945
  495.4 79.0 %all-to-all-start.5 = ((bf16[4,128,256]{2,1,0:T(8,128)(2,1)}), bf16[4,128,256]{2,1,0:T(8,128)(2,1)S(1)}, u32[]{:S(2)}, u32[]{:S(2)}) async-start(bf16[4,128,256]{2,1,0:T(8,128)(2,1)} %add_convert_fusion.3), calls=%async_computation.9 | async-start | bytes 524288 | tf_op jit(solution)/shard_map/all_to_all | solution.py:1029
  501.3 115.5 %reduce-scatter.7.cloned.1.call-start = ((), (), s32[]{:S(2)}) async-start(), calls=%async_computation.12 | async-start | bytes 245760 | tf_op jit(solution)/shard_map/reduce_scatter | solution.py:964
  507.7 26.1 %collective-permute-start.21 = (bf16[2,2,128,1024]{3,2,1,0:T(8,128)(2,1)S(1)}, bf16[2,2,128,1024]{3,2,1,0:T(8,128)(2,1)S(1)}, u32[]{:S(2)}, u32[]{:S(2)}) collective-permute-start(bf16[2,2,128,1024]{3,2,1,0:T(8,128)(2,1)S(1)} %slice_bitcast_fusion.10), channel_id=1, source_target_pairs={{0,8},{4,12},{8,0},{12,4},{16,24},{20,28},{24,16},{28,20},{1,9},{5... | collective-permute-start | bytes 3145736 | tf_op jit(solution)/shard_map/ppermute | solution.py:945
  509.1 26.7 %collective-permute-start.34 = (bf16[2,2,128,1024]{3,2,1,0:T(8,128)(2,1)S(1)}, bf16[2,2,128,1024]{3,2,1,0:T(8,128)(2,1)S(1)}, u32[]{:S(2)}, u32[]{:S(2)}) collective-permute-start(bf16[2,2,128,1024]{3,2,1,0:T(8,128)(2,1)S(1)} %slice_bitcast_fusion.5), channel_id=1, source_target_pairs={{0,16},{4,20},{8,24},{12,28},{16,0},{20,4},{24,8},{28,12},{1,17},{... | collective-permute-start | bytes 3145736 | tf_op jit(solution)/shard_map/ppermute | solution.py:945
  513.8 57.9 %collective-permute-start.29 = (bf16[2,2,128,768]{3,2,1,0:T(8,128)(2,1)S(1)}, bf16[2,2,128,768]{3,2,1,0:T(8,128)(2,1)S(1)}, u32[]{:S(2)}, u32[]{:S(2)}) collective-permute-start(bf16[2,2,128,768]{3,2,1,0:T(8,128)(2,1)S(1)} %slice_bitcast_fusion.14), channel_id=1, source_target_pairs={{0,8},{4,12},{8,0},{12,4},{16,24},{20,28},{24,16},{28,20},{1,9},{5... | collective-permute-start | bytes 2359304 | tf_op jit(solution)/shard_map/ppermute | solution.py:945
  514.5 66.4 %collective-permute-start.32 = (bf16[2,2,128,768]{3,2,1,0:T(8,128)(2,1)S(1)}, bf16[2,2,128,768]{3,2,1,0:T(8,128)(2,1)}, u32[]{:S(2)}, u32[]{:S(2)}) collective-permute-start(bf16[2,2,128,768]{3,2,1,0:T(8,128)(2,1)S(1)} %slice_bitcast_fusion.12), channel_id=1, source_target_pairs={{0,16},{4,20},{8,24},{12,28},{16,0},{20,4},{24,8},{28,12},{1,17},{... | collective-permute-start | bytes 2359304 | tf_op jit(solution)/shard_map/ppermute | solution.py:945
  534.2 27.6 %collective-permute-start.24 = (bf16[2,128,1024]{2,1,0:T(8,128)(2,1)S(1)}, bf16[2,128,1024]{2,1,0:T(8,128)(2,1)S(1)}, u32[]{:S(2)}, u32[]{:S(2)}) collective-permute-start(bf16[2,128,1024]{2,1,0:T(8,128)(2,1)S(1)} %fusion.6), channel_id=1, source_target_pairs={{0,16},{4,20},{8,24},{12,28},{16,0},{20,4},{24,8},{28,12},{1,17},{... | collective-permute-start | bytes 1572872 | tf_op jit(solution)/shard_map/ppermute | solution.py:945
  536.2 27.0 %collective-permute-start.35 = (bf16[2,128,1024]{2,1,0:T(8,128)(2,1)S(1)}, bf16[2,128,1024]{2,1,0:T(8,128)(2,1)S(1)}, u32[]{:S(2)}, u32[]{:S(2)}) collective-permute-start(bf16[2,128,1024]{2,1,0:T(8,128)(2,1)S(1)} %fusion.8), channel_id=1, source_target_pairs={{0,8},{4,12},{8,0},{12,4},{16,24},{20,28},{24,16},{28,20},{1,9},{5... | collective-permute-start | bytes 1572872 | tf_op jit(solution)/shard_map/ppermute | solution.py:945
  574.4 28.1 %all-to-all-start.6 = ((bf16[4,128,1024]{2,1,0:T(8,128)(2,1)}), bf16[4,128,1024]{2,1,0:T(8,128)(2,1)}, u32[]{:S(2)}, u32[]{:S(2)}) async-start(bf16[4,128,1024]{2,1,0:T(8,128)(2,1)} %pad_maximum_fusion.1), calls=%async_computation.10 | async-start | bytes 2097152 | tf_op jit(solution)/shard_map/all_to_all | solution.py:1029
  611.8 22.1 %all-to-all-start.4 = ((bf16[4,128,768]{2,1,0:T(8,128)(2,1)}), bf16[4,128,768]{2,1,0:T(8,128)(2,1)S(1)}, u32[]{:S(2)}, u32[]{:S(2)}) async-start(bf16[4,128,768]{2,1,0:T(8,128)(2,1)} %pad_maximum_fusion.3), calls=%async_computation.8 | async-start | bytes 1572864 | tf_op jit(solution)/shard_map/all_to_all | solution.py:1029
  (128 other events, 1175.6 us)
Sparse Core Ops, SparseCore 0:
  57.2 106.7 all-gather.2
  348.2 82.1 reduce-scatter.8
  438.8 55.5 reduce-scatter.4
  496.7 30.2 reduce-scatter.10
  529.1 18.5 reduce-scatter.6

commit v3 on v2

--- a/solution.py
+++ b/solution.py
@@ -30,6 +30,7 @@
 WIDE = D // BLOCKS
 VMEM_MB = 1024 * 1024
 VMEM = 28
+WIDE_VMEM = 56
 TABLE = NG + 8
 
 
@@ -144,7 +145,7 @@
         norm_store(perm, h_ref, g_ref, s_ref, n_ref, 32)
 
 
-def project(perm, a, chunk, at, res, b, g, s):
+def project(perm, a, chunk, at, res, b, g, s, grant=VMEM):
     rows, depth = a.shape
     width = D // 4
     full = lambda shape: pl.BlockSpec(shape, lambda z, p: (0, 0))
@@ -168,7 +169,7 @@
             out_specs=[full((rows, D)), full((rows, D))],
         ),
         out_shape=[jax.ShapeDtypeStruct((rows, D), F32), jax.ShapeDtypeStruct((rows, D), BF16)],
-        compiler_params=params(VMEM),
+        compiler_params=params(grant),
         cost_estimate=pl.CostEstimate(
             flops=2 * rows * D * depth,
             bytes_accessed=rows * D * 10 + 2 * D * depth + 2 * rows * depth,
@@ -442,7 +443,7 @@
             scratch_shapes=[pltpu.VMEM((rows, part), F32)],
         ),
         out_shape=[jax.ShapeDtypeStruct((rows, FF), BF16), jax.ShapeDtypeStruct((1, FF), F32)],
-        compiler_params=params(VMEM),
+        compiler_params=params(WIDE_VMEM),
         cost_estimate=pl.CostEstimate(
             flops=2 * rows * D * FF, bytes_accessed=rows * FF * 6 + 2 * D * FF, transcendentals=rows * FF
         ),
@@ -592,7 +593,7 @@
     return jnp.where(mine, keys, rest)
 
 
-def attend_kernel(perm, lens, q_ref, k0_ref, k1_ref, v0_ref, v1_ref, o_ref, l_ref):
+def attend_kernel(perm, lens, q_ref, k0_ref, k1_ref, v0_ref, v1_ref, o_ref, l_ref, f_ref):
     v0, v1 = v0_ref[...], v1_ref[...]
     sides = [lanes_of(side) for side in range(2)]
     keys = [
@@ -616,7 +617,9 @@
             outs.append((nn(e0.astype(BF16), v0) + nn(e1.astype(BF16), v1)) * (1.0 / total))
             logs.append(top + jnp.log(total))
         lane = sides[0][0]
-        o_ref[rows, :] = jnp.where(lane < HD, outs[0], outs[1]).astype(BF16)
+        mixed = jnp.where(lane < HD, outs[0], outs[1])
+        o_ref[rows, :] = mixed.astype(BF16)
+        f_ref[rows, :] = mixed
         l_ref[rows, :] = jnp.where(lane < HD, logs[1], logs[0])
 
 
@@ -632,10 +635,12 @@
             out_specs=[
                 pl.BlockSpec((rows, PAIR), lambda h, m, n: (0, m[8 + h])),
                 block(0),
+                block(0),
             ],
         ),
         out_shape=[
             jax.ShapeDtypeStruct((rows, D), BF16),
+            jax.ShapeDtypeStruct((rows, D), F32),
             jax.ShapeDtypeStruct((rows, D), F32),
         ],
         compiler_params=params(VMEM),
@@ -649,55 +654,68 @@
 
 
 def attend_back_kernel(
-    perm, lens, q_ref, k0_ref, k1_ref, v0_ref, v1_ref, do_ref, l_ref, dq_ref, own_ref, far_ref
+    perm, lens, q_ref, k0_ref, k1_ref, v0_ref, v1_ref, do_ref, l_ref, f_ref, dq_ref, own_ref, far_ref
 ):
-    values = [v0_ref[...], v1_ref[...]]
+    values = []
+    for side in range(2):
+        lane, mine, free = lanes_of(side)
+        ones = jnp.logical_and(lane >= free, lane < free + 3)
+        rest = jnp.where(ones, 1.0, 0.0).astype(BF16)
+        values.append([jnp.where(mine, ref[...], rest) for ref in (v0_ref, v1_ref)])
     q_all, do_all = q_ref[...], do_ref[...]
     sides = [lanes_of(side) for side in range(2)]
     keys = [
         [masked_keys(ref[...], where, lens[j], 3) for j, ref in enumerate((k0_ref, k1_ref))]
         for where in sides
     ]
+    turned = [[k.T for k in pair] for pair in keys]
     chunk = 256
     dk = [None, None]
     dv = [None, None]
     for i in range(q_ref.shape[0] // chunk):
         rows = slice(i * chunk, (i + 1) * chunk)
-        logs = l_ref[rows, :]
-        first = logs.astype(BF16)
-        left = logs - first.astype(F32)
-        second = left.astype(BF16)
-        third = (left - second.astype(F32)).astype(BF16)
+
+        def thirds(x):
+            first = x.astype(BF16)
+            left = x - first.astype(F32)
+            second = left.astype(BF16)
+            return first, second, (left - second.astype(F32)).astype(BF16)
+
+        logs = thirds(l_ref[rows, :])
+        flow = do_all[rows, :].astype(F32) * f_ref[rows, :]
         dqs = []
-        for (lane, mine, free), (k0, k1) in zip(sides, keys):
+        for (lane, mine, free), (k0, k1), vs, across in zip(sides, keys, values, turned):
             qm = jnp.where(mine, q_all[rows, :], 0.0).astype(BF16)
             dom = jnp.where(mine, do_all[rows, :], 0.0).astype(BF16)
             rest = jnp.where(lane == free, 1.0, 0.0).astype(BF16)
-            for at, part in enumerate((first, second, third)):
+            for at, part in enumerate(logs):
                 rest = jnp.where(lane == free + 1 + at, -part, rest)
             qs = jnp.where(mine, (q_all[rows, :] * SCALE).astype(BF16), rest)
             probs = [jnp.exp(nt(k, qs)) for k in (k0, k1)]
-            da = [nt(v, dom) for v in values]
-            delta = jnp.sum(probs[0] * da[0] + probs[1] * da[1], axis=0, keepdims=True)
+            delta = jnp.sum(jnp.where(mine, flow, 0.0), axis=1, keepdims=True)
+            less = dom
+            for at, part in enumerate(thirds(delta)):
+                less = jnp.where(lane == free + at, -part, less)
+            da = [nt(v, less) for v in vs]
             dq = None
-            for j, k in enumerate((k0, k1)):
-                ds = (probs[j] * (da[j] - delta)).astype(BF16)
-                term = tn(ds, k)
+            for j in range(2):
+                ds = (probs[j] * da[j]).astype(BF16)
+                term = nn(across[j], ds)
                 dq = term if dq is None else dq + term
                 term = nn(ds, qm)
                 dk[j] = term if dk[j] is None else dk[j] + term
                 term = nn(probs[j].astype(BF16), dom)
                 dv[j] = term if dv[j] is None else dv[j] + term
             dqs.append(dq)
-        lane = sides[0][0]
-        dq_ref[rows, :] = (jnp.where(lane < HD, dqs[0], dqs[1]) * SCALE).astype(BF16)
+        dq = jnp.concatenate([dqs[0][:HD], dqs[1][HD:]], axis=0) * SCALE
+        dq_ref[rows, :] = dq.T.astype(BF16)
     own_ref[0] = dk[0] * SCALE
     own_ref[1] = dv[0]
     far_ref[0] = (dk[1] * SCALE).astype(BF16)
     far_ref[1] = dv[1].astype(BF16)
 
 
-def attend_back(perm, lens, p, kv, do, logs):
+def attend_back(perm, lens, p, kv, do, logs, flat):
     rows = p.shape[0]
     block = lambda first: pl.BlockSpec((rows, PAIR), lambda h, m, n: (0, first + h))
     both = pl.BlockSpec((2, rows, PAIR), lambda h, m, n: (0, 0, h))
@@ -714,6 +732,7 @@
                 block(PAIRS),
                 pl.BlockSpec((rows, PAIR), lambda h, m, n: (0, m[8 + h])),
                 block(0),
+                block(0),
             ],
             out_specs=[block(0), both, both],
         ),
@@ -729,7 +748,7 @@
             transcendentals=2 * rows * rows * HEADS,
         ),
         name="attend_back",
-    )(perm, lens, p, p, kv, p, kv, do, logs)
+    )(perm, lens, p, p, kv, p, kv, do, logs, flat)
 
 
 def iota(shape, dim):
@@ -945,7 +964,17 @@
     return lax.ppermute(x, axis, flip_pairs(lax.axis_size(axis), bit))
 
 
+CORE, XBIT, YBIT = 1, 2, 4
+PLACES = np.array([0, 2, 4, 6, 1, 3, 5, 7], np.int32)
+
+
 def total_sum(x):
+    if lax.axis_size("scene") == BLOCKS and lax.axis_size("rows") == 4:
+        x = x + swap(x, "scene", CORE)
+        near, far, both = (swap(x, "scene", bit) for bit in (XBIT, YBIT, XBIT | YBIT))
+        x = (x + near) + (far + both)
+        near, far, both = (swap(x, "rows", bit) for bit in (1, 2, 3))
+        return (x + near) + (far + both)
     for axis in ("scene", "rows"):
         bit = 1
         while bit < lax.axis_size(axis):
@@ -957,11 +986,6 @@
 def gather_whole(shard):
     whole = lax.all_gather(shard, ("scene", "rows"), axis=0)
     return (whole.reshape((BLOCKS, 4) + shard.shape),) * 2
-
-
-def scatter_whole(grad):
-    part = lax.psum_scatter(grad[0], "scene", scatter_dimension=0)
-    return lax.psum_scatter(part, "rows", scatter_dimension=0).astype(F32)
 
 
 def gather_plain(shards, turned):
@@ -990,39 +1014,44 @@
     return lax.psum_scatter(part, "rows", scatter_dimension=1 - turned, tiled=True).astype(F32)
 
 
-CORE, XBIT, YBIT = 1, 2, 4
-PLACES = np.array([0, 2, 4, 6, 1, 3, 5, 7], np.int32)
-
-
 def stack_kernel(*refs):
-    *parts, out_ref = refs
-    for i, ref in enumerate(parts):
+    own, x, y, *both, out_ref = refs
+    for i, ref in enumerate((own, x, y)):
         out_ref[i] = ref[...]
-
-
-def stack(parts):
+    if len(both) == 1:
+        out_ref[3] = both[0][...]
+    else:
+        early = pl.program_id(0) < 2
+        for ref, now in zip(both, (early, jnp.logical_not(early))):
+
+            @pl.when(now)
+            def _(ref=ref):
+                out_ref[3] = ref[...]
+
+
+def stack(parts, both):
+    both = both if isinstance(both, list) else [both]
     shape = parts[0].shape
-    lead = shape[:-2]
-    steps = lead[0] if lead else 1
-    block = (1,) * len(lead) + shape[-2:]
-    rest = (0,) * (len(shape) - 1) if lead else (0, 0)
-    place = lambda i: ((i,) + rest) if lead else rest
+    block = (1,) + shape[1:]
+    places = [lambda i: (i, 0, 0)] * 4
+    if len(both) == 2:
+        places[3:] = [lambda i: (jnp.minimum(i, 1), 0, 0), lambda i: (jnp.maximum(i - 2, 0), 0, 0)]
     return pl.pallas_call(
         stack_kernel,
-        grid=(steps,),
-        in_specs=[pl.BlockSpec(block, place)] * len(parts),
-        out_specs=pl.BlockSpec((len(parts),) + block, lambda i: (0,) + place(i)),
-        out_shape=jax.ShapeDtypeStruct((len(parts),) + shape, parts[0].dtype),
+        grid=(4,),
+        in_specs=[pl.BlockSpec(block, place) for place in places],
+        out_specs=pl.BlockSpec((4,) + block, lambda i: (0, i, 0, 0)),
+        out_shape=jax.ShapeDtypeStruct((4,) + shape, parts[0].dtype),
         compiler_params=params(VMEM),
         cost_estimate=pl.CostEstimate(
-            flops=0, bytes_accessed=4 * len(parts) * parts[0].size, transcendentals=0
+            flops=0, bytes_accessed=16 * parts[0].size, transcendentals=0
         ),
         name="stack",
-    )(*parts)
-
-
-def tie(x, *earlier):
-    return lax.optimization_barrier((x,) + earlier)[0]
+    )(*parts, *both)
+
+
+def together(*arrays):
+    return lax.optimization_barrier(arrays)
 
 
 def share_rows(x):
@@ -1034,28 +1063,26 @@
         self.shard = shard
         self.first, self.second = (XBIT, YBIT) if order == "xy" else (YBIT, XBIT)
 
-    def rows(self, *earlier):
-        shard = tie(self.shard, *earlier)
-        self.own = share_rows(jnp.broadcast_to(shard[None], (4,) + shard.shape))
-
-    def near(self, *earlier):
-        self.own = tie(self.own, *earlier)
+    def rows(self):
+        self.own = share_rows(jnp.broadcast_to(self.shard[None], (4,) + self.shard.shape))
+
+    def near(self):
         self.one = swap(self.own, "scene", self.first)
         self.two = swap(self.own, "scene", self.second)
-        return self.own
-
-    def cross(self, *earlier):
-        self.one = tie(self.one, *earlier)
+
+    def cross(self):
         self.both = swap(self.one, "scene", self.second)
-        return self.one
-
-    def core(self, *earlier):
+
+    def cross_halves(self):
+        self.both = [
+            swap(self.one[:2], "scene", self.second),
+            swap(self.two[2:], "scene", self.first),
+        ]
+
+    def get(self):
         x, y = (self.one, self.two) if self.first == XBIT else (self.two, self.one)
-        self.half = stack([tie(self.own, *earlier), x, y, self.both])
-        return self.half
-
-    def get(self):
-        return self.half, swap(self.half, "scene", CORE)
+        half = stack([self.own, x, y], self.both)
+        return half, swap(half, "scene", CORE)
 
 
 class Scatter:
@@ -1064,39 +1091,57 @@
         self.streams = streams
         self.got = swap(send, "scene", CORE)
 
-    def near(self, *earlier):
-        keep = tie(self.keep, *earlier)
-        shape = (2, 2) + keep.shape[1:]
-        total = keep.reshape(shape).astype(F32) + self.got.reshape(shape).astype(F32)
+    def near(self):
+        shape = (2, 2) + self.keep.shape[1:]
+        keep, got = self.keep.reshape(shape), self.got.reshape(shape)
         count = 4 // len(self.streams)
-        self.sums, self.moved = [], []
+        self.sums, self.away = [], []
         for i, order in enumerate(self.streams):
-            part = total[:, :, i * count : (i + 1) * count]
-            if order == "xy":
-                near, far, bit = part[:, 0], part[:, 1], XBIT
-            else:
-                near, far, bit = part[0], part[1], YBIT
-            self.sums.append(near)
-            self.moved.append(swap(far.astype(BF16), "scene", bit))
-        return self.moved[0]
-
-    def cross(self, *earlier):
-        for i, order in enumerate(self.streams):
-            near = self.sums[i] + tie(self.moved[i], *earlier).astype(F32)
-            self.sums[i] = near[0]
-            self.moved[i] = swap(near[1].astype(BF16), "scene", YBIT if order == "xy" else XBIT)
-        return self.moved[0]
-
-    def rows(self, *earlier):
+            zs = slice(i * count, (i + 1) * count)
+
+            def part(place):
+                pick = (slice(None), place, zs) if order == "xy" else (place, slice(None), zs)
+                return keep[pick].astype(F32) + got[pick].astype(F32)
+
+            self.sums.append(part(0))
+            self.away.append(part(1).astype(BF16))
+
+    def send(self, step):
+        bits = {"xy": (XBIT, YBIT), "yx": (YBIT, XBIT)}
+        self.moved = [
+            swap(away, "scene", bits[order][step])
+            for away, order in zip(self.away, self.streams)
+        ]
+
+    def cross(self):
+        whole = [near + moved.astype(F32) for near, moved in zip(self.sums, self.moved)]
+        self.sums = [part[0] for part in whole]
+        self.away = [part[1].astype(BF16) for part in whole]
+
+    def last(self):
         mine = [
-            (near + tie(moved, *earlier).astype(F32)).astype(BF16)
-            for near, moved in zip(self.sums, self.moved)
+            (near + moved.astype(F32)).astype(BF16) for near, moved in zip(self.sums, self.moved)
         ]
-        self.sums = share_rows(mine[0] if len(mine) == 1 else jnp.concatenate(mine, axis=0))
-        return mine[0]
-
-    def get(self, *earlier):
-        return jnp.sum(tie(self.sums, *earlier).astype(F32), axis=0)
+        self.away = [mine[0] if len(mine) == 1 else jnp.concatenate(mine, axis=0)]
+
+    def rows(self):
+        self.total = share_rows(self.away[0])
+
+    def rows_apart(self):
+        z = lax.axis_index("rows")
+        block = lambda k: lax.dynamic_index_in_dim(self.away[0], z ^ k, 0, keepdims=False)
+        self.total = jnp.stack([block(0)] + [swap(block(k), "rows", k) for k in (1, 2, 3)])
+
+    def get(self):
+        return jnp.sum(self.total.astype(F32), axis=0)
+
+
+def settle(scatters, *arrays):
+    flat = [a for t in scatters for a in t.away]
+    out = list(together(*flat, *arrays))
+    for t in scatters:
+        t.away = [out.pop(0) for _ in t.away]
+    return out[0] if len(out) == 1 else out
 
 
 def weight_step(grad, factor, moment, master, average):
@@ -1106,7 +1151,7 @@
     return moment_new, weight_new, AVERAGE_DECAY * average + (1.0 - AVERAGE_DECAY) * weight_new
 
 
-def to_items(x):
+def items_sent(x):
     scenes, rows = lax.axis_size("scene"), lax.axis_size("rows")
     z = lax.axis_index("rows")
     pairs = [[], []]
@@ -1119,7 +1164,12 @@
     even = z % 2 == 0
     first = lax.ppermute(jnp.where(even, x[0], x[1]), ("scene", "rows"), pairs[0])
     second = lax.ppermute(jnp.where(even, x[1], x[0]), ("scene", "rows"), pairs[1])
-    early = z // 2 == 0
+    return first, second
+
+
+def items_placed(parts):
+    first, second = parts
+    early = lax.axis_index("rows") // 2 == 0
     return jnp.stack([jnp.where(early, first, second), jnp.where(early, second, first)])
 
 
@@ -1164,45 +1214,53 @@
         first_w = Gather(low[1], "xy")
         second_w = Gather(jnp.concatenate([low[3], low[2]], axis=1), "yx")
         side_w.rows()
-        x = to_items(x_in)
-        first_w.rows(side_w.own)
-        own = side_w.near()
-        one = side_w.cross(own, x)
-        own = first_w.near(one)
-        second_w.rows(own)
-        w_third = gather_whole(tie(low[4], own))
-        half = side_w.core(own)
+        side_w.own, first_w.shard = together(side_w.own, first_w.shard)
+        first_w.rows()
+        side_w.near()
+        first_w.own, side_w.one, side_w.two, x_in = together(
+            first_w.own, side_w.one, side_w.two, x_in
+        )
+        first_w.near()
+        side_w.cross()
+        x = items_sent(x_in)
+        second_w.shard, *x = together(second_w.shard, *x)
+        second_w.rows()
+        first_w.one, first_w.two, side_w.both = together(
+            first_w.one, first_w.two, side_w.both
+        )
+        first_w.cross()
         w_side = side_w.get()
-        one = first_w.cross(half)
-        x = tie(x, one)
+        x = items_placed(x)
     else:
         w_side = gather_plain([low[0], low[5]], True)
         w_first = gather_plain([low[1]], False)
         w_second = gather_plain([low[3], low[2]], False)
         w_third = gather_plain([low[4]], False)
     if not placed:
-        x = to_items(x_in)
+        x = items_placed(items_sent(x_in))
     x = x.reshape(tokens, -1)
     h0, a1 = embed(perm, x, w_side, gains[6], gains[0], gains[3])
     if placed:
-        own = second_w.near(a1)
-        first_w.core(own)
+        second_w.own, a1, first_w.both, shard = together(second_w.own, a1, first_w.both, low[4])
+        second_w.near()
+        w_third = gather_whole(shard)
         w_first = first_w.get()
     p = joint(perm, a1, w_first)
     kv = swap(p[:, D:], "scene", 1)
-    if placed:
-        second_w.cross(p)
-        drawn = tie(drawn, second_w.one)
-    mixed, logs = attend(perm, lens, p, kv)
-    if placed:
-        second_w.core(mixed)
+    mixed, logs, flat = attend(perm, lens, p, kv)
+    if placed:
+        mixed, logs, second_w.one, second_w.two = together(
+            mixed, logs, second_w.one, second_w.two
+        )
+        second_w.cross_halves()
         w_second = second_w.get()
-    rd = to_items(drawn)
+    rd = items_sent(drawn)
     h1, a2 = project(perm, mixed, w_second, 4, h0, gains[7], gains[1], gains[4])
     u, act = up_project(plain, a2, w_second, bias_up)
-    h2, a3 = project(perm, act, w_third, 0, h1, gains[8], gains[2], gains[5])
+    h2, a3 = project(perm, act, w_third, 0, h1, gains[8], gains[2], gains[5], WIDE_VMEM)
     zt = gauss(perm, a3, w_side, bias_gauss)
-    rd = tie(rd, zt)
+    zt, *rd = together(zt, *rd)
+    rd = items_placed(rd)
 
     edge = swap(jnp.where(side == 0, zt[:, tokens - HT :], zt[:, :HT]), "scene", 1)
     before = jnp.where(side == 0, 0.0, edge)
@@ -1222,61 +1280,96 @@
     dz = dzt.astype(BF16)
 
     streams = ("xy", "yx")
-    dw_gauss = side_grad(perm, dz, a3, placed)
-    if placed:
-        r_gauss = scatter_whole(dw_gauss)
-        dz = tie(dz, dw_gauss[0])
+    dw_gauss = side_grad(perm, dz, a3)
+    if placed:
+        sg = Scatter(dw_gauss, ("yx",))
+        sg.keep, dz = together(sg.keep, dz)
     dh2, dh2_low, sums3 = norm_back(perm, dz, w_side, True, h2, gains[2], None, False)
     dw_down = weight_grad(plain, act, dh2_low, placed)
     d_low = dh2_low
     if placed:
-        r_down = scatter_whole(dw_down)
-        d_low = tie(dh2_low, dw_down[0])
+        whole_down, d_low = together(dw_down[0], d_low)
+        part_down = lax.psum_scatter(whole_down, "scene", scatter_dimension=0)
+        sg.near()
+        d_low = settle([sg], d_low)
+        sg.send(0)
     du, d_bias_up = down_back(plain, d_low, w_third, u)
+    if placed:
+        du, *sg.moved = together(du, *sg.moved)
+        sg.cross()
+        du = settle([sg], du)
+        sg.send(1)
     dw_up = weight_grad(perm, a2, du)
     if placed:
         su = Scatter(dw_up, streams)
-        du = tie(du, dw_up[0])
+        su.keep, du = together(su.keep, du)
     dh1, dh1_low, sums2 = norm_back(perm, du, w_second, False, h1, gains[1], dh2, False)
-    d_low = dh1_low
-    if placed:
-        su.near(dh1_low)
-        d_low = tie(dh1_low, su.sums[0])
-    dw_out = weight_grad(perm, mixed, d_low)
+    if placed:
+        dh1_low, su.got, *sg.moved = together(dh1_low, su.got, *sg.moved)
+        su.near()
+        sg.last()
+        dh1_low = settle([su, sg], dh1_low)
+        su.send(0)
+        sg.rows()
+    dw_out = weight_grad(perm, mixed, dh1_low)
     if placed:
         so = Scatter(dw_out, ("xy",))
-        d_low = tie(dh1_low, dw_out[0])
-    do = out_back(perm, d_low, w_second)
-    dq, own, far = attend_back(perm, lens, p, kv, do, logs)
+        so.keep, dh1_low = together(so.keep, dh1_low)
+    do = out_back(perm, dh1_low, w_second)
+    dq, own, far = attend_back(perm, lens, p, kv, do, logs, flat)
+    if placed:
+        dq, own, far, so.got, sg.total, part_down, *su.moved = together(
+            dq, own, far, so.got, sg.total, part_down, *su.moved
+        )
+        r_down = lax.psum_scatter(part_down, "rows", scatter_dimension=0)
     got = swap(far, "scene", 1)
     if placed:
-        su.cross(dq)
-        so.near(su.sums[0])
-        got = tie(got, so.sums[0])
+        su.cross()
+        so.near()
+        got = settle([su, so], got)
+        su.send(1)
+        so.send(0)
     dkv = (own + got.astype(F32)).astype(BF16)
     dp = jnp.concatenate([dq, dkv[0], dkv[1]], axis=1)
     dw_joint = weight_grad(perm, a1, dp)
-    dp_last = dp
     if placed:
         sj = Scatter(dw_joint, streams)
-        dp_last = tie(dp, dw_joint[0])
-    dh0_low, sums1 = norm_back(perm, dp_last, w_first, False, h0, gains[0], dh1, True)
-    d_low = dh0_low
-    if placed:
-        sj.near(dh0_low)
-        d_low = tie(dh0_low, sj.sums[0])
-    dw_patch = side_grad(perm, x.T, d_low)
+        sj.keep, dp, *su.moved = together(sj.keep, dp, *su.moved)
+        su.last()
+        dp = settle([su], dp)
+        su.rows()
+    dh0_low, sums1 = norm_back(perm, dp, w_first, False, h0, gains[0], dh1, True)
+    if placed:
+        dh0_low, sj.got, su.total, r_down, *so.moved = together(
+            dh0_low, sj.got, su.total, r_down, *so.moved
+        )
+        r_down = r_down.astype(F32)
+        sj.near()
+        so.cross()
+        dh0_low = settle([sj, so], dh0_low)
+        sj.send(0)
+        so.send(1)
+    dw_patch = side_grad(perm, x.T, dh0_low)
     if placed:
         sp = Scatter(dw_patch, ("yx",))
-        so.cross(dw_patch[0], r_gauss)
-        moved = su.rows(so.sums[0])
-        sp.near(moved)
-        sj.cross(sp.sums[0], r_down)
-        moved = so.rows(sj.sums[0])
-        sp.cross(moved)
-        moved = sj.rows(sp.sums[0])
-        sp.rows(moved)
-        reduced = [t.get() for t in (sp, sj, so, su)] + [r_down, r_gauss]
+        sp.keep, *moved = together(sp.keep, *sj.moved, *so.moved)
+        sj.moved, so.moved = moved[:2], moved[2:]
+        so.last()
+        sj.cross()
+        settle([sj])
+        sj.send(1)
+        sp.near()
+        sp.send(0)
+        sj.last()
+        wide = sj.away[0].shape[-1]
+        sj.away = [jnp.concatenate([sj.away[0], so.away[0]], axis=-1)]
+        sj.rows()
+        sj.total, so.total = sj.total[..., :wide], sj.total[..., wide:]
+        sp.cross()
+        sp.send(1)
+        sp.last()
+        sp.rows_apart()
+        reduced = [t.get() for t in (sp, sj, so, su)] + [r_down, sg.get()]
     else:
         grads = [dw_patch, dw_joint, dw_out, dw_up, dw_down, dw_gauss]
         reduced = [scatter_plain(g, i in (0, 5)) for i, g in enumerate(grads)]

time: 690 us -> 616 us (0.89)
  waiting for transfers between devices: 217 us -> 161 us
  Pallas kernels: 211 us -> 195 us
    ppermute x37 -> x46, waiting for transfers between devices: 164 us -> 126 us  [swap(): return lax.ppermute(x, axis, flip_pairs(lax.axis_size(axis), bit))]
    pallas_call x1, Pallas kernels: 30.3 us -> 12.4 us  [render(): pl.pallas_call(render_kernel, in_specs=[smem, smem, whole(zt), whole(zx),...]
    ppermute x37 -> x46, starting transfers between devices: 51 us -> 64.6 us  [swap(): return lax.ppermute(x, axis, flip_pairs(lax.axis_size(axis), bit))]
    add x15 -> x8, other arithmetic: 19.3 us -> 9.11 us  [the longest x5 9.07 us: cross(): near + moved.astype(F32)]
    all_to_all x7 -> x6, waiting for transfers between devices: 35.5 us -> 26.2 us  [share_rows(): return lax.all_to_all(x, 'rows', 0, 0)]
    ppermute x4, waiting for transfers between devices: 17.2 us -> 8.61 us  [the longest x2 8.6 us: items_sent(): lax.ppermute(jnp.where(even, x[1], x[0]), ('scene', 'rows'), pairs[1])]
    convert_element_type x6 -> x14, other arithmetic: 2.98 us -> 11.4 us  [the longest x7 8.84 us: near(): self.away.append(part(1).astype(BF16))]
    pallas_call x1, Pallas kernels: 35.4 us -> 28.1 us  [attend_back(): pl.pallas_call(attend_back_kernel, grid_spec=pltpu.PrefetchScalarGridSpec...]
  transfers between devices with their start and end apart: 53 -> 59, of which waited for: 28 -> 28; matrix products, arithmetic and copies ran while one was open for 8% -> 8% of each run, Pallas kernels for 22% -> 26%
where the time goes in v3:
time: 616 us; the launch traced here: 606 us
  Pallas kernels  195 us (32%)
  waiting for transfers between devices  161 us (26%)
  starting transfers between devices  103 us (17%)
  local copies, waits for them, and re-layouts  68.9 us (11%)
  other arithmetic  52.9 us (9%)
  between operations  25.1 us (4%)
    ppermute x46, waiting for transfers between devices, swap(): return lax.ppermute(x, axis, flip_pairs(lax.axis_size(axis), bit))  126 us
    ppermute x46, starting transfers between devices, swap(): return lax.ppermute(x, axis, flip_pairs(lax.axis_size(axis), bit))  64.6 us
    unnamed x236, local copies, waits for them, and re-layouts  51 us
    all_to_all x6, starting transfers between devices, share_rows(): return lax.all_to_all(x, 'rows', 0, 0)  31 us
    pallas_call x3, Pallas kernels, norm_back(): pl.pallas_call(functools.partial(back_kernel, res is not None, placed, tu...  30.2 us
    pallas_call x1, Pallas kernels, attend_back(): pl.pallas_call(attend_back_kernel, grid_spec=pltpu.PrefetchScalarGridSpec...  28.1 us
    all_to_all x6, waiting for transfers between devices, share_rows(): return lax.all_to_all(x, 'rows', 0, 0)  26.2 us
    pallas_call x4, Pallas kernels, weight_grad(): pl.pallas_call(grad_kernel, grid_spec=pltpu.PrefetchScalarGridSpec(num_sc...  23.9 us
  transfers between devices with their start and end apart: 59, of which 28 were waited for; matrix products, arithmetic and copies ran while one was open for 8% of the time, Pallas kernels for 26%

profile of v3, /device:TPU:0, one launch (start us, length us, event | category | flops | bytes accessed | tf_op | source)
XLA Modules:
  0.0 605.9 jit_solution(7452389146189317181)
XLA Ops:
  9.8 6.3 %all-to-all-start = ((bf16[4,336,128]{2,1,0:T(8,128)(2,1)}), bf16[4,336,128]{2,1,0:T(8,128)(2,1)S(1)}, u32[]{:S(2)}, u32[]{:S(2)}) async-start(bf16[4,336,128]{2,1,0:T(8,128)(2,1)} %broadcast_in_dim.71), calls=%async_computation | async-start | bytes 688128 | tf_op jit(solution)/shard_map/all_to_all | solution.py:1058
  17.2 9.6 %all-to-all-done.refs_0_ = bf16[4,336,128]{2,1,0:T(8,128)(2,1)S(1)} async-done(((bf16[4,336,128]{2,1,0:T(8,128)(2,1)}), bf16[4,336,128]{2,1,0:T(8,128)(2,1)S(1)}, u32[]{:S(2)}, u32[]{:S(2)}) %all-to-all-start) | async-done | bytes 344096 | tf_op jit(solution)/shard_map/all_to_all | solution.py:1058
  40.3 9.3 %all-to-all-done.1.refs_0_ = bf16[4,128,768]{2,1,0:T(8,128)(2,1)S(1)} async-done(((bf16[4,128,768]{2,1,0:T(8,128)(2,1)}), bf16[4,128,768]{2,1,0:T(8,128)(2,1)S(1)}, u32[]{:S(2)}, u32[]{:S(2)}) %all-to-all-start.1) | async-done | bytes 786464 | tf_op jit(solution)/shard_map/all_to_all | solution.py:1058
  55.3 8.6 %collective-permute-done.3 = bf16[256,576]{0,1:T(8,128)(2,1)} collective-permute-done((bf16[256,576]{0,1:T(8,128)(2,1)S(1)}, bf16[256,576]{0,1:T(8,128)(2,1)}, u32[]{:S(2)}, u32[]{:S(2)}) %collective-permute-start.3) | collective-permute-done | bytes 294944 | tf_op jit(solution)/shard_map/ppermute | solution.py:1166
  65.1 6.4 %all-to-all-start.2 = ((bf16[4,128,1280]{2,1,0:T(8,128)(2,1)}), bf16[4,128,1280]{2,1,0:T(8,128)(2,1)}, u32[]{:S(2)}, u32[]{:S(2)}) async-start(bf16[4,128,1280]{2,1,0:T(8,128)(2,1)} %broadcast_in_dim.73), calls=%async_computation.2 | async-start | bytes 2621440 | tf_op jit(solution)/shard_map/all_to_all | solution.py:1058
  73.0 8.5 %collective-permute-done.6.refs_3_ = bf16[4,336,128]{2,1,0:T(8,128)(2,1)S(1)} collective-permute-done((bf16[4,336,128]{2,1,0:T(8,128)(2,1)S(1)}, bf16[4,336,128]{2,1,0:T(8,128)(2,1)S(1)}, u32[]{:S(2)}, u32[]{:S(2)}) %collective-permute-start.6) | collective-permute-done | bytes 344096 | tf_op jit(solution)/shard_map/ppermute | solution.py:964
  106.9 5.6 collective-permute-done.9.w1_ref.refs_2_
  112.6 5.2 joint.1.q_ref.k0_ref.v0_ref
  126.5 20.2 %attend.1 = (bf16[512,1024]{1,0:T(8,128)(2,1)S(1)}, f32[512,1024]{1,0:T(8,128)S(1)}, f32[512,1024]{1,0:T(8,128)S(1)}) custom-call(s32[20]{0:T(128)S(1)} %get-tuple-element.318.perm, s32[2]{0:T(128)S(1)} %pad_add_fusion.lens, bf16[512,3072]{1,0:T(8,128)(2,1)S(1)} %copy-done.32, bf16[512,3072]{1,0:T(8,128)(2,1)S(1)} %copy-done.32, ...), custom_call_target="tpu_custom_call" | custom-call | flops 2147483648 | bytes 6291456 | tf_op jit(solution)/shard_map/attend/pallas_call | solution.py:629
  149.0 10.3 %collective-permute-done.12.refs_1_ = bf16[4,128,1280]{2,1,0:T(8,128)(2,1)} collective-permute-done((bf16[4,128,1280]{2,1,0:T(8,128)(2,1)}, bf16[4,128,1280]{2,1,0:T(8,128)(2,1)}, u32[]{:S(2)}, u32[]{:S(2)}) %collective-permute-start.12) | collective-permute-done | bytes 1310752 | tf_op jit(solution)/shard_map/ppermute | solution.py:964
  164.1 24.3 %collective-permute-done.13.refs_3_ = bf16[2,128,1280]{2,1,0:T(8,128)(2,1)S(1)} collective-permute-done((bf16[2,128,1280]{2,1,0:T(8,128)(2,1)S(1)}, bf16[2,128,1280]{2,1,0:T(8,128)(2,1)S(1)}, u32[]{:S(2)}, u32[]{:S(2)}) %collective-permute-start.13) | collective-permute-done | bytes 655392 | tf_op jit(solution)/shard_map/ppermute | solution.py:964
  207.3 7.3 %project_norm.2 = (f32[512,1024]{1,0:T(8,128)S(1)}, bf16[512,1024]{1,0:T(8,128)(2,1)S(1)}) custom-call(s32[20]{0:T(128)S(1)} %get-tuple-element.318.perm, bf16[512,1024]{1,0:T(8,128)(2,1)S(1)} %copy-done.37, bf16[4,4,128,1280]{3,2,1,0:T(8,128)(2,1)} %stack.58.w0_ref.refs_1_, bf16[4,4,128,1280]{3,2,1,0:T(8,128)(2,1)} %collective-permute-done.15.w1_ref.refs_2_, ...), custom_call_target="tpu_custom_call" | custom-call | flops 1073741824 | bytes 8388608 | tf_op jit(solution)/shard_map/project_norm/pallas_call | solution.py:156
  216.0 10.9 %up_gelu.1 = (f32[512,4096]{1,0:T(8,128)S(1)}, bf16[512,4096]{1,0:T(8,128)(2,1)S(1)}) custom-call(s32[20]{0:T(128)S(1)} %copy-done.55, bf16[512,1024]{1,0:T(8,128)(2,1)S(1)} %get-tuple-element.160.a_ref, bf16[4,4,128,1280]{3,2,1,0:T(8,128)(2,1)} %stack.58.w0_ref.refs_1_, bf16[4,4,128,1280]{3,2,1,0:T(8,128)(2,1)} %collective-permute-done.15.w1_ref.refs_2_, ...), custom_call_target="tpu_custom_call" | custom-call | flops 4294967296 | bytes 20971520 | tf_op jit(solution)/shard_map/up_gelu/pallas_call | solution.py:375
  233.4 14.4 %project_norm.3 = (f32[512,1024]{1,0:T(8,128)}, bf16[512,1024]{1,0:T(8,128)(2,1)}) custom-call(s32[20]{0:T(128)} %copy-done.48, bf16[512,4096]{1,0:T(8,128)(2,1)} %copy-done.13, bf16[8,4,512,256]{3,2,1,0:T(8,128)(2,1)} %bitcast.256, bf16[8,4,512,256]{3,2,1,0:T(8,128)(2,1)} %bitcast.257, f32[512,1024]{1,0:T(8,128)} %copy-done.4, f32[1,1024]{1,0:T(1,128)} %bitcast.275, ...), custom_call_target="tpu_custom_call" | custom-call | flops 4294967296 | bytes 17825792 | tf_op jit(solution)/shard_map/project_norm/pallas_call | solution.py:156
  254.6 12.4 %render.1 = (f32[768,512]{1,0:T(8,128)S(1)}, f32[768,128]{1,0:T(8,128)S(1)}, f32[8,128]{1,0:T(8,128)S(1)}) custom-call(s32[1]{0:T(128)} %bitcast.15.views_ref, f32[1]{0:T(128)} %bitcast.16.inv_ref, f32[768,512]{1,0:T(8,128)S(1)} %gauss.1.z_ref, f32[768,128]{1,0:T(8,128)S(1)} %maximum_maximum_fusion.zx_ref, f32[2,12,19,256]{3,2,1,0:T(8,128)S(1)} %pad_maximum_fusion.4.rd_ref, ...), custom_call_target="tpu_custom_call" | custom-call | flops 21743271936 | bytes 4194304 | tf_op jit(solution)/shard_map/render/pallas_call | solution.py:935
  274.1 6.2 %norm_back.3 = (f32[512,1024]{1,0:T(8,128)S(1)}, bf16[512,1024]{1,0:T(8,128)(2,1)S(1)}, f32[8,1024]{1,0:T(8,128)S(1)}) custom-call(s32[20]{0:T(128)S(1)} %copy-done.49, bf16[768,512]{1,0:T(8,128)(2,1)S(1)} %pad_maximum_fusion.3.d_ref.refs_0_, bf16[4,4,336,128]{3,2,1,0:T(8,128)(2,1)S(1)} %stack.56.w0_ref.refs_1_, ...), custom_call_target="tpu_custom_call" | custom-call | flops 805306368 | bytes 9699328 | tf_op jit(solution)/shard_map/norm_back/pallas_call | solution.py:554
  282.3 7.9 %weight_grad.4 = bf16[8,4,512,256]{3,2,1,0:T(8,128)(2,1)S(1)} custom-call(s32[20]{0:T(128)S(1)} %copy-done.56, bf16[512,4096]{1,0:T(8,128)(2,1)S(1)} %copy-done.14, bf16[512,1024]{1,0:T(8,128)(2,1)S(1)} %get-tuple-element.177.d_ref), custom_call_target="tpu_custom_call" | custom-call | flops 4294967296 | bytes 13631488 | tf_op jit(solution)/shard_map/weight_grad/pallas_call | solution.py:305
  298.0 25.0 %collective-permute-start.21 = (bf16[2,4,192,128]{3,2,1,0:T(8,128)(2,1)S(1)}, bf16[2,4,192,128]{3,2,1,0:T(8,128)(2,1)S(1)}, u32[]{:S(2)}, u32[]{:S(2)}) collective-permute-start(bf16[2,4,192,128]{3,2,1,0:T(8,128)(2,1)S(1)} %add_convert_fusion.6), channel_id=1, source_target_pairs={{0,16},{4,20},{8,24},{12,28},{16,0},{20,4},{24,8},{28,12},{1,17},{... | collective-permute-start | bytes 1179656 | tf_op jit(solution)/shard_map/ppermute | solution.py:964
  323.1 17.6 %down_back_gelu.1 = (bf16[512,4096]{1,0:T(8,128)(2,1)}, f32[1,4096]{1,0:T(1,128)}) custom-call(s32[20]{0:T(128)} %get-tuple-element.317.perm, bf16[512,1024]{1,0:T(8,128)(2,1)} %copy-done.41, bf16[8,4,512,256]{3,2,1,0:T(8,128)(2,1)} %bitcast.258, bf16[8,4,512,256]{3,2,1,0:T(8,128)(2,1)} %bitcast.259, f32[512,4096]{1,0:T(8,128)} %copy-done.7), custom_call_target="tpu_custom_call" | custom-call | flops 4294967296 | bytes 20971520 | tf_op jit(solution)/shard_map/down_back_gelu/pallas_call | solution.py:426
  344.1 6.8 %weight_grad.5 = (bf16[4,4,128,1024]{3,2,1,0:T(8,128)(2,1)S(1)}, bf16[4,4,128,1024]{3,2,1,0:T(8,128)(2,1)S(1)}) custom-call(s32[20]{0:T(128)S(1)} %copy-done.49, bf16[512,1024]{1,0:T(8,128)(2,1)S(1)} %copy-done.62, bf16[512,4096]{1,0:T(8,128)(2,1)S(1)} %copy-done.18), custom_call_target="tpu_custom_call" | custom-call | flops 4294967296 | bytes 13631488 | tf_op jit(solution)/shard_map/weight_grad/pallas_call | solution.py:305
  351.1 13.6 %norm_back.4 = (f32[512,1024]{1,0:T(8,128)S(1)}, bf16[512,1024]{1,0:T(8,128)(2,1)S(1)}, f32[8,1024]{1,0:T(8,128)S(1)}) custom-call(s32[20]{0:T(128)S(1)} %copy-done.49, bf16[512,4096]{1,0:T(8,128)(2,1)S(1)} %copy-done.19, bf16[4,4,128,1280]{3,2,1,0:T(8,128)(2,1)} %stack.58.w0_ref.refs_1_, bf16[4,4,128,1280]{3,2,1,0:T(8,128)(2,1)} %collective-permute-done.15.w1_ref.refs_2_, ...), custom_call_target="tpu_custom_call" | custom-call | flops 4294967296 | bytes 19922944 | tf_op jit(solution)/shard_map/norm_back/pallas_call | solution.py:554
  373.7 5.7 all-to-all-start.3
  383.7 28.1 %attend_back.1 = (bf16[512,1024]{1,0:T(8,128)(2,1)S(1)}, f32[2,512,1024]{2,1,0:T(8,128)S(1)}, bf16[2,512,1024]{2,1,0:T(8,128)(2,1)S(1)}) custom-call(s32[20]{0:T(128)S(1)} %copy-done.49, s32[2]{0:T(128)S(1)} %copy-done.69, bf16[512,3072]{1,0:T(8,128)(2,1)S(1)} %copy-done.33, bf16[512,3072]{1,0:T(8,128)(2,1)S(1)} %copy-done.33, ...), custom_call_target="tpu_custom_call" | custom-call | flops 5368709120 | bytes 14680064 | tf_op jit(solution)/shard_map/attend_back/pallas_call | solution.py:722
  426.3 6.2 %weight_grad.7 = (bf16[4,4,128,768]{3,2,1,0:T(8,128)(2,1)S(1)}, bf16[4,4,128,768]{3,2,1,0:T(8,128)(2,1)}) custom-call(s32[20]{0:T(128)S(1)} %copy-done.49, bf16[512,1024]{1,0:T(8,128)(2,1)S(1)} %copy-done.60, bf16[512,3072]{1,0:T(8,128)(2,1)S(1)} %pad_maximum_fusion.d_ref.refs_0_), custom_call_target="tpu_custom_call" | custom-call | flops 3221225472 | bytes 10485760 | tf_op jit(solution)/shard_map/weight_grad/pallas_call | solution.py:305
  437.6 11.2 %collective-permute-done.28 = bf16[2,128,1024]{2,1,0:T(8,128)(2,1)S(1)} collective-permute-done((bf16[2,128,1024]{2,1,0:T(8,128)(2,1)}, bf16[2,128,1024]{2,1,0:T(8,128)(2,1)S(1)}, u32[]{:S(2)}, u32[]{:S(2)}) %collective-permute-start.28) | collective-permute-done | bytes 524320 | tf_op jit(solution)/shard_map/ppermute | solution.py:964
  452.5 5.4 all-to-all-start.4
  467.5 10.4 %norm_back.5 = (bf16[512,1024]{1,0:T(8,128)(2,1)S(1)}, f32[8,1024]{1,0:T(8,128)S(1)}) custom-call(s32[20]{0:T(128)S(1)} %copy-done.49, bf16[512,3072]{1,0:T(8,128)(2,1)S(1)} %copy-done.3, bf16[4,4,128,768]{3,2,1,0:T(8,128)(2,1)S(1)} %copy-done.1, bf16[4,4,128,768]{3,2,1,0:T(8,128)(2,1)S(1)} %copy-done.21, f32[512,1024]{1,0:T(8,128)S(1)} %copy-done.10, ...), custom_call_target="tpu_custom_call" | custom-call | flops 3221225472 | bytes 16777216 | tf_op jit(solution)/shard_map/norm_back/pallas_call | solution.py:554
  479.0 7.3 %all-to-all-done.4 = bf16[4,128,1024]{2,1,0:T(8,128)(2,1)} async-done(((bf16[4,128,1024]{2,1,0:T(8,128)(2,1)}), bf16[4,128,1024]{2,1,0:T(8,128)(2,1)}, u32[]{:S(2)}, u32[]{:S(2)}) %all-to-all-start.4) | async-done | bytes 1048608 | tf_op jit(solution)/shard_map/all_to_all | solution.py:1058
  497.1 20.4 %collective-permute-done.34 = bf16[4,128,256]{2,1,0:T(8,128)(2,1)S(1)} collective-permute-done((bf16[4,128,256]{2,1,0:T(8,128)(2,1)S(1)}, bf16[4,128,256]{2,1,0:T(8,128)(2,1)S(1)}, u32[]{:S(2)}, u32[]{:S(2)}) %collective-permute-start.34) | collective-permute-done | bytes 262176 | tf_op jit(solution)/shard_map/ppermute | solution.py:964
  522.4 9.2 %collective-permute-done.41 = bf16[2,128,768]{2,1,0:T(8,128)(2,1)S(1)} collective-permute-done((bf16[2,128,768]{2,1,0:T(8,128)(2,1)S(1)}, bf16[2,128,768]{2,1,0:T(8,128)(2,1)S(1)}, u32[]{:S(2)}, u32[]{:S(2)}) %collective-permute-start.41) | collective-permute-done | bytes 393248 | tf_op jit(solution)/shard_map/ppermute | solution.py:964
  549.0 7.0 %collective-permute-done.40 = bf16[144,128]{1,0:T(8,128)(2,1)S(1)} collective-permute-done((bf16[144,128]{1,0:T(8,128)(2,1)S(1)}, bf16[144,128]{1,0:T(8,128)(2,1)S(1)}, u32[]{:S(2)}, u32[]{:S(2)}) %collective-permute-start.40) | collective-permute-done | bytes 36896 | tf_op jit(solution)/shard_map/ppermute | solution.py:964
  556.0 6.1 %collective-permute-done.39 = bf16[144,128]{1,0:T(8,128)(2,1)S(1)} collective-permute-done((bf16[144,128]{1,0:T(8,128)(2,1)S(1)}, bf16[144,128]{1,0:T(8,128)(2,1)S(1)}, u32[]{:S(2)}, u32[]{:S(2)}) %collective-permute-start.39) | collective-permute-done | bytes 36896 | tf_op jit(solution)/shard_map/ppermute | solution.py:964
  (456 shorter events, 227.3 us)
Async XLA Ops:
  9.8 17.0 %all-to-all-start = ((bf16[4,336,128]{2,1,0:T(8,128)(2,1)}), bf16[4,336,128]{2,1,0:T(8,128)(2,1)S(1)}, u32[]{:S(2)}, u32[]{:S(2)}) async-start(bf16[4,336,128]{2,1,0:T(8,128)(2,1)} %broadcast_in_dim.71), calls=%async_computation | async-start | bytes 688128 | tf_op jit(solution)/shard_map/all_to_all | solution.py:1058
  27.8 21.9 %all-to-all-start.1 = ((bf16[4,128,768]{2,1,0:T(8,128)(2,1)}), bf16[4,128,768]{2,1,0:T(8,128)(2,1)S(1)}, u32[]{:S(2)}, u32[]{:S(2)}) async-start(bf16[4,128,768]{2,1,0:T(8,128)(2,1)} %broadcast_in_dim.72), calls=%async_computation.1 | async-start | bytes 1572864 | tf_op jit(solution)/shard_map/all_to_all | solution.py:1058
  52.2 29.3 %collective-permute-start.5 = (bf16[4,128,768]{2,1,0:T(8,128)(2,1)S(1)}, bf16[4,128,768]{2,1,0:T(8,128)(2,1)S(1)}, u32[]{:S(2)}, u32[]{:S(2)}) collective-permute-start(bf16[4,128,768]{2,1,0:T(8,128)(2,1)S(1)} %all-to-all-done.1.refs_0_), channel_id=1, source_target_pairs={{0,16},{4,20},{8,24},{12,28},{16,0},{20,4},{24,8},{28,12},{1,17},{... | collective-permute-start | bytes 2359304 | tf_op jit(solution)/shard_map/ppermute | solution.py:964
  53.7 28.7 %collective-permute-start.4 = (bf16[4,128,768]{2,1,0:T(8,128)(2,1)S(1)}, bf16[4,128,768]{2,1,0:T(8,128)(2,1)}, u32[]{:S(2)}, u32[]{:S(2)}) collective-permute-start(bf16[4,128,768]{2,1,0:T(8,128)(2,1)S(1)} %all-to-all-done.1.refs_0_), channel_id=1, source_target_pairs={{0,8},{4,12},{8,0},{12,4},{16,24},{20,28},{24,16},{28,20},{1,9},{5... | collective-permute-start | bytes 2359304 | tf_op jit(solution)/shard_map/ppermute | solution.py:964
  65.1 37.9 %all-to-all-start.2 = ((bf16[4,128,1280]{2,1,0:T(8,128)(2,1)}), bf16[4,128,1280]{2,1,0:T(8,128)(2,1)}, u32[]{:S(2)}, u32[]{:S(2)}) async-start(bf16[4,128,1280]{2,1,0:T(8,128)(2,1)} %broadcast_in_dim.73), calls=%async_computation.2 | async-start | bytes 2621440 | tf_op jit(solution)/shard_map/all_to_all | solution.py:1058
  71.5 161.9 %all-gather.3.cloned.1.call-start = ((), (), s32[]{:S(2)}) async-start(), calls=%async_computation.10 | async-start | bytes 8650752 | tf_op jit(solution)/shard_map/all_gather | solution.py:987
  82.7 20.3 %collective-permute-start.8 = (bf16[4,128,768]{2,1,0:T(8,128)(2,1)}, bf16[4,128,768]{2,1,0:T(8,128)(2,1)}, u32[]{:S(2)}, u32[]{:S(2)}) collective-permute-start(bf16[4,128,768]{2,1,0:T(8,128)(2,1)} %collective-permute-done.4.refs_1_), channel_id=1, source_target_pairs={{0,16},{4,20},{8,24},{12,28},{16,0},{20,4},{24,8},{28,12},{1,17},{... | collective-permute-start | bytes 2359304 | tf_op jit(solution)/shard_map/ppermute | solution.py:964
  103.0 312.2 %reduce-scatter.3.cloned.1.call-start = ((), (), s32[]{:S(2)}) async-start(), calls=%async_computation.8 | async-start | bytes 9437184 | tf_op jit(solution)/shard_map/reduce_scatter | solution.py:1292
  120.3 39.0 %collective-permute-start.12 = (bf16[4,128,1280]{2,1,0:T(8,128)(2,1)}, bf16[4,128,1280]{2,1,0:T(8,128)(2,1)}, u32[]{:S(2)}, u32[]{:S(2)}) collective-permute-start(bf16[4,128,1280]{2,1,0:T(8,128)(2,1)} %all-to-all-done.2.refs_0_), channel_id=1, source_target_pairs={{0,8},{4,12},{8,0},{12,4},{16,24},{20,28},{24,16},{28,20},{1,9},{5... | collective-permute-start | bytes 3932168 | tf_op jit(solution)/shard_map/ppermute | solution.py:964
  121.8 37.5 %collective-permute-start.11 = (bf16[4,128,1280]{2,1,0:T(8,128)(2,1)}, bf16[4,128,1280]{2,1,0:T(8,128)(2,1)}, u32[]{:S(2)}, u32[]{:S(2)}) collective-permute-start(bf16[4,128,1280]{2,1,0:T(8,128)(2,1)} %all-to-all-done.2.refs_0_), channel_id=1, source_target_pairs={{0,16},{4,20},{8,24},{12,28},{16,0},{20,4},{24,8},{28,12},{1,17},{... | collective-permute-start | bytes 3932168 | tf_op jit(solution)/shard_map/ppermute | solution.py:964
  161.6 26.8 %collective-permute-start.13 = (bf16[2,128,1280]{2,1,0:T(8,128)(2,1)S(1)}, bf16[2,128,1280]{2,1,0:T(8,128)(2,1)S(1)}, u32[]{:S(2)}, u32[]{:S(2)}) collective-permute-start(bf16[2,128,1280]{2,1,0:T(8,128)(2,1)S(1)} %slice.285), channel_id=1, source_target_pairs={{0,8},{4,12},{8,0},{12,4},{16,24},{20,28},{24,16},{28,20},{1,9},{5... | collective-permute-start | bytes 1966088 | tf_op jit(solution)/shard_map/ppermute | solution.py:964
  164.1 24.3 %collective-permute-start.14 = (bf16[2,128,1280]{2,1,0:T(8,128)(2,1)S(1)}, bf16[2,128,1280]{2,1,0:T(8,128)(2,1)S(1)}, u32[]{:S(2)}, u32[]{:S(2)}) collective-permute-start(bf16[2,128,1280]{2,1,0:T(8,128)(2,1)S(1)} %slice.286), channel_id=1, source_target_pairs={{0,16},{4,20},{8,24},{12,28},{16,0},{20,4},{24,8},{28,12},{1,17},{... | collective-permute-start | bytes 1966088 | tf_op jit(solution)/shard_map/ppermute | solution.py:964
  194.5 57.4 %collective-permute-start.17 = (f32[12,19,256]{2,1,0:T(8,128)}, f32[12,19,256]{2,1,0:T(8,128)S(1)}, u32[]{:S(2)}, u32[]{:S(2)}) collective-permute-start(f32[12,19,256]{2,1,0:T(8,128)} %get-tuple-element.285), channel_id=1, source_target_pairs={{0,2},{1,0},{2,6},{3,4},{4,3},{5,1},{6,7},{7,5},{8,10},{9,8},{10,1... | collective-permute-start | bytes 700424 | tf_op jit(solution)/shard_map/ppermute | solution.py:1166
  196.9 55.0 %collective-permute-start.16 = (f32[12,19,256]{2,1,0:T(8,128)}, f32[12,19,256]{2,1,0:T(8,128)}, u32[]{:S(2)}, u32[]{:S(2)}) collective-permute-start(f32[12,19,256]{2,1,0:T(8,128)} %get-tuple-element.286), channel_id=1, source_target_pairs={{0,0},{1,2},{2,4},{3,6},{4,1},{5,3},{6,5},{7,7},{8,8},{9,10},{10,1... | collective-permute-start | bytes 700424 | tf_op jit(solution)/shard_map/ppermute | solution.py:1165
  298.0 42.6 %collective-permute-start.21 = (bf16[2,4,192,128]{3,2,1,0:T(8,128)(2,1)S(1)}, bf16[2,4,192,128]{3,2,1,0:T(8,128)(2,1)S(1)}, u32[]{:S(2)}, u32[]{:S(2)}) collective-permute-start(bf16[2,4,192,128]{3,2,1,0:T(8,128)(2,1)S(1)} %add_convert_fusion.6), channel_id=1, source_target_pairs={{0,16},{4,20},{8,24},{12,28},{16,0},{20,4},{24,8},{28,12},{1,17},{... | collective-permute-start | bytes 1179656 | tf_op jit(solution)/shard_map/ppermute | solution.py:964
  372.0 43.2 %collective-permute-start.24 = (bf16[4,4,128,256]{3,2,1,0:T(8,128)(2,1)S(1)}, bf16[4,4,128,256]{3,2,1,0:T(8,128)(2,1)}, u32[]{:S(2)}, u32[]{:S(2)}) collective-permute-start(bf16[4,4,128,256]{3,2,1,0:T(8,128)(2,1)S(1)} %get-tuple-element.202), channel_id=1, source_target_pairs={{0,4},{4,0},{8,12},{12,8},{16,20},{20,16},{24,28},{28,24},{1,5},{5... | collective-permute-start | bytes 3145736 | tf_op jit(solution)/shard_map/ppermute | solution.py:964
  372.0 43.2 %collective-permute-start.25 = (bf16[2,2,128,1024]{3,2,1,0:T(8,128)(2,1)}, bf16[2,2,128,1024]{3,2,1,0:T(8,128)(2,1)}, u32[]{:S(2)}, u32[]{:S(2)}) collective-permute-start(bf16[2,2,128,1024]{3,2,1,0:T(8,128)(2,1)} %fusion), channel_id=1, source_target_pairs={{0,8},{4,12},{8,0},{12,4},{16,24},{20,28},{24,16},{28,20},{1,9},{5... | collective-permute-start | bytes 3145736 | tf_op jit(solution)/shard_map/ppermute | solution.py:964
  373.7 41.5 %collective-permute-start.26 = (bf16[2,2,128,1024]{3,2,1,0:T(8,128)(2,1)}, bf16[2,2,128,1024]{3,2,1,0:T(8,128)(2,1)}, u32[]{:S(2)}, u32[]{:S(2)}) collective-permute-start(bf16[2,2,128,1024]{3,2,1,0:T(8,128)(2,1)} %fusion.1), channel_id=1, source_target_pairs={{0,16},{4,20},{8,24},{12,28},{16,0},{20,4},{24,8},{28,12},{1,17},{... | collective-permute-start | bytes 3145736 | tf_op jit(solution)/shard_map/ppermute | solution.py:964
  373.7 41.5 %all-to-all-start.3 = ((bf16[4,192,128]{2,1,0:T(8,128)(2,1)}), bf16[4,192,128]{2,1,0:T(8,128)(2,1)S(1)}, u32[]{:S(2)}, u32[]{:S(2)}) async-start(bf16[4,192,128]{2,1,0:T(8,128)(2,1)} %fusion.25), calls=%async_computation.3 | async-start | bytes 393216 | tf_op jit(solution)/shard_map/all_to_all | solution.py:1058
  379.4 99.6 %reduce-scatter.5.cloned.1.call-start = ((), (), s32[]{:S(2)}) async-start(), calls=%async_computation.9 | async-start | bytes 1310720 | tf_op jit(solution)/shard_map/reduce_scatter | solution.py:1324
  434.2 52.1 %collective-permute-start.30 = (bf16[4,4,128,768]{3,2,1,0:T(8,128)(2,1)}, bf16[4,4,128,768]{3,2,1,0:T(8,128)(2,1)}, u32[]{:S(2)}, u32[]{:S(2)}) collective-permute-start(bf16[4,4,128,768]{3,2,1,0:T(8,128)(2,1)} %get-tuple-element.230), channel_id=1, source_target_pairs={{0,4},{4,0},{8,12},{12,8},{16,20},{20,16},{24,28},{28,24},{1,5},{5... | collective-permute-start | bytes 9437192 | tf_op jit(solution)/shard_map/ppermute | solution.py:964
  434.7 14.1 %collective-permute-start.28 = (bf16[2,128,1024]{2,1,0:T(8,128)(2,1)}, bf16[2,128,1024]{2,1,0:T(8,128)(2,1)S(1)}, u32[]{:S(2)}, u32[]{:S(2)}) collective-permute-start(bf16[2,128,1024]{2,1,0:T(8,128)(2,1)} %fusion.18), channel_id=1, source_target_pairs={{0,16},{4,20},{8,24},{12,28},{16,0},{20,4},{24,8},{28,12},{1,17},{... | collective-permute-start | bytes 1572872 | tf_op jit(solution)/shard_map/ppermute | solution.py:964
  452.5 33.9 %all-to-all-start.4 = ((bf16[4,128,1024]{2,1,0:T(8,128)(2,1)}), bf16[4,128,1024]{2,1,0:T(8,128)(2,1)}, u32[]{:S(2)}, u32[]{:S(2)}) async-start(bf16[4,128,1024]{2,1,0:T(8,128)(2,1)} %pad_maximum_fusion.1), calls=%async_computation.5 | async-start | bytes 2097152 | tf_op jit(solution)/shard_map/all_to_all | solution.py:1058
  459.4 19.5 %collective-permute-start.31 = (bf16[2,4,128,256]{3,2,1,0:T(8,128)(2,1)}, bf16[2,4,128,256]{3,2,1,0:T(8,128)(2,1)}, u32[]{:S(2)}, u32[]{:S(2)}) collective-permute-start(bf16[2,4,128,256]{3,2,1,0:T(8,128)(2,1)} %fusion.17), channel_id=1, source_target_pairs={{0,8},{4,12},{8,0},{12,4},{16,24},{20,28},{24,16},{28,20},{1,9},{5... | collective-permute-start | bytes 1572872 | tf_op jit(solution)/shard_map/ppermute | solution.py:964
  491.3 26.1 %collective-permute-start.32 = (bf16[2,2,128,768]{3,2,1,0:T(8,128)(2,1)S(1)}, bf16[2,2,128,768]{3,2,1,0:T(8,128)(2,1)S(1)}, u32[]{:S(2)}, u32[]{:S(2)}) collective-permute-start(bf16[2,2,128,768]{3,2,1,0:T(8,128)(2,1)S(1)} %fusion.6), channel_id=1, source_target_pairs={{0,8},{4,12},{8,0},{12,4},{16,24},{20,28},{24,16},{28,20},{1,9},{5... | collective-permute-start | bytes 2359304 | tf_op jit(solution)/shard_map/ppermute | solution.py:964
  492.8 24.6 %collective-permute-start.33 = (bf16[2,2,128,768]{3,2,1,0:T(8,128)(2,1)S(1)}, bf16[2,2,128,768]{3,2,1,0:T(8,128)(2,1)S(1)}, u32[]{:S(2)}, u32[]{:S(2)}) collective-permute-start(bf16[2,2,128,768]{3,2,1,0:T(8,128)(2,1)S(1)} %fusion.7), channel_id=1, source_target_pairs={{0,16},{4,20},{8,24},{12,28},{16,0},{20,4},{24,8},{28,12},{1,17},{... | collective-permute-start | bytes 2359304 | tf_op jit(solution)/shard_map/ppermute | solution.py:964
  494.3 23.1 %collective-permute-start.34 = (bf16[4,128,256]{2,1,0:T(8,128)(2,1)S(1)}, bf16[4,128,256]{2,1,0:T(8,128)(2,1)S(1)}, u32[]{:S(2)}, u32[]{:S(2)}) collective-permute-start(bf16[4,128,256]{2,1,0:T(8,128)(2,1)S(1)} %fusion.28), channel_id=1, source_target_pairs={{0,16},{4,20},{8,24},{12,28},{16,0},{20,4},{24,8},{28,12},{1,17},{... | collective-permute-start | bytes 786440 | tf_op jit(solution)/shard_map/ppermute | solution.py:964
  497.0 24.1 %collective-permute-start.35 = (bf16[4,4,144,128]{3,2,1,0:T(8,128)(2,1)S(1)}, bf16[4,4,144,128]{3,2,1,0:T(8,128)(2,1)S(1)}, u32[]{:S(2)}, u32[]{:S(2)}) collective-permute-start(bf16[4,4,144,128]{3,2,1,0:T(8,128)(2,1)S(1)} %get-tuple-element.243), channel_id=1, source_target_pairs={{0,4},{4,0},{8,12},{12,8},{16,20},{20,16},{24,28},{28,24},{1,5},{5... | collective-permute-start | bytes 1769480 | tf_op jit(solution)/shard_map/ppermute | solution.py:964
  521.2 16.1 %collective-permute-start.36 = (bf16[2,4,144,128]{3,2,1,0:T(8,128)(2,1)S(1)}, bf16[2,4,144,128]{3,2,1,0:T(8,128)(2,1)}, u32[]{:S(2)}, u32[]{:S(2)}) collective-permute-start(bf16[2,4,144,128]{3,2,1,0:T(8,128)(2,1)S(1)} %add_convert_fusion.7), channel_id=1, source_target_pairs={{0,16},{4,20},{8,24},{12,28},{16,0},{20,4},{24,8},{28,12},{1,17},{... | collective-permute-start | bytes 884744 | tf_op jit(solution)/shard_map/ppermute | solution.py:964
  532.9 29.8 %all-to-all-start.5 = ((bf16[4,128,1024]{2,1,0:T(8,128)(2,1)}), bf16[4,128,1024]{2,1,0:T(8,128)(2,1)S(1)}, u32[]{:S(2)}, u32[]{:S(2)}) async-start(bf16[4,128,1024]{2,1,0:T(8,128)(2,1)} %pad_maximum_fusion.2), calls=%async_computation.7 | async-start | bytes 2097152 | tf_op jit(solution)/shard_map/all_to_all | solution.py:1058
  547.6 14.5 %collective-permute-start.39 = (bf16[144,128]{1,0:T(8,128)(2,1)S(1)}, bf16[144,128]{1,0:T(8,128)(2,1)S(1)}, u32[]{:S(2)}, u32[]{:S(2)}) collective-permute-start(bf16[144,128]{1,0:T(8,128)(2,1)S(1)} %get-tuple-element.295), channel_id=1, source_target_pairs={{0,2},{1,3},{2,0},{3,1},{4,6},{5,7},{6,4},{7,5},{8,10},{9,11},{10,... | collective-permute-start | bytes 110600 | tf_op jit(solution)/shard_map/ppermute | solution.py:964
  547.6 14.5 %collective-permute-start.38 = (bf16[144,128]{1,0:T(8,128)(2,1)S(1)}, bf16[144,128]{1,0:T(8,128)(2,1)S(1)}, u32[]{:S(2)}, u32[]{:S(2)}) collective-permute-start(bf16[144,128]{1,0:T(8,128)(2,1)S(1)} %get-tuple-element.296), channel_id=1, source_target_pairs={{0,1},{1,0},{2,3},{3,2},{4,5},{5,4},{6,7},{7,6},{8,9},{9,8},{10,11... | collective-permute-start | bytes 110600 | tf_op jit(solution)/shard_map/ppermute | solution.py:964
  (140 other events, 1508.1 us)
Sparse Core Ops, SparseCore 0:
  103.2 100.6 all-gather.2
  294.7 117.0 reduce-scatter.2
  437.7 29.5 reduce-scatter.4

commit v4 on v3

--- a/solution.py
+++ b/solution.py
@@ -97,7 +97,7 @@
         for j in range(BLOCKS // 2):
             cols = lane_block(perm[i * BLOCKS // 2 + j], WIDE)
             h_ref[:, cols] = hr[:, j * WIDE : (j + 1) * WIDE] + b_ref[:, cols]
-    norm_store(perm, h_ref, g_ref, s_ref, a_ref, 32)
+    norm_store(perm, h_ref, g_ref, s_ref, a_ref, 128)
 
 
 def embed(perm, x, chunk, b, g, s):
@@ -142,7 +142,7 @@
 
     @pl.when(z == pl.num_programs(0) - 1)
     def _():
-        norm_store(perm, h_ref, g_ref, s_ref, n_ref, 32)
+        norm_store(perm, h_ref, g_ref, s_ref, n_ref, 128)
 
 
 def project(perm, a, chunk, at, res, b, g, s, grant=VMEM):
@@ -389,7 +389,7 @@
             ],
         ),
         out_shape=[jax.ShapeDtypeStruct((rows, FF), F32), jax.ShapeDtypeStruct((rows, FF), BF16)],
-        compiler_params=params(VMEM),
+        compiler_params=params(WIDE_VMEM),
         cost_estimate=pl.CostEstimate(
             flops=2 * rows * D * FF, bytes_accessed=rows * FF * 6 + 2 * D * FF, transcendentals=rows * FF
         ),
@@ -487,7 +487,7 @@
 
     @pl.when(n == pl.num_programs(0) - 1)
     def _():
-        chunk = 32
+        chunk = 128
         part_ref[...] = jnp.zeros_like(part_ref)
 
         def fold(x):
@@ -561,7 +561,7 @@
             scratch_shapes=[pltpu.VMEM((rows, D), F32), pltpu.VMEM((3, 8, D), F32)],
         ),
         out_shape=out_shape,
-        compiler_params=params(VMEM),
+        compiler_params=params(WIDE_VMEM if placed else VMEM),
         cost_estimate=pl.CostEstimate(
             flops=2 * rows * D * wide,
             bytes_accessed=rows * D * 14 + 2 * D * wide + 2 * rows * wide,
@@ -1334,33 +1334,30 @@
     dw_joint = weight_grad(perm, a1, dp)
     if placed:
         sj = Scatter(dw_joint, streams)
-        sj.keep, dp, *su.moved = together(sj.keep, dp, *su.moved)
+        sj.keep, dp = together(sj.keep, dp)
+    dh0_low, sums1 = norm_back(perm, dp, w_first, False, h0, gains[0], dh1, True)
+    if placed:
+        dh0_low, sj.got, *su.moved = together(dh0_low, sj.got, *su.moved)
+        sj.near()
         su.last()
-        dp = settle([su], dp)
+        dh0_low = settle([sj, su], dh0_low)
+        sj.send(0)
         su.rows()
-    dh0_low, sums1 = norm_back(perm, dp, w_first, False, h0, gains[0], dh1, True)
-    if placed:
-        dh0_low, sj.got, su.total, r_down, *so.moved = together(
-            dh0_low, sj.got, su.total, r_down, *so.moved
-        )
+    dw_patch = side_grad(perm, x.T, dh0_low)
+    if placed:
+        sp = Scatter(dw_patch, ("yx",))
+        sp.keep, r_down, *moved = together(sp.keep, r_down, *sj.moved, *so.moved)
+        sj.moved, so.moved = moved[:2], moved[2:]
         r_down = r_down.astype(F32)
-        sj.near()
         so.cross()
-        dh0_low = settle([sj, so], dh0_low)
-        sj.send(0)
+        sj.cross()
+        settle([sj, so])
+        sj.send(1)
         so.send(1)
-    dw_patch = side_grad(perm, x.T, dh0_low)
-    if placed:
-        sp = Scatter(dw_patch, ("yx",))
-        sp.keep, *moved = together(sp.keep, *sj.moved, *so.moved)
-        sj.moved, so.moved = moved[:2], moved[2:]
-        so.last()
-        sj.cross()
-        settle([sj])
-        sj.send(1)
         sp.near()
         sp.send(0)
         sj.last()
+        so.last()
         wide = sj.away[0].shape[-1]
         sj.away = [jnp.concatenate([sj.away[0], so.away[0]], axis=-1)]
         sj.rows()

time: 616 us -> 580 us (0.942)
  waiting for transfers between devices: 161 us -> 132 us
  starting transfers between devices: 103 us -> 78.5 us
  Pallas kernels: 195 us -> 215 us
    pallas_call x1, Pallas kernels: 12.4 us -> 38.8 us  [render(): pl.pallas_call(render_kernel, in_specs=[smem, smem, whole(zt), whole(zx),...]
    ppermute x46, starting transfers between devices: 64.6 us -> 40.8 us  [swap(): return lax.ppermute(x, axis, flip_pairs(lax.axis_size(axis), bit))]
    ppermute x46, waiting for transfers between devices: 126 us -> 104 us  [swap(): return lax.ppermute(x, axis, flip_pairs(lax.axis_size(axis), bit))]
    unnamed x236 -> x216, local copies, waits for them, and re-layouts: 51 us -> 42.1 us
    all_to_all x6, waiting for transfers between devices: 26.2 us -> 18.9 us  [share_rows(): return lax.all_to_all(x, 'rows', 0, 0)]
  transfers between devices with their start and end apart: 59 -> 59, of which waited for: 28 -> 28; matrix products, arithmetic and copies ran while one was open for 8% -> 10% of each run, Pallas kernels for 26% -> 27%
where the time goes in v4:
time: 580 us; the launch traced here: 570 us
  Pallas kernels  215 us (37%)
  waiting for transfers between devices  132 us (23%)
  starting transfers between devices  78.5 us (14%)
  local copies, waits for them, and re-layouts  63.5 us (11%)
  other arithmetic  56 us (10%)
  between operations  24.9 us (4%)
    ppermute x46, waiting for transfers between devices, swap(): return lax.ppermute(x, axis, flip_pairs(lax.axis_size(axis), bit))  104 us
    unnamed x216, local copies, waits for them, and re-layouts  42.1 us
    ppermute x46, starting transfers between devices, swap(): return lax.ppermute(x, axis, flip_pairs(lax.axis_size(axis), bit))  40.8 us
    pallas_call x1, Pallas kernels, render(): pl.pallas_call(render_kernel, in_specs=[smem, smem, whole(zt), whole(zx),...  38.8 us
    all_to_all x6, starting transfers between devices, share_rows(): return lax.all_to_all(x, 'rows', 0, 0)  29.8 us
    pallas_call x1, Pallas kernels, attend_back(): pl.pallas_call(attend_back_kernel, grid_spec=pltpu.PrefetchScalarGridSpec...  28.1 us
    pallas_call x3, Pallas kernels, norm_back(): pl.pallas_call(functools.partial(back_kernel, res is not None, placed, tu...  26.8 us
    pallas_call x4, Pallas kernels, weight_grad(): pl.pallas_call(grad_kernel, grid_spec=pltpu.PrefetchScalarGridSpec(num_sc...  23.9 us
  transfers between devices with their start and end apart: 59, of which 28 were waited for; matrix products, arithmetic and copies ran while one was open for 10% of the time, Pallas kernels for 27%

profile of v4, /device:TPU:0, one launch (start us, length us, event | category | flops | bytes accessed | tf_op | source)
XLA Modules:
  0.0 570.1 jit_solution(14143861649486407583)
XLA Ops:
  9.8 6.3 %all-to-all-start = ((bf16[4,336,128]{2,1,0:T(8,128)(2,1)}), bf16[4,336,128]{2,1,0:T(8,128)(2,1)S(1)}, u32[]{:S(2)}, u32[]{:S(2)}) async-start(bf16[4,336,128]{2,1,0:T(8,128)(2,1)} %broadcast_in_dim.71), calls=%async_computation | async-start | bytes 688128 | tf_op jit(solution)/shard_map/all_to_all | solution.py:1058
  17.2 9.6 %all-to-all-done.refs_0_ = bf16[4,336,128]{2,1,0:T(8,128)(2,1)S(1)} async-done(((bf16[4,336,128]{2,1,0:T(8,128)(2,1)}), bf16[4,336,128]{2,1,0:T(8,128)(2,1)S(1)}, u32[]{:S(2)}, u32[]{:S(2)}) %all-to-all-start) | async-done | bytes 344096 | tf_op jit(solution)/shard_map/all_to_all | solution.py:1058
  34.3 4.8 collective-permute-done.1.refs_1_
  40.3 9.3 %all-to-all-done.1.refs_0_ = bf16[4,128,768]{2,1,0:T(8,128)(2,1)S(1)} async-done(((bf16[4,128,768]{2,1,0:T(8,128)(2,1)}), bf16[4,128,768]{2,1,0:T(8,128)(2,1)S(1)}, u32[]{:S(2)}, u32[]{:S(2)}) %all-to-all-start.1) | async-done | bytes 786464 | tf_op jit(solution)/shard_map/all_to_all | solution.py:1058
  55.3 8.6 %collective-permute-done.3 = bf16[256,576]{0,1:T(8,128)(2,1)} collective-permute-done((bf16[256,576]{0,1:T(8,128)(2,1)S(1)}, bf16[256,576]{0,1:T(8,128)(2,1)}, u32[]{:S(2)}, u32[]{:S(2)}) %collective-permute-start.3) | collective-permute-done | bytes 294944 | tf_op jit(solution)/shard_map/ppermute | solution.py:1166
  65.1 6.4 %all-to-all-start.2 = ((bf16[4,128,1280]{2,1,0:T(8,128)(2,1)}), bf16[4,128,1280]{2,1,0:T(8,128)(2,1)}, u32[]{:S(2)}, u32[]{:S(2)}) async-start(bf16[4,128,1280]{2,1,0:T(8,128)(2,1)} %broadcast_in_dim.73), calls=%async_computation.2 | async-start | bytes 2621440 | tf_op jit(solution)/shard_map/all_to_all | solution.py:1058
  72.9 8.5 %collective-permute-done.6.refs_3_ = bf16[4,336,128]{2,1,0:T(8,128)(2,1)S(1)} collective-permute-done((bf16[4,336,128]{2,1,0:T(8,128)(2,1)S(1)}, bf16[4,336,128]{2,1,0:T(8,128)(2,1)S(1)}, u32[]{:S(2)}, u32[]{:S(2)}) %collective-permute-start.6) | collective-permute-done | bytes 344096 | tf_op jit(solution)/shard_map/ppermute | solution.py:964
  106.9 5.6 collective-permute-done.9.w1_ref.refs_2_
  112.5 5.2 joint.1.q_ref.k0_ref.v0_ref
  126.5 20.2 %attend.1 = (bf16[512,1024]{1,0:T(8,128)(2,1)S(1)}, f32[512,1024]{1,0:T(8,128)S(1)}, f32[512,1024]{1,0:T(8,128)S(1)}) custom-call(s32[20]{0:T(128)S(1)} %get-tuple-element.312.perm, s32[2]{0:T(128)S(1)} %pad_add_fusion.lens, bf16[512,3072]{1,0:T(8,128)(2,1)S(1)} %copy-done.25, bf16[512,3072]{1,0:T(8,128)(2,1)S(1)} %copy-done.25, ...), custom_call_target="tpu_custom_call" | custom-call | flops 2147483648 | bytes 6291456 | tf_op jit(solution)/shard_map/attend/pallas_call | solution.py:629
  149.0 10.1 %collective-permute-done.12.refs_1_ = bf16[4,128,1280]{2,1,0:T(8,128)(2,1)} collective-permute-done((bf16[4,128,1280]{2,1,0:T(8,128)(2,1)}, bf16[4,128,1280]{2,1,0:T(8,128)(2,1)}, u32[]{:S(2)}, u32[]{:S(2)}) %collective-permute-start.12) | collective-permute-done | bytes 1310752 | tf_op jit(solution)/shard_map/ppermute | solution.py:964
  163.7 24.9 %collective-permute-done.13.refs_3_ = bf16[2,128,1280]{2,1,0:T(8,128)(2,1)S(1)} collective-permute-done((bf16[2,128,1280]{2,1,0:T(8,128)(2,1)S(1)}, bf16[2,128,1280]{2,1,0:T(8,128)(2,1)S(1)}, u32[]{:S(2)}, u32[]{:S(2)}) %collective-permute-start.13) | collective-permute-done | bytes 655392 | tf_op jit(solution)/shard_map/ppermute | solution.py:964
  188.6 5.0 stack.58.w0_ref.refs_1_
  209.9 5.3 project_norm.2
  217.5 13.8 %up_gelu.1 = (f32[512,4096]{1,0:T(8,128)}, bf16[512,4096]{1,0:T(8,128)(2,1)}) custom-call(s32[20]{0:T(128)} %get-tuple-element.311.perm, bf16[512,1024]{1,0:T(8,128)(2,1)} %copy-done.56, bf16[4,4,128,1280]{3,2,1,0:T(8,128)(2,1)} %stack.58.w0_ref.refs_1_, bf16[4,4,128,1280]{3,2,1,0:T(8,128)(2,1)} %collective-permute-done.15.w1_ref.refs_2_, f32[1,4096]{1,0:T(1,128)} %bitcast.276), custom_call_target="tpu_custom_call" | custom-call | flops 4294967296 | bytes 20971520 | tf_op jit(solution)/shard_map/up_gelu/pallas_call | solution.py:375
  231.4 12.4 %project_norm.3 = (f32[512,1024]{1,0:T(8,128)}, bf16[512,1024]{1,0:T(8,128)(2,1)}) custom-call(s32[20]{0:T(128)} %copy-done.42, bf16[512,4096]{1,0:T(8,128)(2,1)} %get-tuple-element.158.a_ref, bf16[8,4,512,256]{3,2,1,0:T(8,128)(2,1)} %bitcast.255, bf16[8,4,512,256]{3,2,1,0:T(8,128)(2,1)} %bitcast.256, f32[512,1024]{1,0:T(8,128)} %copy-done.2, ...), custom_call_target="tpu_custom_call" | custom-call | flops 4294967296 | bytes 17825792 | tf_op jit(solution)/shard_map/project_norm/pallas_call | solution.py:156
  250.7 38.8 %render.1 = (f32[768,512]{1,0:T(8,128)S(1)}, f32[768,128]{1,0:T(8,128)S(1)}, f32[8,128]{1,0:T(8,128)S(1)}) custom-call(s32[1]{0:T(128)} %bitcast.15.views_ref, f32[1]{0:T(128)} %bitcast.16.inv_ref, f32[768,512]{1,0:T(8,128)S(1)} %gauss.1.z_ref, f32[768,128]{1,0:T(8,128)S(1)} %maximum_maximum_fusion.zx_ref, f32[2,12,19,256]{3,2,1,0:T(8,128)S(1)} %pad_maximum_fusion.4.rd_ref, ...), custom_call_target="tpu_custom_call" | custom-call | flops 21743271936 | bytes 4194304 | tf_op jit(solution)/shard_map/render/pallas_call | solution.py:935
  302.0 7.9 %weight_grad.4 = bf16[8,4,512,256]{3,2,1,0:T(8,128)(2,1)S(1)} custom-call(s32[20]{0:T(128)S(1)} %copy-done.51, bf16[512,4096]{1,0:T(8,128)(2,1)S(1)} %copy-done.9, bf16[512,1024]{1,0:T(8,128)(2,1)S(1)} %get-tuple-element.174.d_ref), custom_call_target="tpu_custom_call" | custom-call | flops 4294967296 | bytes 13631488 | tf_op jit(solution)/shard_map/weight_grad/pallas_call | solution.py:305
  317.8 17.3 %down_back_gelu.1 = (bf16[512,4096]{1,0:T(8,128)(2,1)}, f32[1,4096]{1,0:T(1,128)}) custom-call(s32[20]{0:T(128)} %get-tuple-element.311.perm, bf16[512,1024]{1,0:T(8,128)(2,1)} %copy-done.33, bf16[8,4,512,256]{3,2,1,0:T(8,128)(2,1)} %bitcast.257, bf16[8,4,512,256]{3,2,1,0:T(8,128)(2,1)} %bitcast.258, f32[512,4096]{1,0:T(8,128)} %get-tuple-element.175.u_ref), custom_call_target="tpu_custom_call" | custom-call | flops 4294967296 | bytes 20971520 | tf_op jit(solution)/shard_map/down_back_gelu/pallas_call | solution.py:426
  338.5 6.8 %weight_grad.5 = (bf16[4,4,128,1024]{3,2,1,0:T(8,128)(2,1)S(1)}, bf16[4,4,128,1024]{3,2,1,0:T(8,128)(2,1)S(1)}) custom-call(s32[20]{0:T(128)S(1)} %copy-done.43, bf16[512,1024]{1,0:T(8,128)(2,1)S(1)} %copy-done.57, bf16[512,4096]{1,0:T(8,128)(2,1)S(1)} %copy-done.13), custom_call_target="tpu_custom_call" | custom-call | flops 4294967296 | bytes 13631488 | tf_op jit(solution)/shard_map/weight_grad/pallas_call | solution.py:305
  345.6 10.9 %norm_back.4 = (f32[512,1024]{1,0:T(8,128)S(1)}, bf16[512,1024]{1,0:T(8,128)(2,1)S(1)}, f32[8,1024]{1,0:T(8,128)S(1)}) custom-call(s32[20]{0:T(128)S(1)} %copy-done.43, bf16[512,4096]{1,0:T(8,128)(2,1)S(1)} %copy-done.14, bf16[4,4,128,1280]{3,2,1,0:T(8,128)(2,1)} %stack.58.w0_ref.refs_1_, bf16[4,4,128,1280]{3,2,1,0:T(8,128)(2,1)} %collective-permute-done.15.w1_ref.refs_2_, ...), custom_call_target="tpu_custom_call" | custom-call | flops 4294967296 | bytes 19922944 | tf_op jit(solution)/shard_map/norm_back/pallas_call | solution.py:554
  370.8 4.2 out_back.1.do_ref
  375.0 28.1 %attend_back.1 = (bf16[512,1024]{1,0:T(8,128)(2,1)S(1)}, f32[2,512,1024]{2,1,0:T(8,128)S(1)}, bf16[2,512,1024]{2,1,0:T(8,128)(2,1)S(1)}) custom-call(s32[20]{0:T(128)S(1)} %copy-done.43, s32[2]{0:T(128)S(1)} %copy-done.63, bf16[512,3072]{1,0:T(8,128)(2,1)S(1)} %copy-done.26, bf16[512,3072]{1,0:T(8,128)(2,1)S(1)} %copy-done.26, ...), custom_call_target="tpu_custom_call" | custom-call | flops 5368709120 | bytes 14680064 | tf_op jit(solution)/shard_map/attend_back/pallas_call | solution.py:722
  406.7 4.4 bitcast_add_fusion
  417.7 6.2 %weight_grad.7 = (bf16[4,4,128,768]{3,2,1,0:T(8,128)(2,1)S(1)}, bf16[4,4,128,768]{3,2,1,0:T(8,128)(2,1)}) custom-call(s32[20]{0:T(128)S(1)} %copy-done.43, bf16[512,1024]{1,0:T(8,128)(2,1)S(1)} %copy-done.55, bf16[512,3072]{1,0:T(8,128)(2,1)S(1)} %pad_maximum_fusion.d_ref.refs_0_), custom_call_target="tpu_custom_call" | custom-call | flops 3221225472 | bytes 10485760 | tf_op jit(solution)/shard_map/weight_grad/pallas_call | solution.py:305
  430.3 12.5 %norm_back.5 = (bf16[512,1024]{1,0:T(8,128)(2,1)}, f32[8,1024]{1,0:T(8,128)}) custom-call(s32[20]{0:T(128)} %copy-done.42, bf16[512,3072]{1,0:T(8,128)(2,1)} %copy-done.1, bf16[4,4,128,768]{3,2,1,0:T(8,128)(2,1)} %copy-done, bf16[4,4,128,768]{3,2,1,0:T(8,128)(2,1)} %copy-done.15, f32[512,1024]{1,0:T(8,128)} %copy-done.5, f32[1,1024]{1,0:T(1,128)} %bitcast.246, ...), custom_call_target="tpu_custom_call" | custom-call | flops 3221225472 | bytes 16777216 | tf_op jit(solution)/shard_map/norm_back/pallas_call | solution.py:554
  454.1 5.2 all-to-all-start.5
  465.4 5.0 collective-permute-done.31
  484.5 8.4 %collective-permute-done.40 = bf16[2,128,768]{2,1,0:T(8,128)(2,1)S(1)} collective-permute-done((bf16[2,128,768]{2,1,0:T(8,128)(2,1)S(1)}, bf16[2,128,768]{2,1,0:T(8,128)(2,1)S(1)}, u32[]{:S(2)}, u32[]{:S(2)}) %collective-permute-start.40) | collective-permute-done | bytes 393248 | tf_op jit(solution)/shard_map/ppermute | solution.py:964
  494.2 5.1 all-to-all-start.4
  510.9 5.6 collective-permute-done.39
  516.5 6.1 %collective-permute-done.38 = bf16[144,128]{1,0:T(8,128)(2,1)S(1)} collective-permute-done((bf16[144,128]{1,0:T(8,128)(2,1)S(1)}, bf16[144,128]{1,0:T(8,128)(2,1)S(1)}, u32[]{:S(2)}, u32[]{:S(2)}) %collective-permute-start.38) | collective-permute-done | bytes 36896 | tf_op jit(solution)/shard_map/ppermute | solution.py:964
  (435 shorter events, 216.8 us)
Async XLA Ops:
  9.8 17.0 %all-to-all-start = ((bf16[4,336,128]{2,1,0:T(8,128)(2,1)}), bf16[4,336,128]{2,1,0:T(8,128)(2,1)S(1)}, u32[]{:S(2)}, u32[]{:S(2)}) async-start(bf16[4,336,128]{2,1,0:T(8,128)(2,1)} %broadcast_in_dim.71), calls=%async_computation | async-start | bytes 688128 | tf_op jit(solution)/shard_map/all_to_all | solution.py:1058
  27.7 21.9 %all-to-all-start.1 = ((bf16[4,128,768]{2,1,0:T(8,128)(2,1)}), bf16[4,128,768]{2,1,0:T(8,128)(2,1)S(1)}, u32[]{:S(2)}, u32[]{:S(2)}) async-start(bf16[4,128,768]{2,1,0:T(8,128)(2,1)} %broadcast_in_dim.72), calls=%async_computation.1 | async-start | bytes 1572864 | tf_op jit(solution)/shard_map/all_to_all | solution.py:1058
  50.7 13.2 %collective-permute-start.3 = (bf16[256,576]{0,1:T(8,128)(2,1)S(1)}, bf16[256,576]{0,1:T(8,128)(2,1)}, u32[]{:S(2)}, u32[]{:S(2)}) collective-permute-start(bf16[256,576]{0,1:T(8,128)(2,1)S(1)} %get-tuple-element.283), channel_id=1, source_target_pairs={{0,2},{1,0},{2,6},{3,4},{4,3},{5,1},{6,7},{7,5},{8,10},{9,8},{10,1... | collective-permute-start | bytes 884744 | tf_op jit(solution)/shard_map/ppermute | solution.py:1166
  52.2 29.3 %collective-permute-start.5 = (bf16[4,128,768]{2,1,0:T(8,128)(2,1)S(1)}, bf16[4,128,768]{2,1,0:T(8,128)(2,1)S(1)}, u32[]{:S(2)}, u32[]{:S(2)}) collective-permute-start(bf16[4,128,768]{2,1,0:T(8,128)(2,1)S(1)} %all-to-all-done.1.refs_0_), channel_id=1, source_target_pairs={{0,16},{4,20},{8,24},{12,28},{16,0},{20,4},{24,8},{28,12},{1,17},{... | collective-permute-start | bytes 2359304 | tf_op jit(solution)/shard_map/ppermute | solution.py:964
  53.7 28.7 %collective-permute-start.4 = (bf16[4,128,768]{2,1,0:T(8,128)(2,1)S(1)}, bf16[4,128,768]{2,1,0:T(8,128)(2,1)}, u32[]{:S(2)}, u32[]{:S(2)}) collective-permute-start(bf16[4,128,768]{2,1,0:T(8,128)(2,1)S(1)} %all-to-all-done.1.refs_0_), channel_id=1, source_target_pairs={{0,8},{4,12},{8,0},{12,4},{16,24},{20,28},{24,16},{28,20},{1,9},{5... | collective-permute-start | bytes 2359304 | tf_op jit(solution)/shard_map/ppermute | solution.py:964
  65.1 37.9 %all-to-all-start.2 = ((bf16[4,128,1280]{2,1,0:T(8,128)(2,1)}), bf16[4,128,1280]{2,1,0:T(8,128)(2,1)}, u32[]{:S(2)}, u32[]{:S(2)}) async-start(bf16[4,128,1280]{2,1,0:T(8,128)(2,1)} %broadcast_in_dim.73), calls=%async_computation.2 | async-start | bytes 2621440 | tf_op jit(solution)/shard_map/all_to_all | solution.py:1058
  71.4 159.9 %all-gather.3.cloned.1.call-start = ((), (), s32[]{:S(2)}) async-start(), calls=%async_computation.10 | async-start | bytes 8650752 | tf_op jit(solution)/shard_map/all_gather | solution.py:987
  82.7 20.3 %collective-permute-start.8 = (bf16[4,128,768]{2,1,0:T(8,128)(2,1)}, bf16[4,128,768]{2,1,0:T(8,128)(2,1)}, u32[]{:S(2)}, u32[]{:S(2)}) collective-permute-start(bf16[4,128,768]{2,1,0:T(8,128)(2,1)} %collective-permute-done.4.refs_1_), channel_id=1, source_target_pairs={{0,16},{4,20},{8,24},{12,28},{16,0},{20,4},{24,8},{28,12},{1,17},{... | collective-permute-start | bytes 2359304 | tf_op jit(solution)/shard_map/ppermute | solution.py:964
  103.0 303.6 %reduce-scatter.3.cloned.1.call-start = ((), (), s32[]{:S(2)}) async-start(), calls=%async_computation.8 | async-start | bytes 9437184 | tf_op jit(solution)/shard_map/reduce_scatter | solution.py:1292
  120.2 38.8 %collective-permute-start.12 = (bf16[4,128,1280]{2,1,0:T(8,128)(2,1)}, bf16[4,128,1280]{2,1,0:T(8,128)(2,1)}, u32[]{:S(2)}, u32[]{:S(2)}) collective-permute-start(bf16[4,128,1280]{2,1,0:T(8,128)(2,1)} %all-to-all-done.2.refs_0_), channel_id=1, source_target_pairs={{0,8},{4,12},{8,0},{12,4},{16,24},{20,28},{24,16},{28,20},{1,9},{5... | collective-permute-start | bytes 3932168 | tf_op jit(solution)/shard_map/ppermute | solution.py:964
  121.7 37.3 %collective-permute-start.11 = (bf16[4,128,1280]{2,1,0:T(8,128)(2,1)}, bf16[4,128,1280]{2,1,0:T(8,128)(2,1)}, u32[]{:S(2)}, u32[]{:S(2)}) collective-permute-start(bf16[4,128,1280]{2,1,0:T(8,128)(2,1)} %all-to-all-done.2.refs_0_), channel_id=1, source_target_pairs={{0,16},{4,20},{8,24},{12,28},{16,0},{20,4},{24,8},{28,12},{1,17},{... | collective-permute-start | bytes 3932168 | tf_op jit(solution)/shard_map/ppermute | solution.py:964
  161.3 27.3 %collective-permute-start.13 = (bf16[2,128,1280]{2,1,0:T(8,128)(2,1)S(1)}, bf16[2,128,1280]{2,1,0:T(8,128)(2,1)S(1)}, u32[]{:S(2)}, u32[]{:S(2)}) collective-permute-start(bf16[2,128,1280]{2,1,0:T(8,128)(2,1)S(1)} %slice.285), channel_id=1, source_target_pairs={{0,8},{4,12},{8,0},{12,4},{16,24},{20,28},{24,16},{28,20},{1,9},{5... | collective-permute-start | bytes 1966088 | tf_op jit(solution)/shard_map/ppermute | solution.py:964
  163.7 24.9 %collective-permute-start.14 = (bf16[2,128,1280]{2,1,0:T(8,128)(2,1)S(1)}, bf16[2,128,1280]{2,1,0:T(8,128)(2,1)S(1)}, u32[]{:S(2)}, u32[]{:S(2)}) collective-permute-start(bf16[2,128,1280]{2,1,0:T(8,128)(2,1)S(1)} %slice.286), channel_id=1, source_target_pairs={{0,16},{4,20},{8,24},{12,28},{16,0},{20,4},{24,8},{28,12},{1,17},{... | collective-permute-start | bytes 1966088 | tf_op jit(solution)/shard_map/ppermute | solution.py:964
  193.6 13.5 %collective-permute-start.15 = (bf16[4,4,128,1280]{3,2,1,0:T(8,128)(2,1)}, bf16[4,4,128,1280]{3,2,1,0:T(8,128)(2,1)}, u32[]{:S(2)}, u32[]{:S(2)}) collective-permute-start(bf16[4,4,128,1280]{3,2,1,0:T(8,128)(2,1)} %stack.58.w0_ref.refs_1_), channel_id=1, source_target_pairs={{0,4},{4,0},{8,12},{12,8},{16,20},{20,16},{24,28},{28,24},{1,5},{5... | collective-permute-start | bytes 15728648 | tf_op jit(solution)/shard_map/ppermute | solution.py:964
  194.6 53.2 %collective-permute-start.17 = (f32[12,19,256]{2,1,0:T(8,128)}, f32[12,19,256]{2,1,0:T(8,128)S(1)}, u32[]{:S(2)}, u32[]{:S(2)}) collective-permute-start(f32[12,19,256]{2,1,0:T(8,128)} %get-tuple-element.279), channel_id=1, source_target_pairs={{0,2},{1,0},{2,6},{3,4},{4,3},{5,1},{6,7},{7,5},{8,10},{9,8},{10,1... | collective-permute-start | bytes 700424 | tf_op jit(solution)/shard_map/ppermute | solution.py:1166
  197.1 50.8 %collective-permute-start.16 = (f32[12,19,256]{2,1,0:T(8,128)}, f32[12,19,256]{2,1,0:T(8,128)}, u32[]{:S(2)}, u32[]{:S(2)}) collective-permute-start(f32[12,19,256]{2,1,0:T(8,128)} %get-tuple-element.280), channel_id=1, source_target_pairs={{0,0},{1,2},{2,4},{3,6},{4,1},{5,3},{6,5},{7,7},{8,8},{9,10},{10,1... | collective-permute-start | bytes 700424 | tf_op jit(solution)/shard_map/ppermute | solution.py:1165
  317.7 17.4 %collective-permute-start.21 = (bf16[2,4,192,128]{3,2,1,0:T(8,128)(2,1)S(1)}, bf16[2,4,192,128]{3,2,1,0:T(8,128)(2,1)S(1)}, u32[]{:S(2)}, u32[]{:S(2)}) collective-permute-start(bf16[2,4,192,128]{3,2,1,0:T(8,128)(2,1)S(1)} %add_convert_fusion.6), channel_id=1, source_target_pairs={{0,16},{4,20},{8,24},{12,28},{16,0},{20,4},{24,8},{28,12},{1,17},{... | collective-permute-start | bytes 1179656 | tf_op jit(solution)/shard_map/ppermute | solution.py:964
  364.1 42.5 %collective-permute-start.24 = (bf16[4,4,128,256]{3,2,1,0:T(8,128)(2,1)S(1)}, bf16[4,4,128,256]{3,2,1,0:T(8,128)(2,1)}, u32[]{:S(2)}, u32[]{:S(2)}) collective-permute-start(bf16[4,4,128,256]{3,2,1,0:T(8,128)(2,1)S(1)} %get-tuple-element.199), channel_id=1, source_target_pairs={{0,4},{4,0},{8,12},{12,8},{16,20},{20,16},{24,28},{28,24},{1,5},{5... | collective-permute-start | bytes 3145736 | tf_op jit(solution)/shard_map/ppermute | solution.py:964
  364.2 42.4 %collective-permute-start.25 = (bf16[2,2,128,1024]{3,2,1,0:T(8,128)(2,1)}, bf16[2,2,128,1024]{3,2,1,0:T(8,128)(2,1)}, u32[]{:S(2)}, u32[]{:S(2)}) collective-permute-start(bf16[2,2,128,1024]{3,2,1,0:T(8,128)(2,1)} %fusion), channel_id=1, source_target_pairs={{0,8},{4,12},{8,0},{12,4},{16,24},{20,28},{24,16},{28,20},{1,9},{5... | collective-permute-start | bytes 3145736 | tf_op jit(solution)/shard_map/ppermute | solution.py:964
  365.1 41.5 %collective-permute-start.26 = (bf16[2,2,128,1024]{3,2,1,0:T(8,128)(2,1)}, bf16[2,2,128,1024]{3,2,1,0:T(8,128)(2,1)}, u32[]{:S(2)}, u32[]{:S(2)}) collective-permute-start(bf16[2,2,128,1024]{3,2,1,0:T(8,128)(2,1)} %fusion.1), channel_id=1, source_target_pairs={{0,16},{4,20},{8,24},{12,28},{16,0},{20,4},{24,8},{28,12},{1,17},{... | collective-permute-start | bytes 3145736 | tf_op jit(solution)/shard_map/ppermute | solution.py:964
  367.3 39.2 %all-to-all-start.3 = ((bf16[4,192,128]{2,1,0:T(8,128)(2,1)}), bf16[4,192,128]{2,1,0:T(8,128)(2,1)S(1)}, u32[]{:S(2)}, u32[]{:S(2)}) async-start(bf16[4,192,128]{2,1,0:T(8,128)(2,1)} %fusion.25), calls=%async_computation.3 | async-start | bytes 393216 | tf_op jit(solution)/shard_map/all_to_all | solution.py:1058
  370.7 94.6 %reduce-scatter.5.cloned.1.call-start = ((), (), s32[]{:S(2)}) async-start(), calls=%async_computation.9 | async-start | bytes 1310720 | tf_op jit(solution)/shard_map/reduce_scatter | solution.py:1324
  425.6 18.3 %collective-permute-start.28 = (bf16[4,4,128,768]{3,2,1,0:T(8,128)(2,1)}, bf16[4,4,128,768]{3,2,1,0:T(8,128)(2,1)}, u32[]{:S(2)}, u32[]{:S(2)}) collective-permute-start(bf16[4,4,128,768]{3,2,1,0:T(8,128)(2,1)} %get-tuple-element.222), channel_id=1, source_target_pairs={{0,4},{4,0},{8,12},{12,8},{16,20},{20,16},{24,28},{28,24},{1,5},{5... | collective-permute-start | bytes 9437192 | tf_op jit(solution)/shard_map/ppermute | solution.py:964
  428.3 15.6 %collective-permute-start.29 = (bf16[2,128,1024]{2,1,0:T(8,128)(2,1)S(1)}, bf16[2,128,1024]{2,1,0:T(8,128)(2,1)S(1)}, u32[]{:S(2)}, u32[]{:S(2)}) collective-permute-start(bf16[2,128,1024]{2,1,0:T(8,128)(2,1)S(1)} %copy-done.81), channel_id=1, source_target_pairs={{0,16},{4,20},{8,24},{12,28},{16,0},{20,4},{24,8},{28,12},{1,17},{... | collective-permute-start | bytes 1572872 | tf_op jit(solution)/shard_map/ppermute | solution.py:964
  428.3 15.6 %collective-permute-start.30 = (bf16[2,128,1024]{2,1,0:T(8,128)(2,1)S(1)}, bf16[2,128,1024]{2,1,0:T(8,128)(2,1)S(1)}, u32[]{:S(2)}, u32[]{:S(2)}) collective-permute-start(bf16[2,128,1024]{2,1,0:T(8,128)(2,1)S(1)} %copy-done.80), channel_id=1, source_target_pairs={{0,8},{4,12},{8,0},{12,4},{16,24},{20,28},{24,16},{28,20},{1,9},{5... | collective-permute-start | bytes 1572872 | tf_op jit(solution)/shard_map/ppermute | solution.py:964
  429.4 36.0 %collective-permute-start.33 = (bf16[2,4,128,256]{3,2,1,0:T(8,128)(2,1)}, bf16[2,4,128,256]{3,2,1,0:T(8,128)(2,1)}, u32[]{:S(2)}, u32[]{:S(2)}) collective-permute-start(bf16[2,4,128,256]{3,2,1,0:T(8,128)(2,1)} %fusion.17), channel_id=1, source_target_pairs={{0,8},{4,12},{8,0},{12,4},{16,24},{20,28},{24,16},{28,20},{1,9},{5... | collective-permute-start | bytes 1572872 | tf_op jit(solution)/shard_map/ppermute | solution.py:964
  451.2 19.2 %collective-permute-start.31 = (bf16[2,2,128,768]{3,2,1,0:T(8,128)(2,1)}, bf16[2,2,128,768]{3,2,1,0:T(8,128)(2,1)}, u32[]{:S(2)}, u32[]{:S(2)}) collective-permute-start(bf16[2,2,128,768]{3,2,1,0:T(8,128)(2,1)} %fusion.6), channel_id=1, source_target_pairs={{0,8},{4,12},{8,0},{12,4},{16,24},{20,28},{24,16},{28,20},{1,9},{5... | collective-permute-start | bytes 2359304 | tf_op jit(solution)/shard_map/ppermute | solution.py:964
  452.1 18.9 %collective-permute-start.32 = (bf16[2,2,128,768]{3,2,1,0:T(8,128)(2,1)}, bf16[2,2,128,768]{3,2,1,0:T(8,128)(2,1)}, u32[]{:S(2)}, u32[]{:S(2)}) collective-permute-start(bf16[2,2,128,768]{3,2,1,0:T(8,128)(2,1)} %fusion.7), channel_id=1, source_target_pairs={{0,16},{4,20},{8,24},{12,28},{16,0},{20,4},{24,8},{28,12},{1,17},{... | collective-permute-start | bytes 2359304 | tf_op jit(solution)/shard_map/ppermute | solution.py:964
  454.1 40.0 %all-to-all-start.5 = ((bf16[4,128,1024]{2,1,0:T(8,128)(2,1)}), bf16[4,128,1024]{2,1,0:T(8,128)(2,1)}, u32[]{:S(2)}, u32[]{:S(2)}) async-start(bf16[4,128,1024]{2,1,0:T(8,128)(2,1)} %pad_maximum_fusion.1), calls=%async_computation.7 | async-start | bytes 2097152 | tf_op jit(solution)/shard_map/all_to_all | solution.py:1058
  476.9 16.0 %collective-permute-start.40 = (bf16[2,128,768]{2,1,0:T(8,128)(2,1)S(1)}, bf16[2,128,768]{2,1,0:T(8,128)(2,1)S(1)}, u32[]{:S(2)}, u32[]{:S(2)}) collective-permute-start(bf16[2,128,768]{2,1,0:T(8,128)(2,1)S(1)} %fusion.22), channel_id=1, source_target_pairs={{0,16},{4,20},{8,24},{12,28},{16,0},{20,4},{24,8},{28,12},{1,17},{... | collective-permute-start | bytes 1179656 | tf_op jit(solution)/shard_map/ppermute | solution.py:964
  478.4 20.9 %collective-permute-start.35 = (bf16[2,4,144,128]{3,2,1,0:T(8,128)(2,1)S(1)}, bf16[2,4,144,128]{3,2,1,0:T(8,128)(2,1)S(1)}, u32[]{:S(2)}, u32[]{:S(2)}) collective-permute-start(bf16[2,4,144,128]{3,2,1,0:T(8,128)(2,1)S(1)} %add_convert_fusion.7), channel_id=1, source_target_pairs={{0,16},{4,20},{8,24},{12,28},{16,0},{20,4},{24,8},{28,12},{1,17},{... | collective-permute-start | bytes 884744 | tf_op jit(solution)/shard_map/ppermute | solution.py:964
  494.2 31.4 %all-to-all-start.4 = ((bf16[4,128,1024]{2,1,0:T(8,128)(2,1)}), bf16[4,128,1024]{2,1,0:T(8,128)(2,1)S(1)}, u32[]{:S(2)}, u32[]{:S(2)}) async-start(bf16[4,128,1024]{2,1,0:T(8,128)(2,1)} %pad_maximum_fusion.2), calls=%async_computation.6 | async-start | bytes 2097152 | tf_op jit(solution)/shard_map/all_to_all | solution.py:1058
  (129 other events, 1229.8 us)
Sparse Core Ops, SparseCore 0:
  103.1 101.4 all-gather.2
  314.3 89.3 reduce-scatter.2
  427.7 27.0 reduce-scatter.4

commit v5 on v4

--- a/solution.py
+++ b/solution.py
@@ -600,7 +600,7 @@
         [masked_keys(ref[...], where, lens[j], 0) for j, ref in enumerate((k0_ref, k1_ref))]
         for where in sides
     ]
-    chunk = 256
+    chunk = 512
     for i in range(q_ref.shape[0] // chunk):
         rows = slice(i * chunk, (i + 1) * chunk)
         q = (q_ref[rows, :] * SCALE).astype(BF16)
@@ -1339,21 +1339,24 @@
     if placed:
         dh0_low, sj.got, *su.moved = together(dh0_low, sj.got, *su.moved)
         sj.near()
+        first, *su.moved = settle([sj], su.moved[0], su.moved[1], dh0_low)
+        dh0_low = su.moved.pop()
+        su.moved.insert(0, first)
+        sj.send(0)
         su.last()
-        dh0_low = settle([sj, su], dh0_low)
-        sj.send(0)
         su.rows()
     dw_patch = side_grad(perm, x.T, dh0_low)
     if placed:
         sp = Scatter(dw_patch, ("yx",))
-        sp.keep, r_down, *moved = together(sp.keep, r_down, *sj.moved, *so.moved)
-        sj.moved, so.moved = moved[:2], moved[2:]
+        sp.keep, *so.moved = together(sp.keep, *so.moved)
+        so.cross()
+        sp.keep = settle([so], sp.keep)
+        so.send(1)
+        sp.keep, r_down, *sj.moved = together(sp.keep, r_down, *sj.moved)
         r_down = r_down.astype(F32)
-        so.cross()
         sj.cross()
-        settle([sj, so])
+        settle([sj])
         sj.send(1)
-        so.send(1)
         sp.near()
         sp.send(0)
         sj.last()

time: 580 us -> 575 us (level)
  starting transfers between devices: 78.5 us -> 113 us
  Pallas kernels: 215 us -> 181 us
    ppermute x46, starting transfers between devices: 40.8 us -> 75.1 us  [swap(): return lax.ppermute(x, axis, flip_pairs(lax.axis_size(axis), bit))]
    pallas_call x1, Pallas kernels: 38.8 us -> 6.53 us  [render(): pl.pallas_call(render_kernel, in_specs=[smem, smem, whole(zt), whole(zx),...]
    unnamed x216 -> x220, local copies, waits for them, and re-layouts: 42.1 us -> 40.2 us
  transfers between devices with their start and end apart: 59 -> 59, of which waited for: 28 -> 26; matrix products, arithmetic and copies ran while one was open for 10% -> 10% of each run, Pallas kernels for 27% -> 27%
where the time goes in v5:
time: 575 us; the launch traced here: 566 us
  Pallas kernels  181 us (31%)
  waiting for transfers between devices  129 us (22%)
  starting transfers between devices  113 us (20%)
  local copies, waits for them, and re-layouts  61.5 us (11%)
  other arithmetic  57.8 us (10%)
  between operations  25 us (4%)
    ppermute x46, waiting for transfers between devices, swap(): return lax.ppermute(x, axis, flip_pairs(lax.axis_size(axis), bit))  101 us
    ppermute x46, starting transfers between devices, swap(): return lax.ppermute(x, axis, flip_pairs(lax.axis_size(axis), bit))  75.1 us
    unnamed x220, local copies, waits for them, and re-layouts  40.2 us
    all_to_all x6, starting transfers between devices, share_rows(): return lax.all_to_all(x, 'rows', 0, 0)  29.7 us
    pallas_call x1, Pallas kernels, attend_back(): pl.pallas_call(attend_back_kernel, grid_spec=pltpu.PrefetchScalarGridSpec...  28.1 us
    pallas_call x3, Pallas kernels, norm_back(): pl.pallas_call(functools.partial(back_kernel, res is not None, placed, tu...  26.4 us
    pallas_call x4, Pallas kernels, weight_grad(): pl.pallas_call(grad_kernel, grid_spec=pltpu.PrefetchScalarGridSpec(num_sc...  23.8 us
    pallas_call x1, Pallas kernels, attend(): pl.pallas_call(attend_kernel, grid_spec=pltpu.PrefetchScalarGridSpec(num_...  19.5 us
  transfers between devices with their start and end apart: 59, of which 26 were waited for; matrix products, arithmetic and copies ran while one was open for 10% of the time, Pallas kernels for 27%

profile of v5, /device:TPU:0, one launch (start us, length us, event | category | flops | bytes accessed | tf_op | source)
XLA Modules:
  0.0 566.2 jit_solution(2803379467575737198)
XLA Ops:
  9.8 6.3 %all-to-all-start = ((bf16[4,336,128]{2,1,0:T(8,128)(2,1)}), bf16[4,336,128]{2,1,0:T(8,128)(2,1)S(1)}, u32[]{:S(2)}, u32[]{:S(2)}) async-start(bf16[4,336,128]{2,1,0:T(8,128)(2,1)} %broadcast_in_dim.71), calls=%async_computation | async-start | bytes 688128 | tf_op jit(solution)/shard_map/all_to_all | solution.py:1058
  17.2 9.6 %all-to-all-done.refs_0_ = bf16[4,336,128]{2,1,0:T(8,128)(2,1)S(1)} async-done(((bf16[4,336,128]{2,1,0:T(8,128)(2,1)}), bf16[4,336,128]{2,1,0:T(8,128)(2,1)S(1)}, u32[]{:S(2)}, u32[]{:S(2)}) %all-to-all-start) | async-done | bytes 344096 | tf_op jit(solution)/shard_map/all_to_all | solution.py:1058
  34.3 4.8 collective-permute-done.1.refs_1_
  40.3 9.3 %all-to-all-done.1.refs_0_ = bf16[4,128,768]{2,1,0:T(8,128)(2,1)S(1)} async-done(((bf16[4,128,768]{2,1,0:T(8,128)(2,1)}), bf16[4,128,768]{2,1,0:T(8,128)(2,1)S(1)}, u32[]{:S(2)}, u32[]{:S(2)}) %all-to-all-start.1) | async-done | bytes 786464 | tf_op jit(solution)/shard_map/all_to_all | solution.py:1058
  55.3 8.6 %collective-permute-done.3 = bf16[256,576]{0,1:T(8,128)(2,1)} collective-permute-done((bf16[256,576]{0,1:T(8,128)(2,1)S(1)}, bf16[256,576]{0,1:T(8,128)(2,1)}, u32[]{:S(2)}, u32[]{:S(2)}) %collective-permute-start.3) | collective-permute-done | bytes 294944 | tf_op jit(solution)/shard_map/ppermute | solution.py:1166
  65.1 6.4 %all-to-all-start.2 = ((bf16[4,128,1280]{2,1,0:T(8,128)(2,1)}), bf16[4,128,1280]{2,1,0:T(8,128)(2,1)}, u32[]{:S(2)}, u32[]{:S(2)}) async-start(bf16[4,128,1280]{2,1,0:T(8,128)(2,1)} %broadcast_in_dim.73), calls=%async_computation.2 | async-start | bytes 2621440 | tf_op jit(solution)/shard_map/all_to_all | solution.py:1058
  72.9 8.5 %collective-permute-done.6.refs_3_ = bf16[4,336,128]{2,1,0:T(8,128)(2,1)S(1)} collective-permute-done((bf16[4,336,128]{2,1,0:T(8,128)(2,1)S(1)}, bf16[4,336,128]{2,1,0:T(8,128)(2,1)S(1)}, u32[]{:S(2)}, u32[]{:S(2)}) %collective-permute-start.6) | collective-permute-done | bytes 344096 | tf_op jit(solution)/shard_map/ppermute | solution.py:964
  106.9 5.6 collective-permute-done.9.w1_ref.refs_2_
  112.6 5.2 joint.1.q_ref.k0_ref.v0_ref
  126.5 19.5 %attend.1 = (bf16[512,1024]{1,0:T(8,128)(2,1)S(1)}, f32[512,1024]{1,0:T(8,128)S(1)}, f32[512,1024]{1,0:T(8,128)S(1)}) custom-call(s32[20]{0:T(128)S(1)} %get-tuple-element.318.perm, s32[2]{0:T(128)S(1)} %pad_add_fusion.lens, bf16[512,3072]{1,0:T(8,128)(2,1)S(1)} %copy-done.25, bf16[512,3072]{1,0:T(8,128)(2,1)S(1)} %copy-done.25, ...), custom_call_target="tpu_custom_call" | custom-call | flops 2147483648 | bytes 6291456 | tf_op jit(solution)/shard_map/attend/pallas_call | solution.py:629
  148.3 10.9 %collective-permute-done.12.refs_1_ = bf16[4,128,1280]{2,1,0:T(8,128)(2,1)} collective-permute-done((bf16[4,128,1280]{2,1,0:T(8,128)(2,1)}, bf16[4,128,1280]{2,1,0:T(8,128)(2,1)}, u32[]{:S(2)}, u32[]{:S(2)}) %collective-permute-start.12) | collective-permute-done | bytes 1310752 | tf_op jit(solution)/shard_map/ppermute | solution.py:964
  164.1 24.3 %collective-permute-done.13.refs_3_ = bf16[2,128,1280]{2,1,0:T(8,128)(2,1)S(1)} collective-permute-done((bf16[2,128,1280]{2,1,0:T(8,128)(2,1)S(1)}, bf16[2,128,1280]{2,1,0:T(8,128)(2,1)S(1)}, u32[]{:S(2)}, u32[]{:S(2)}) %collective-permute-start.13) | collective-permute-done | bytes 655392 | tf_op jit(solution)/shard_map/ppermute | solution.py:964
  188.4 5.0 stack.58.w0_ref.refs_1_
  209.7 5.3 project_norm.2
  217.2 13.9 %up_gelu.1 = (f32[512,4096]{1,0:T(8,128)}, bf16[512,4096]{1,0:T(8,128)(2,1)}) custom-call(s32[20]{0:T(128)} %get-tuple-element.317.perm, bf16[512,1024]{1,0:T(8,128)(2,1)} %copy-done.56, bf16[4,4,128,1280]{3,2,1,0:T(8,128)(2,1)} %stack.58.w0_ref.refs_1_, bf16[4,4,128,1280]{3,2,1,0:T(8,128)(2,1)} %collective-permute-done.15.w1_ref.refs_2_, f32[1,4096]{1,0:T(1,128)} %bitcast.276), custom_call_target="tpu_custom_call" | custom-call | flops 4294967296 | bytes 20971520 | tf_op jit(solution)/shard_map/up_gelu/pallas_call | solution.py:375
  231.1 12.4 %project_norm.3 = (f32[512,1024]{1,0:T(8,128)}, bf16[512,1024]{1,0:T(8,128)(2,1)}) custom-call(s32[20]{0:T(128)} %copy-done.42, bf16[512,4096]{1,0:T(8,128)(2,1)} %get-tuple-element.161.a_ref, bf16[8,4,512,256]{3,2,1,0:T(8,128)(2,1)} %bitcast.255, bf16[8,4,512,256]{3,2,1,0:T(8,128)(2,1)} %bitcast.256, f32[512,1024]{1,0:T(8,128)} %copy-done.2, ...), custom_call_target="tpu_custom_call" | custom-call | flops 4294967296 | bytes 17825792 | tf_op jit(solution)/shard_map/project_norm/pallas_call | solution.py:156
  250.4 6.5 %render.1 = (f32[768,512]{1,0:T(8,128)S(1)}, f32[768,128]{1,0:T(8,128)S(1)}, f32[8,128]{1,0:T(8,128)S(1)}) custom-call(s32[1]{0:T(128)} %bitcast.15.views_ref, f32[1]{0:T(128)} %bitcast.16.inv_ref, f32[768,512]{1,0:T(8,128)S(1)} %gauss.1.z_ref, f32[768,128]{1,0:T(8,128)S(1)} %maximum_maximum_fusion.zx_ref, f32[2,12,19,256]{3,2,1,0:T(8,128)S(1)} %pad_maximum_fusion.4.rd_ref, ...), custom_call_target="tpu_custom_call" | custom-call | flops 21743271936 | bytes 4194304 | tf_op jit(solution)/shard_map/render/pallas_call | solution.py:935
  269.5 7.9 %weight_grad.4 = bf16[8,4,512,256]{3,2,1,0:T(8,128)(2,1)S(1)} custom-call(s32[20]{0:T(128)S(1)} %copy-done.51, bf16[512,4096]{1,0:T(8,128)(2,1)S(1)} %copy-done.9, bf16[512,1024]{1,0:T(8,128)(2,1)S(1)} %get-tuple-element.177.d_ref), custom_call_target="tpu_custom_call" | custom-call | flops 4294967296 | bytes 13631488 | tf_op jit(solution)/shard_map/weight_grad/pallas_call | solution.py:305
  285.1 16.2 %collective-permute-start.21 = (bf16[2,4,192,128]{3,2,1,0:T(8,128)(2,1)S(1)}, bf16[2,4,192,128]{3,2,1,0:T(8,128)(2,1)S(1)}, u32[]{:S(2)}, u32[]{:S(2)}) collective-permute-start(bf16[2,4,192,128]{3,2,1,0:T(8,128)(2,1)S(1)} %add_convert_fusion.6), channel_id=1, source_target_pairs={{0,16},{4,20},{8,24},{12,28},{16,0},{20,4},{24,8},{28,12},{1,17},{... | collective-permute-start | bytes 1179656 | tf_op jit(solution)/shard_map/ppermute | solution.py:964
  301.3 16.0 %down_back_gelu.1 = (bf16[512,4096]{1,0:T(8,128)(2,1)}, f32[1,4096]{1,0:T(1,128)}) custom-call(s32[20]{0:T(128)} %get-tuple-element.317.perm, bf16[512,1024]{1,0:T(8,128)(2,1)} %copy-done.33, bf16[8,4,512,256]{3,2,1,0:T(8,128)(2,1)} %bitcast.257, bf16[8,4,512,256]{3,2,1,0:T(8,128)(2,1)} %bitcast.258, f32[512,4096]{1,0:T(8,128)} %get-tuple-element.178.u_ref), custom_call_target="tpu_custom_call" | custom-call | flops 4294967296 | bytes 20971520 | tf_op jit(solution)/shard_map/down_back_gelu/pallas_call | solution.py:426
  321.6 6.8 %weight_grad.5 = (bf16[4,4,128,1024]{3,2,1,0:T(8,128)(2,1)S(1)}, bf16[4,4,128,1024]{3,2,1,0:T(8,128)(2,1)S(1)}) custom-call(s32[20]{0:T(128)S(1)} %copy-done.43, bf16[512,1024]{1,0:T(8,128)(2,1)S(1)} %copy-done.57, bf16[512,4096]{1,0:T(8,128)(2,1)S(1)} %copy-done.13), custom_call_target="tpu_custom_call" | custom-call | flops 4294967296 | bytes 13631488 | tf_op jit(solution)/shard_map/weight_grad/pallas_call | solution.py:305
  328.5 17.9 %collective-permute-start.23 = (bf16[4,192,128]{2,1,0:T(8,128)(2,1)S(1)}, bf16[4,192,128]{2,1,0:T(8,128)(2,1)S(1)}, u32[]{:S(2)}, u32[]{:S(2)}) collective-permute-start(bf16[4,192,128]{2,1,0:T(8,128)(2,1)S(1)} %fusion.29), channel_id=1, source_target_pairs={{0,8},{4,12},{8,0},{12,4},{16,24},{20,28},{24,16},{28,20},{1,9},{5... | collective-permute-start | bytes 589832 | tf_op jit(solution)/shard_map/ppermute | solution.py:964
  346.5 10.3 %norm_back.4 = (f32[512,1024]{1,0:T(8,128)S(1)}, bf16[512,1024]{1,0:T(8,128)(2,1)S(1)}, f32[8,1024]{1,0:T(8,128)S(1)}) custom-call(s32[20]{0:T(128)S(1)} %copy-done.43, bf16[512,4096]{1,0:T(8,128)(2,1)S(1)} %copy-done.14, bf16[4,4,128,1280]{3,2,1,0:T(8,128)(2,1)} %stack.58.w0_ref.refs_1_, bf16[4,4,128,1280]{3,2,1,0:T(8,128)(2,1)} %collective-permute-done.15.w1_ref.refs_2_, ...), custom_call_target="tpu_custom_call" | custom-call | flops 4294967296 | bytes 19922944 | tf_op jit(solution)/shard_map/norm_back/pallas_call | solution.py:554
  375.3 28.1 %attend_back.1 = (bf16[512,1024]{1,0:T(8,128)(2,1)S(1)}, f32[2,512,1024]{2,1,0:T(8,128)S(1)}, bf16[2,512,1024]{2,1,0:T(8,128)(2,1)S(1)}) custom-call(s32[20]{0:T(128)S(1)} %copy-done.43, s32[2]{0:T(128)S(1)} %copy-done.63, bf16[512,3072]{1,0:T(8,128)(2,1)S(1)} %copy-done.26, bf16[512,3072]{1,0:T(8,128)(2,1)S(1)} %copy-done.26, ...), custom_call_target="tpu_custom_call" | custom-call | flops 5368709120 | bytes 14680064 | tf_op jit(solution)/shard_map/attend_back/pallas_call | solution.py:722
  417.9 6.2 %weight_grad.7 = (bf16[4,4,128,768]{3,2,1,0:T(8,128)(2,1)S(1)}, bf16[4,4,128,768]{3,2,1,0:T(8,128)(2,1)}) custom-call(s32[20]{0:T(128)S(1)} %copy-done.43, bf16[512,1024]{1,0:T(8,128)(2,1)S(1)} %copy-done.55, bf16[512,3072]{1,0:T(8,128)(2,1)S(1)} %pad_maximum_fusion.d_ref.refs_0_), custom_call_target="tpu_custom_call" | custom-call | flops 3221225472 | bytes 10485760 | tf_op jit(solution)/shard_map/weight_grad/pallas_call | solution.py:305
  430.5 12.6 %norm_back.5 = (bf16[512,1024]{1,0:T(8,128)(2,1)}, f32[8,1024]{1,0:T(8,128)}) custom-call(s32[20]{0:T(128)} %copy-done.42, bf16[512,3072]{1,0:T(8,128)(2,1)} %copy-done.1, bf16[4,4,128,768]{3,2,1,0:T(8,128)(2,1)} %copy-done, bf16[4,4,128,768]{3,2,1,0:T(8,128)(2,1)} %copy-done.15, f32[512,1024]{1,0:T(8,128)} %copy-done.5, f32[1,1024]{1,0:T(1,128)} %bitcast.246, ...), custom_call_target="tpu_custom_call" | custom-call | flops 3221225472 | bytes 16777216 | tf_op jit(solution)/shard_map/norm_back/pallas_call | solution.py:554
  457.0 5.0 all-to-all-start.5
  465.5 5.1 collective-permute-done.32
  479.4 6.0 %collective-permute-done.40 = bf16[2,128,768]{2,1,0:T(8,128)(2,1)S(1)} collective-permute-done((bf16[2,128,768]{2,1,0:T(8,128)(2,1)S(1)}, bf16[2,128,768]{2,1,0:T(8,128)(2,1)S(1)}, u32[]{:S(2)}, u32[]{:S(2)}) %collective-permute-start.40) | collective-permute-done | bytes 393248 | tf_op jit(solution)/shard_map/ppermute | solution.py:964
  487.0 5.1 all-to-all-start.4
  503.7 8.8 %collective-permute-done.39 = bf16[144,128]{1,0:T(8,128)(2,1)S(1)} collective-permute-done((bf16[144,128]{1,0:T(8,128)(2,1)S(1)}, bf16[144,128]{1,0:T(8,128)(2,1)S(1)}, u32[]{:S(2)}, u32[]{:S(2)}) %collective-permute-start.39) | collective-permute-done | bytes 36896 | tf_op jit(solution)/shard_map/ppermute | solution.py:964
  512.5 6.2 %collective-permute-done.38 = bf16[144,128]{1,0:T(8,128)(2,1)S(1)} collective-permute-done((bf16[144,128]{1,0:T(8,128)(2,1)S(1)}, bf16[144,128]{1,0:T(8,128)(2,1)S(1)}, u32[]{:S(2)}, u32[]{:S(2)}) %collective-permute-start.38) | collective-permute-done | bytes 36896 | tf_op jit(solution)/shard_map/ppermute | solution.py:964
  (439 shorter events, 220.8 us)
Async XLA Ops:
  9.8 17.0 %all-to-all-start = ((bf16[4,336,128]{2,1,0:T(8,128)(2,1)}), bf16[4,336,128]{2,1,0:T(8,128)(2,1)S(1)}, u32[]{:S(2)}, u32[]{:S(2)}) async-start(bf16[4,336,128]{2,1,0:T(8,128)(2,1)} %broadcast_in_dim.71), calls=%async_computation | async-start | bytes 688128 | tf_op jit(solution)/shard_map/all_to_all | solution.py:1058
  27.7 21.9 %all-to-all-start.1 = ((bf16[4,128,768]{2,1,0:T(8,128)(2,1)}), bf16[4,128,768]{2,1,0:T(8,128)(2,1)S(1)}, u32[]{:S(2)}, u32[]{:S(2)}) async-start(bf16[4,128,768]{2,1,0:T(8,128)(2,1)} %broadcast_in_dim.72), calls=%async_computation.1 | async-start | bytes 1572864 | tf_op jit(solution)/shard_map/all_to_all | solution.py:1058
  52.1 29.3 %collective-permute-start.5 = (bf16[4,128,768]{2,1,0:T(8,128)(2,1)S(1)}, bf16[4,128,768]{2,1,0:T(8,128)(2,1)S(1)}, u32[]{:S(2)}, u32[]{:S(2)}) collective-permute-start(bf16[4,128,768]{2,1,0:T(8,128)(2,1)S(1)} %all-to-all-done.1.refs_0_), channel_id=1, source_target_pairs={{0,16},{4,20},{8,24},{12,28},{16,0},{20,4},{24,8},{28,12},{1,17},{... | collective-permute-start | bytes 2359304 | tf_op jit(solution)/shard_map/ppermute | solution.py:964
  53.7 28.7 %collective-permute-start.4 = (bf16[4,128,768]{2,1,0:T(8,128)(2,1)S(1)}, bf16[4,128,768]{2,1,0:T(8,128)(2,1)}, u32[]{:S(2)}, u32[]{:S(2)}) collective-permute-start(bf16[4,128,768]{2,1,0:T(8,128)(2,1)S(1)} %all-to-all-done.1.refs_0_), channel_id=1, source_target_pairs={{0,8},{4,12},{8,0},{12,4},{16,24},{20,28},{24,16},{28,20},{1,9},{5... | collective-permute-start | bytes 2359304 | tf_op jit(solution)/shard_map/ppermute | solution.py:964
  65.1 37.9 %all-to-all-start.2 = ((bf16[4,128,1280]{2,1,0:T(8,128)(2,1)}), bf16[4,128,1280]{2,1,0:T(8,128)(2,1)}, u32[]{:S(2)}, u32[]{:S(2)}) async-start(bf16[4,128,1280]{2,1,0:T(8,128)(2,1)} %broadcast_in_dim.73), calls=%async_computation.2 | async-start | bytes 2621440 | tf_op jit(solution)/shard_map/all_to_all | solution.py:1058
  71.4 159.7 %all-gather.3.cloned.1.call-start = ((), (), s32[]{:S(2)}) async-start(), calls=%async_computation.10 | async-start | bytes 8650752 | tf_op jit(solution)/shard_map/all_gather | solution.py:987
  82.7 20.3 %collective-permute-start.8 = (bf16[4,128,768]{2,1,0:T(8,128)(2,1)}, bf16[4,128,768]{2,1,0:T(8,128)(2,1)}, u32[]{:S(2)}, u32[]{:S(2)}) collective-permute-start(bf16[4,128,768]{2,1,0:T(8,128)(2,1)} %collective-permute-done.4.refs_1_), channel_id=1, source_target_pairs={{0,16},{4,20},{8,24},{12,28},{16,0},{20,4},{24,8},{28,12},{1,17},{... | collective-permute-start | bytes 2359304 | tf_op jit(solution)/shard_map/ppermute | solution.py:964
  103.0 303.8 %reduce-scatter.3.cloned.1.call-start = ((), (), s32[]{:S(2)}) async-start(), calls=%async_computation.8 | async-start | bytes 9437184 | tf_op jit(solution)/shard_map/reduce_scatter | solution.py:1292
  120.2 39.0 %collective-permute-start.12 = (bf16[4,128,1280]{2,1,0:T(8,128)(2,1)}, bf16[4,128,1280]{2,1,0:T(8,128)(2,1)}, u32[]{:S(2)}, u32[]{:S(2)}) collective-permute-start(bf16[4,128,1280]{2,1,0:T(8,128)(2,1)} %all-to-all-done.2.refs_0_), channel_id=1, source_target_pairs={{0,8},{4,12},{8,0},{12,4},{16,24},{20,28},{24,16},{28,20},{1,9},{5... | collective-permute-start | bytes 3932168 | tf_op jit(solution)/shard_map/ppermute | solution.py:964
  121.7 37.5 %collective-permute-start.11 = (bf16[4,128,1280]{2,1,0:T(8,128)(2,1)}, bf16[4,128,1280]{2,1,0:T(8,128)(2,1)}, u32[]{:S(2)}, u32[]{:S(2)}) collective-permute-start(bf16[4,128,1280]{2,1,0:T(8,128)(2,1)} %all-to-all-done.2.refs_0_), channel_id=1, source_target_pairs={{0,16},{4,20},{8,24},{12,28},{16,0},{20,4},{24,8},{28,12},{1,17},{... | collective-permute-start | bytes 3932168 | tf_op jit(solution)/shard_map/ppermute | solution.py:964
  161.5 26.9 %collective-permute-start.13 = (bf16[2,128,1280]{2,1,0:T(8,128)(2,1)S(1)}, bf16[2,128,1280]{2,1,0:T(8,128)(2,1)S(1)}, u32[]{:S(2)}, u32[]{:S(2)}) collective-permute-start(bf16[2,128,1280]{2,1,0:T(8,128)(2,1)S(1)} %slice.285), channel_id=1, source_target_pairs={{0,8},{4,12},{8,0},{12,4},{16,24},{20,28},{24,16},{28,20},{1,9},{5... | collective-permute-start | bytes 1966088 | tf_op jit(solution)/shard_map/ppermute | solution.py:964
  164.1 24.4 %collective-permute-start.14 = (bf16[2,128,1280]{2,1,0:T(8,128)(2,1)S(1)}, bf16[2,128,1280]{2,1,0:T(8,128)(2,1)S(1)}, u32[]{:S(2)}, u32[]{:S(2)}) collective-permute-start(bf16[2,128,1280]{2,1,0:T(8,128)(2,1)S(1)} %slice.286), channel_id=1, source_target_pairs={{0,16},{4,20},{8,24},{12,28},{16,0},{20,4},{24,8},{28,12},{1,17},{... | collective-permute-start | bytes 1966088 | tf_op jit(solution)/shard_map/ppermute | solution.py:964
  194.4 53.2 %collective-permute-start.17 = (f32[12,19,256]{2,1,0:T(8,128)}, f32[12,19,256]{2,1,0:T(8,128)S(1)}, u32[]{:S(2)}, u32[]{:S(2)}) collective-permute-start(f32[12,19,256]{2,1,0:T(8,128)} %get-tuple-element.285), channel_id=1, source_target_pairs={{0,2},{1,0},{2,6},{3,4},{4,3},{5,1},{6,7},{7,5},{8,10},{9,8},{10,1... | collective-permute-start | bytes 700424 | tf_op jit(solution)/shard_map/ppermute | solution.py:1166
  196.8 50.8 %collective-permute-start.16 = (f32[12,19,256]{2,1,0:T(8,128)}, f32[12,19,256]{2,1,0:T(8,128)}, u32[]{:S(2)}, u32[]{:S(2)}) collective-permute-start(f32[12,19,256]{2,1,0:T(8,128)} %get-tuple-element.286), channel_id=1, source_target_pairs={{0,0},{1,2},{2,4},{3,6},{4,1},{5,3},{6,5},{7,7},{8,8},{9,10},{10,1... | collective-permute-start | bytes 700424 | tf_op jit(solution)/shard_map/ppermute | solution.py:1165
  285.1 32.2 %collective-permute-start.21 = (bf16[2,4,192,128]{3,2,1,0:T(8,128)(2,1)S(1)}, bf16[2,4,192,128]{3,2,1,0:T(8,128)(2,1)S(1)}, u32[]{:S(2)}, u32[]{:S(2)}) collective-permute-start(bf16[2,4,192,128]{3,2,1,0:T(8,128)(2,1)S(1)} %add_convert_fusion.6), channel_id=1, source_target_pairs={{0,16},{4,20},{8,24},{12,28},{16,0},{20,4},{24,8},{28,12},{1,17},{... | collective-permute-start | bytes 1179656 | tf_op jit(solution)/shard_map/ppermute | solution.py:964
  328.5 28.4 %collective-permute-start.22 = (bf16[4,4,128,1024]{3,2,1,0:T(8,128)(2,1)S(1)}, bf16[4,4,128,1024]{3,2,1,0:T(8,128)(2,1)S(1)}, u32[]{:S(2)}, u32[]{:S(2)}) collective-permute-start(bf16[4,4,128,1024]{3,2,1,0:T(8,128)(2,1)S(1)} %get-tuple-element.189), channel_id=1, source_target_pairs={{0,4},{4,0},{8,12},{12,8},{16,20},{20,16},{24,28},{28,24},{1,5},{5... | collective-permute-start | bytes 12582920 | tf_op jit(solution)/shard_map/ppermute | solution.py:964
  328.5 28.3 %collective-permute-start.23 = (bf16[4,192,128]{2,1,0:T(8,128)(2,1)S(1)}, bf16[4,192,128]{2,1,0:T(8,128)(2,1)S(1)}, u32[]{:S(2)}, u32[]{:S(2)}) collective-permute-start(bf16[4,192,128]{2,1,0:T(8,128)(2,1)S(1)} %fusion.29), channel_id=1, source_target_pairs={{0,8},{4,12},{8,0},{12,4},{16,24},{20,28},{24,16},{28,20},{1,9},{5... | collective-permute-start | bytes 589832 | tf_op jit(solution)/shard_map/ppermute | solution.py:964
  364.0 42.8 %collective-permute-start.24 = (bf16[4,4,128,256]{3,2,1,0:T(8,128)(2,1)S(1)}, bf16[4,4,128,256]{3,2,1,0:T(8,128)(2,1)}, u32[]{:S(2)}, u32[]{:S(2)}) collective-permute-start(bf16[4,4,128,256]{3,2,1,0:T(8,128)(2,1)S(1)} %get-tuple-element.202), channel_id=1, source_target_pairs={{0,4},{4,0},{8,12},{12,8},{16,20},{20,16},{24,28},{28,24},{1,5},{5... | collective-permute-start | bytes 3145736 | tf_op jit(solution)/shard_map/ppermute | solution.py:964
  364.2 42.6 %collective-permute-start.25 = (bf16[2,2,128,1024]{3,2,1,0:T(8,128)(2,1)}, bf16[2,2,128,1024]{3,2,1,0:T(8,128)(2,1)}, u32[]{:S(2)}, u32[]{:S(2)}) collective-permute-start(bf16[2,2,128,1024]{3,2,1,0:T(8,128)(2,1)} %fusion), channel_id=1, source_target_pairs={{0,8},{4,12},{8,0},{12,4},{16,24},{20,28},{24,16},{28,20},{1,9},{5... | collective-permute-start | bytes 3145736 | tf_op jit(solution)/shard_map/ppermute | solution.py:964
  365.2 41.6 %collective-permute-start.26 = (bf16[2,2,128,1024]{3,2,1,0:T(8,128)(2,1)}, bf16[2,2,128,1024]{3,2,1,0:T(8,128)(2,1)}, u32[]{:S(2)}, u32[]{:S(2)}) collective-permute-start(bf16[2,2,128,1024]{3,2,1,0:T(8,128)(2,1)} %fusion.1), channel_id=1, source_target_pairs={{0,16},{4,20},{8,24},{12,28},{16,0},{20,4},{24,8},{28,12},{1,17},{... | collective-permute-start | bytes 3145736 | tf_op jit(solution)/shard_map/ppermute | solution.py:964
  367.6 39.2 %all-to-all-start.3 = ((bf16[4,192,128]{2,1,0:T(8,128)(2,1)}), bf16[4,192,128]{2,1,0:T(8,128)(2,1)S(1)}, u32[]{:S(2)}, u32[]{:S(2)}) async-start(bf16[4,192,128]{2,1,0:T(8,128)(2,1)} %fusion.25), calls=%async_computation.3 | async-start | bytes 393216 | tf_op jit(solution)/shard_map/all_to_all | solution.py:1058
  371.0 94.6 %reduce-scatter.5.cloned.1.call-start = ((), (), s32[]{:S(2)}) async-start(), calls=%async_computation.9 | async-start | bytes 1310720 | tf_op jit(solution)/shard_map/reduce_scatter | solution.py:1324
  425.7 18.4 %collective-permute-start.28 = (bf16[4,4,128,768]{3,2,1,0:T(8,128)(2,1)}, bf16[4,4,128,768]{3,2,1,0:T(8,128)(2,1)}, u32[]{:S(2)}, u32[]{:S(2)}) collective-permute-start(bf16[4,4,128,768]{3,2,1,0:T(8,128)(2,1)} %get-tuple-element.225), channel_id=1, source_target_pairs={{0,4},{4,0},{8,12},{12,8},{16,20},{20,16},{24,28},{28,24},{1,5},{5... | collective-permute-start | bytes 9437192 | tf_op jit(solution)/shard_map/ppermute | solution.py:964
  428.4 15.7 %collective-permute-start.29 = (bf16[2,128,1024]{2,1,0:T(8,128)(2,1)}, bf16[2,128,1024]{2,1,0:T(8,128)(2,1)S(1)}, u32[]{:S(2)}, u32[]{:S(2)}) collective-permute-start(bf16[2,128,1024]{2,1,0:T(8,128)(2,1)} %fusion.18), channel_id=1, source_target_pairs={{0,16},{4,20},{8,24},{12,28},{16,0},{20,4},{24,8},{28,12},{1,17},{... | collective-permute-start | bytes 1572872 | tf_op jit(solution)/shard_map/ppermute | solution.py:964
  428.4 15.7 %collective-permute-start.30 = (bf16[2,128,1024]{2,1,0:T(8,128)(2,1)}, bf16[2,128,1024]{2,1,0:T(8,128)(2,1)S(1)}, u32[]{:S(2)}, u32[]{:S(2)}) collective-permute-start(bf16[2,128,1024]{2,1,0:T(8,128)(2,1)} %fusion.19), channel_id=1, source_target_pairs={{0,8},{4,12},{8,0},{12,4},{16,24},{20,28},{24,16},{28,20},{1,9},{5... | collective-permute-start | bytes 1572872 | tf_op jit(solution)/shard_map/ppermute | solution.py:964
  429.2 26.7 %collective-permute-start.31 = (bf16[2,4,128,256]{3,2,1,0:T(8,128)(2,1)}, bf16[2,4,128,256]{3,2,1,0:T(8,128)(2,1)}, u32[]{:S(2)}, u32[]{:S(2)}) collective-permute-start(bf16[2,4,128,256]{3,2,1,0:T(8,128)(2,1)} %fusion.17), channel_id=1, source_target_pairs={{0,8},{4,12},{8,0},{12,4},{16,24},{20,28},{24,16},{28,20},{1,9},{5... | collective-permute-start | bytes 1572872 | tf_op jit(solution)/shard_map/ppermute | solution.py:964
  449.0 21.7 %collective-permute-start.32 = (bf16[2,2,128,768]{3,2,1,0:T(8,128)(2,1)}, bf16[2,2,128,768]{3,2,1,0:T(8,128)(2,1)}, u32[]{:S(2)}, u32[]{:S(2)}) collective-permute-start(bf16[2,2,128,768]{3,2,1,0:T(8,128)(2,1)} %fusion.6), channel_id=1, source_target_pairs={{0,8},{4,12},{8,0},{12,4},{16,24},{20,28},{24,16},{28,20},{1,9},{5... | collective-permute-start | bytes 2359304 | tf_op jit(solution)/shard_map/ppermute | solution.py:964
  449.6 21.1 %collective-permute-start.33 = (bf16[2,2,128,768]{3,2,1,0:T(8,128)(2,1)}, bf16[2,2,128,768]{3,2,1,0:T(8,128)(2,1)}, u32[]{:S(2)}, u32[]{:S(2)}) collective-permute-start(bf16[2,2,128,768]{3,2,1,0:T(8,128)(2,1)} %fusion.7), channel_id=1, source_target_pairs={{0,16},{4,20},{8,24},{12,28},{16,0},{20,4},{24,8},{28,12},{1,17},{... | collective-permute-start | bytes 2359304 | tf_op jit(solution)/shard_map/ppermute | solution.py:964
  457.0 30.0 %all-to-all-start.5 = ((bf16[4,128,1024]{2,1,0:T(8,128)(2,1)}), bf16[4,128,1024]{2,1,0:T(8,128)(2,1)}, u32[]{:S(2)}, u32[]{:S(2)}) async-start(bf16[4,128,1024]{2,1,0:T(8,128)(2,1)} %pad_maximum_fusion.2), calls=%async_computation.7 | async-start | bytes 2097152 | tf_op jit(solution)/shard_map/all_to_all | solution.py:1058
  487.0 34.6 %all-to-all-start.4 = ((bf16[4,128,1024]{2,1,0:T(8,128)(2,1)}), bf16[4,128,1024]{2,1,0:T(8,128)(2,1)S(1)}, u32[]{:S(2)}, u32[]{:S(2)}) async-start(bf16[4,128,1024]{2,1,0:T(8,128)(2,1)} %pad_maximum_fusion.1), calls=%async_computation.6 | async-start | bytes 2097152 | tf_op jit(solution)/shard_map/all_to_all | solution.py:1058
  502.4 16.4 %collective-permute-start.38 = (bf16[144,128]{1,0:T(8,128)(2,1)S(1)}, bf16[144,128]{1,0:T(8,128)(2,1)S(1)}, u32[]{:S(2)}, u32[]{:S(2)}) collective-permute-start(bf16[144,128]{1,0:T(8,128)(2,1)S(1)} %get-tuple-element.295), channel_id=1, source_target_pairs={{0,2},{1,3},{2,0},{3,1},{4,6},{5,7},{6,4},{7,5},{8,10},{9,11},{10,... | collective-permute-start | bytes 110600 | tf_op jit(solution)/shard_map/ppermute | solution.py:964
  502.4 16.4 %collective-permute-start.37 = (bf16[144,128]{1,0:T(8,128)(2,1)S(1)}, bf16[144,128]{1,0:T(8,128)(2,1)S(1)}, u32[]{:S(2)}, u32[]{:S(2)}) collective-permute-start(bf16[144,128]{1,0:T(8,128)(2,1)S(1)} %get-tuple-element.296), channel_id=1, source_target_pairs={{0,1},{1,0},{2,3},{3,2},{4,5},{5,4},{6,7},{7,6},{8,9},{9,8},{10,11... | collective-permute-start | bytes 110600 | tf_op jit(solution)/shard_map/ppermute | solution.py:964
  (131 other events, 1353.8 us)
Sparse Core Ops, SparseCore 0:
  103.1 101.2 all-gather.2
  281.7 122.2 reduce-scatter.2
  427.9 26.7 reduce-scatter.4
